TPU v7x, 256 devices: a whole 4x4x8 slice. The times are simulated.
256 devices in a mesh: dp: 128 (over z, x, y), pair: 2 (over core).
Axes of the slice: x: 4, y: 4, z: 8, core: 2. Of those that a mesh axis runs over, the one named last changes fastest.
Arguments:
- hidden_in: bfloat16 [32768, 1536], P(('dp', 'pair')), may hold values from -24 to 24
- segment_ids: int32 [32768], replicated, may hold values from 0 to 511, as said below
- frame_mask: int32 [32768], P(('dp', 'pair')), may hold values from 0 to 1, as said below
- dw_kernel: float32 [31, 1536], P(None, ('dp', 'pair')), may hold values from -1 to 1
- norm_scale: float32 [1536], P(('dp', 'pair')), may hold values from 0.1 to 1.9
- norm_shift: float32 [1536], P(('dp', 'pair')), may hold values from -3 to 3
- out_weight: bfloat16 [1536, 1536], P(('dp', 'pair')), may hold values from -0.15625 to 0.15625
- cotangent: bfloat16 [32768, 1536], P(('dp', 'pair')), may hold values from -6 to 6
Outputs:
- module_out: bfloat16 [32768, 1536], P(('dp', 'pair'))
- grad_hidden: bfloat16 [32768, 1536], P(('dp', 'pair'))
- grad_kernel: float32 [31, 1536], P(None, ('dp', 'pair'))
- grad_scale: float32 [1536], P(('dp', 'pair'))
- grad_shift: float32 [1536], P(('dp', 'pair'))
- grad_weight: float32 [1536, 1536], P(('dp', 'pair'))
Inputs may be any that keep to these rules, and one draw needn't show every extreme that they name: `segment_ids`: non-falling along the stream, starting at 0; each utterance has 1 to 192 frames; no utterance begins at a frame whose index is a positive multiple of 128. `frame_mask`: 1 on every frame whose index modulo 16 is 0 or 15.
All inputs are finite; a program needn't handle non-finite values.
Results may differ from a plain program's by a relative error of at most 0.0049.
Values may be sent and summed in bfloat16 or wider, within the bound.
No kernel may reach another device: no remote copies, remote signals or barrier semaphores. Data moves between devices by JAX's collectives and lax.ppermute only.
A program may use at most 128 MiB of HBM per device.

v0:
```python
import jax
import jax.numpy as jnp
from jax import lax
from jax.sharding import PartitionSpec as P

KERNEL = 31


def padded(cells, sides, width):
    for axis, dim in sides:
        count = lax.axis_size(axis)
        ends = count - 1
        head = lax.slice_in_dim(cells, 0, width, axis=dim)
        tail = lax.slice_in_dim(cells, cells.shape[dim] - width, cells.shape[dim], axis=dim)
        cells = jnp.concatenate(
            [
                lax.ppermute(tail, axis, [(i, (i + 1) % count) for i in range(ends)]),
                cells,
                lax.ppermute(head, axis, [((i + 1) % count, i) for i in range(ends)]),
            ],
            axis=dim,
        )
    return cells


def local(
    hidden_in, segment_ids, frame_mask, dw_kernel, norm_scale, norm_shift, out_weight, cotangent
):
    local_rows = hidden_in.shape[0]
    shard_cols = norm_scale.shape[0]
    half = KERNEL // 2
    device_pos = lax.axis_index(("dp", "pair"))
    weight_col = frame_mask.astype(jnp.float32)[:, None]
    stacked = jnp.concatenate([dw_kernel, norm_scale[None, :], norm_shift[None, :]], axis=0)
    params_full = lax.all_gather(stacked, ("dp", "pair"), axis=1, tiled=True)
    kernel_full = params_full[:KERNEL]
    scale_full = params_full[KERNEL]
    shift_full = params_full[KERNEL + 1]
    seg_pad = jnp.pad(segment_ids, (half, half), constant_values=-1)
    seg_local = lax.dynamic_slice_in_dim(seg_pad, device_pos * local_rows, local_rows + 2 * half)
    own_seg = seg_local[half : half + local_rows]
    masked = jnp.where(frame_mask[:, None] == 1, hidden_in, jnp.zeros_like(hidden_in))
    padded_in = padded(masked, ((("dp", "pair"), 0),), half).astype(jnp.float32)
    conv = jnp.zeros((local_rows, params_full.shape[1]), jnp.float32)
    for offset in range(KERNEL):
        same_seg = (seg_local[offset : offset + local_rows] == own_seg)[:, None]
        conv = conv + jnp.where(
            same_seg, kernel_full[offset] * padded_in[offset : offset + local_rows], 0.0
        )
    total, count = lax.psum(
        (jnp.sum(weight_col * conv, axis=0), jnp.sum(weight_col)), ("dp", "pair")
    )
    mean = total / count
    centred = conv - mean
    spread = lax.psum(jnp.sum(weight_col * centred * centred, axis=0), ("dp", "pair"))
    variance = spread / count
    inv_std = lax.rsqrt(variance + 1e-05)
    normed = centred * inv_std
    pre = scale_full * normed + shift_full
    sig = jax.nn.sigmoid(pre)
    act = (weight_col * pre * sig).astype(jnp.bfloat16)
    weight_full = lax.all_gather(out_weight, ("dp", "pair"), axis=0, tiled=True)
    module_out = jnp.dot(act, weight_full, preferred_element_type=jnp.float32).astype(jnp.bfloat16)
    grad_act = lax.dot_general(
        cotangent, weight_full, (((1,), (1,)), ((), ())), preferred_element_type=jnp.float32
    )
    grad_pre = weight_col * grad_act * sig * (1.0 + pre * (1.0 - sig))
    scale_sum, shift_sum = lax.psum(
        (jnp.sum(grad_pre * normed, axis=0), jnp.sum(grad_pre, axis=0)), ("dp", "pair")
    )
    col_start = device_pos * shard_cols
    grad_scale = lax.dynamic_slice_in_dim(scale_sum, col_start, shard_cols)
    grad_shift = lax.dynamic_slice_in_dim(shift_sum, col_start, shard_cols)
    grad_conv = (
        weight_col
        * scale_full
        * inv_std
        * (grad_pre - shift_sum / count - normed * scale_sum / count)
    )
    grad_pad = padded(grad_conv, ((("dp", "pair"), 0),), half)
    grad_local = jnp.zeros_like(grad_conv)
    tap_rows = []
    for offset in range(KERNEL):
        same_fwd = (seg_local[offset : offset + local_rows] == own_seg)[:, None]
        tap_rows.append(
            jnp.sum(
                jnp.where(same_fwd, grad_conv * padded_in[offset : offset + local_rows], 0.0),
                axis=0,
            )
        )
        back = 2 * half - offset
        same_back = (seg_local[back : back + local_rows] == own_seg)[:, None]
        grad_local = grad_local + jnp.where(
            same_back, kernel_full[offset] * grad_pad[back : back + local_rows], 0.0
        )
    grad_kernel = lax.psum_scatter(
        jnp.stack(tap_rows, axis=0), ("dp", "pair"), scatter_dimension=1, tiled=True
    )
    grad_hidden = (weight_col * grad_local).astype(jnp.bfloat16)
    grad_weight = lax.psum_scatter(
        lax.dot_general(
            act, cotangent, (((0,), (0,)), ((), ())), preferred_element_type=jnp.float32
        ),
        ("dp", "pair"),
        scatter_dimension=0,
        tiled=True,
    )
    return (module_out, grad_hidden, grad_kernel, grad_scale, grad_shift, grad_weight)


def solution(mesh):
    return jax.shard_map(
        local,
        mesh=mesh,
        in_specs=(
            P(("dp", "pair"), None),
            P(),
            P(("dp", "pair")),
            P(None, ("dp", "pair")),
            P(("dp", "pair")),
            P(("dp", "pair")),
            P(("dp", "pair"), None),
            P(("dp", "pair"), None),
        ),
        out_specs=(
            P(("dp", "pair"), None),
            P(("dp", "pair"), None),
            P(None, ("dp", "pair")),
            P(("dp", "pair")),
            P(("dp", "pair")),
            P(("dp", "pair"), None),
        ),
        check_vma=False,
    )
```

profile of v0, /device:TPU:1, one launch (start us, length us, event | category | flops | bytes accessed | tf_op | source)
XLA Modules:
  0.0 1933.7 jit_solution(4667449494425731221)
XLA Ops:
  19.3 68.0 %all-gather = f32[256,6,33]{2,1,0:T(8,128)S(1)} all-gather(f32[1,6,33]{2,1,0:T(8,128)S(1)} %maximum_bitcast_fusion), channel_id=1, replica_groups=mesh['dp'=128,'pair'=2] {'dp','pair'}, dimensions={0}, use_global_device_ids=true | all-gather | bytes 203544 | tf_op jit(solution)/shard_map/all_gather | solution.py:35
  107.1 75.7 %all-reduce.5 = (f32[1536]{0:T(1024)S(1)}, f32[]{:T(128)}) all-reduce(f32[1536]{0:T(1024)S(1)} %get-tuple-element.89, f32[]{:T(128)} %convert_reduce_fusion), channel_id=1, replica_groups=mesh['dp'=128,'pair'=2] {'dp','pair'}, use_global_device_ids=true, to_apply=%region_1.2 | all-reduce | flops 1537 | bytes 12296 | tf_op jit(solution)/shard_map/psum | solution.py:50
  183.6 74.2 %psum.37 = f32[1536]{0:T(1024)S(1)} all-reduce(f32[1536]{0:T(1024)S(1)} %fusion.119), channel_id=1, replica_groups=mesh['dp'=128,'pair'=2] {'dp','pair'}, use_global_device_ids=true, to_apply=%region_5.6 | all-reduce | flops 1536 | bytes 12288 | tf_op jit(solution)/shard_map/psum | solution.py:55
  263.7 710.0 %fusion = f32[8,1536]{1,0:T(8,128)S(1)} fusion(f32[1536,1536]{1,0:T(8,128)} %fusion.124), kind=kCustom, calls=%all-reduce-scatter | all-reduce-scatter fusion | flops 3145729 | bytes 9486336
  1005.4 17.9 collective-permute-start.51
  1066.3 13.1 collective-permute-start.34
  1079.4 13.1 collective-permute-start.33
  1092.6 13.1 collective-permute-start.32
  1105.7 13.1 collective-permute-start.31
  1118.9 13.1 collective-permute-start.30
  1132.0 13.1 collective-permute-start.29
  1145.2 13.1 collective-permute-start.28
  1158.3 13.1 collective-permute-start.27
  1171.5 13.1 collective-permute-start.26
  1184.6 13.1 collective-permute-start.25
  1197.8 13.1 collective-permute-start.24
  1210.9 13.1 collective-permute-start.23
  1224.1 13.1 collective-permute-start.22
  1237.2 13.1 collective-permute-start.21
  1250.4 13.1 collective-permute-start.20
  1263.5 13.1 collective-permute-start.19
  1276.7 13.1 collective-permute-start.18
  1289.8 13.1 collective-permute-start.17
  1303.0 13.1 collective-permute-start.16
  1316.1 13.3 collective-permute-start.15
  1408.4 13.7 collective-permute-start.8
  1422.1 13.1 collective-permute-start.7
  1435.3 13.1 collective-permute-start.6
  1448.4 13.1 collective-permute-start.5
  1465.7 97.2 %concatenate.45 = f32[518,1536]{1,0:T(8,128)} concatenate(f32[6,1536]{1,0:T(8,128)S(1)} %collective-permute-done.67, f32[8,1536]{1,0:T(8,128)S(1)} %collective-permute-done.66, f32[8,1536]{1,0:T(8,128)S(1)} %collective-permute-done.65, f32[8,1536]{1,0:T(8,128)S(1)} %collective-permute-done.64, f32[8,1536]{1,0:T(8,128)S(1)} %collective-permute-done.63, ...), dimensions={0} | concatenate | bytes 6365184
  1579.7 79.5 %all-reduce.4 = (f32[1536]{0:T(1024)S(1)}, f32[1536]{0:T(1024)S(1)}) all-reduce(f32[1536]{0:T(1024)S(1)} %get-tuple-element.50, f32[1536]{0:T(1024)S(1)} %get-tuple-element.49), channel_id=1, replica_groups=mesh['dp'=128,'pair'=2] {'dp','pair'}, use_global_device_ids=true, to_apply=%region_9.10 | all-reduce | flops 3072 | bytes 24576 | tf_op jit(solution)/shard_map/psum | solution.py:68
  1687.8 237.1 %all-reduce.8.cloned.1.call-done = f32[31,1536]{1,0:T(8,128)} async-done(((f32[31,1536]{1,0:T(8,128)}), f32[31,1536]{1,0:T(8,128)}) %all-reduce.8.cloned.1.call-update) | async-done | bytes 190480
  (362 shorter events, 241.1 us)
Async XLA Ops:
  7.2 1557.3 %all-gather.4.cloned.1.call-start = ((), (), s32[]{:S(2)}) async-start(), calls=%async_computation | async-start | bytes 6316032 | tf_op jit(solution)/shard_map/all_gather | solution.py:62
  7.9 1917.0 %all-reduce.8.cloned.1.call-start = ((), (), s32[]{:S(2)}) async-start(), calls=%async_computation.1 | async-start | bytes 393216
  9.7 92.4 %collective-permute-start = (bf16[15,1536]{1,0:T(8,128)(2,1)S(1)}, bf16[15,1536]{1,0:T(8,128)(2,1)S(1)}, u32[]{:S(2)}, u32[]{:S(2)}) collective-permute-start(bf16[15,1536]{1,0:T(8,128)(2,1)S(1)} %get-tuple-element.93), channel_id=1, source_target_pairs={{0,1},{1,2},{2,3},{3,4},{4,5},{5,6},{6,7},{7,8},{8,9},{9,10},{10,1... | collective-permute-start | bytes 138248 | tf_op jit(solution)/shard_map/ppermute | solution.py:17
  14.3 87.8 %collective-permute-start.1 = (bf16[15,1536]{1,0:T(8,128)(2,1)S(1)}, bf16[15,1536]{1,0:T(8,128)(2,1)S(1)}, u32[]{:S(2)}, u32[]{:S(2)}) collective-permute-start(bf16[15,1536]{1,0:T(8,128)(2,1)S(1)} %get-tuple-element.94), channel_id=1, source_target_pairs={{1,0},{2,1},{3,2},{4,3},{5,4},{6,5},{7,6},{8,7},{9,8},{10,9},{11,1... | collective-permute-start | bytes 138248 | tf_op jit(solution)/shard_map/ppermute | solution.py:19
  1060.2 58.7 %collective-permute-start.35 = (f32[8,1536]{1,0:T(8,128)S(1)}, f32[8,1536]{1,0:T(8,128)S(1)}, u32[]{:S(2)}, u32[]{:S(2)}) collective-permute-start(f32[8,1536]{1,0:T(8,128)S(1)} %fusion), channel_id=1, source_target_pairs={{0,32},{1,33},{2,34},{3,35},{4,36},{5,37},{6,38},{7,39},{8,40},{9,... | collective-permute-start | bytes 147464
  1066.3 65.7 %collective-permute-start.34 = (f32[8,1536]{1,0:T(8,128)S(1)}, f32[8,1536]{1,0:T(8,128)S(1)}, u32[]{:S(2)}, u32[]{:S(2)}) collective-permute-start(f32[8,1536]{1,0:T(8,128)S(1)} %fusion), channel_id=1, source_target_pairs={{0,31},{1,32},{2,33},{3,34},{4,35},{5,36},{6,37},{7,38},{8,39},{9,... | collective-permute-start | bytes 147464
  1079.4 65.7 %collective-permute-start.33 = (f32[8,1536]{1,0:T(8,128)S(1)}, f32[8,1536]{1,0:T(8,128)S(1)}, u32[]{:S(2)}, u32[]{:S(2)}) collective-permute-start(f32[8,1536]{1,0:T(8,128)S(1)} %fusion), channel_id=1, source_target_pairs={{0,30},{1,31},{2,32},{3,33},{4,34},{5,35},{6,36},{7,37},{8,38},{9,... | collective-permute-start | bytes 147464
  1092.6 65.7 %collective-permute-start.32 = (f32[8,1536]{1,0:T(8,128)S(1)}, f32[8,1536]{1,0:T(8,128)S(1)}, u32[]{:S(2)}, u32[]{:S(2)}) collective-permute-start(f32[8,1536]{1,0:T(8,128)S(1)} %fusion), channel_id=1, source_target_pairs={{0,29},{1,30},{2,31},{3,32},{4,33},{5,34},{6,35},{7,36},{8,37},{9,... | collective-permute-start | bytes 147464
  1105.7 65.7 %collective-permute-start.31 = (f32[8,1536]{1,0:T(8,128)S(1)}, f32[8,1536]{1,0:T(8,128)S(1)}, u32[]{:S(2)}, u32[]{:S(2)}) collective-permute-start(f32[8,1536]{1,0:T(8,128)S(1)} %fusion), channel_id=1, source_target_pairs={{0,28},{1,29},{2,30},{3,31},{4,32},{5,33},{6,34},{7,35},{8,36},{9,... | collective-permute-start | bytes 147464
  1118.9 65.7 %collective-permute-start.30 = (f32[8,1536]{1,0:T(8,128)S(1)}, f32[8,1536]{1,0:T(8,128)S(1)}, u32[]{:S(2)}, u32[]{:S(2)}) collective-permute-start(f32[8,1536]{1,0:T(8,128)S(1)} %fusion), channel_id=1, source_target_pairs={{0,27},{1,28},{2,29},{3,30},{4,31},{5,32},{6,33},{7,34},{8,35},{9,... | collective-permute-start | bytes 147464
  1132.0 65.7 %collective-permute-start.29 = (f32[8,1536]{1,0:T(8,128)S(1)}, f32[8,1536]{1,0:T(8,128)S(1)}, u32[]{:S(2)}, u32[]{:S(2)}) collective-permute-start(f32[8,1536]{1,0:T(8,128)S(1)} %fusion), channel_id=1, source_target_pairs={{0,26},{1,27},{2,28},{3,29},{4,30},{5,31},{6,32},{7,33},{8,34},{9,... | collective-permute-start | bytes 147464
  1145.2 65.7 %collective-permute-start.28 = (f32[8,1536]{1,0:T(8,128)S(1)}, f32[8,1536]{1,0:T(8,128)S(1)}, u32[]{:S(2)}, u32[]{:S(2)}) collective-permute-start(f32[8,1536]{1,0:T(8,128)S(1)} %fusion), channel_id=1, source_target_pairs={{0,25},{1,26},{2,27},{3,28},{4,29},{5,30},{6,31},{7,32},{8,33},{9,... | collective-permute-start | bytes 147464
  1158.3 65.7 %collective-permute-start.27 = (f32[8,1536]{1,0:T(8,128)S(1)}, f32[8,1536]{1,0:T(8,128)S(1)}, u32[]{:S(2)}, u32[]{:S(2)}) collective-permute-start(f32[8,1536]{1,0:T(8,128)S(1)} %fusion), channel_id=1, source_target_pairs={{0,24},{1,25},{2,26},{3,27},{4,28},{5,29},{6,30},{7,31},{8,32},{9,... | collective-permute-start | bytes 147464
  1171.5 65.7 %collective-permute-start.26 = (f32[8,1536]{1,0:T(8,128)S(1)}, f32[8,1536]{1,0:T(8,128)S(1)}, u32[]{:S(2)}, u32[]{:S(2)}) collective-permute-start(f32[8,1536]{1,0:T(8,128)S(1)} %fusion), channel_id=1, source_target_pairs={{0,23},{1,24},{2,25},{3,26},{4,27},{5,28},{6,29},{7,30},{8,31},{9,... | collective-permute-start | bytes 147464
  1184.6 65.7 %collective-permute-start.25 = (f32[8,1536]{1,0:T(8,128)S(1)}, f32[8,1536]{1,0:T(8,128)S(1)}, u32[]{:S(2)}, u32[]{:S(2)}) collective-permute-start(f32[8,1536]{1,0:T(8,128)S(1)} %fusion), channel_id=1, source_target_pairs={{0,22},{1,23},{2,24},{3,25},{4,26},{5,27},{6,28},{7,29},{8,30},{9,... | collective-permute-start | bytes 147464
  1197.8 65.7 %collective-permute-start.24 = (f32[8,1536]{1,0:T(8,128)S(1)}, f32[8,1536]{1,0:T(8,128)S(1)}, u32[]{:S(2)}, u32[]{:S(2)}) collective-permute-start(f32[8,1536]{1,0:T(8,128)S(1)} %fusion), channel_id=1, source_target_pairs={{0,21},{1,22},{2,23},{3,24},{4,25},{5,26},{6,27},{7,28},{8,29},{9,... | collective-permute-start | bytes 147464
  1210.9 65.7 %collective-permute-start.23 = (f32[8,1536]{1,0:T(8,128)S(1)}, f32[8,1536]{1,0:T(8,128)S(1)}, u32[]{:S(2)}, u32[]{:S(2)}) collective-permute-start(f32[8,1536]{1,0:T(8,128)S(1)} %fusion), channel_id=1, source_target_pairs={{0,20},{1,21},{2,22},{3,23},{4,24},{5,25},{6,26},{7,27},{8,28},{9,... | collective-permute-start | bytes 147464
  1224.1 65.7 %collective-permute-start.22 = (f32[8,1536]{1,0:T(8,128)S(1)}, f32[8,1536]{1,0:T(8,128)S(1)}, u32[]{:S(2)}, u32[]{:S(2)}) collective-permute-start(f32[8,1536]{1,0:T(8,128)S(1)} %fusion), channel_id=1, source_target_pairs={{0,19},{1,20},{2,21},{3,22},{4,23},{5,24},{6,25},{7,26},{8,27},{9,... | collective-permute-start | bytes 147464
  1237.2 65.7 %collective-permute-start.21 = (f32[8,1536]{1,0:T(8,128)S(1)}, f32[8,1536]{1,0:T(8,128)S(1)}, u32[]{:S(2)}, u32[]{:S(2)}) collective-permute-start(f32[8,1536]{1,0:T(8,128)S(1)} %fusion), channel_id=1, source_target_pairs={{0,18},{1,19},{2,20},{3,21},{4,22},{5,23},{6,24},{7,25},{8,26},{9,... | collective-permute-start | bytes 147464
  1250.4 65.7 %collective-permute-start.20 = (f32[8,1536]{1,0:T(8,128)S(1)}, f32[8,1536]{1,0:T(8,128)S(1)}, u32[]{:S(2)}, u32[]{:S(2)}) collective-permute-start(f32[8,1536]{1,0:T(8,128)S(1)} %fusion), channel_id=1, source_target_pairs={{0,17},{1,18},{2,19},{3,20},{4,21},{5,22},{6,23},{7,24},{8,25},{9,... | collective-permute-start | bytes 147464
  1263.5 65.9 %collective-permute-start.19 = (f32[8,1536]{1,0:T(8,128)S(1)}, f32[8,1536]{1,0:T(8,128)S(1)}, u32[]{:S(2)}, u32[]{:S(2)}) collective-permute-start(f32[8,1536]{1,0:T(8,128)S(1)} %fusion), channel_id=1, source_target_pairs={{0,16},{1,17},{2,18},{3,19},{4,20},{5,21},{6,22},{7,23},{8,24},{9,... | collective-permute-start | bytes 147464
  1276.7 65.9 %collective-permute-start.18 = (f32[8,1536]{1,0:T(8,128)S(1)}, f32[8,1536]{1,0:T(8,128)S(1)}, u32[]{:S(2)}, u32[]{:S(2)}) collective-permute-start(f32[8,1536]{1,0:T(8,128)S(1)} %fusion), channel_id=1, source_target_pairs={{0,15},{1,16},{2,17},{3,18},{4,19},{5,20},{6,21},{7,22},{8,23},{9,... | collective-permute-start | bytes 147464
  1289.8 65.9 %collective-permute-start.17 = (f32[8,1536]{1,0:T(8,128)S(1)}, f32[8,1536]{1,0:T(8,128)S(1)}, u32[]{:S(2)}, u32[]{:S(2)}) collective-permute-start(f32[8,1536]{1,0:T(8,128)S(1)} %fusion), channel_id=1, source_target_pairs={{0,14},{1,15},{2,16},{3,17},{4,18},{5,19},{6,20},{7,21},{8,22},{9,... | collective-permute-start | bytes 147464
  1303.0 65.9 %collective-permute-start.16 = (f32[8,1536]{1,0:T(8,128)S(1)}, f32[8,1536]{1,0:T(8,128)S(1)}, u32[]{:S(2)}, u32[]{:S(2)}) collective-permute-start(f32[8,1536]{1,0:T(8,128)S(1)} %fusion), channel_id=1, source_target_pairs={{0,13},{1,14},{2,15},{3,16},{4,17},{5,18},{6,19},{7,20},{8,21},{9,... | collective-permute-start | bytes 147464
  1316.1 65.9 %collective-permute-start.15 = (f32[8,1536]{1,0:T(8,128)S(1)}, f32[8,1536]{1,0:T(8,128)S(1)}, u32[]{:S(2)}, u32[]{:S(2)}) collective-permute-start(f32[8,1536]{1,0:T(8,128)S(1)} %fusion), channel_id=1, source_target_pairs={{0,12},{1,13},{2,14},{3,15},{4,16},{5,17},{6,18},{7,19},{8,20},{9,... | collective-permute-start | bytes 147464
  1329.5 65.7 %collective-permute-start.14 = (f32[8,1536]{1,0:T(8,128)S(1)}, f32[8,1536]{1,0:T(8,128)S(1)}, u32[]{:S(2)}, u32[]{:S(2)}) collective-permute-start(f32[8,1536]{1,0:T(8,128)S(1)} %fusion), channel_id=1, source_target_pairs={{0,11},{1,12},{2,13},{3,14},{4,15},{5,16},{6,17},{7,18},{8,19},{9,... | collective-permute-start | bytes 147464
  1342.6 65.7 %collective-permute-start.13 = (f32[8,1536]{1,0:T(8,128)S(1)}, f32[8,1536]{1,0:T(8,128)S(1)}, u32[]{:S(2)}, u32[]{:S(2)}) collective-permute-start(f32[8,1536]{1,0:T(8,128)S(1)} %fusion), channel_id=1, source_target_pairs={{0,10},{1,11},{2,12},{3,13},{4,14},{5,15},{6,16},{7,17},{8,18},{9,... | collective-permute-start | bytes 147464
  1355.8 66.3 %collective-permute-start.12 = (f32[8,1536]{1,0:T(8,128)S(1)}, f32[8,1536]{1,0:T(8,128)S(1)}, u32[]{:S(2)}, u32[]{:S(2)}) collective-permute-start(f32[8,1536]{1,0:T(8,128)S(1)} %fusion), channel_id=1, source_target_pairs={{0,9},{1,10},{2,11},{3,12},{4,13},{5,14},{6,15},{7,16},{8,17},{9,1... | collective-permute-start | bytes 147464
  1368.9 66.3 %collective-permute-start.11 = (f32[8,1536]{1,0:T(8,128)S(1)}, f32[8,1536]{1,0:T(8,128)S(1)}, u32[]{:S(2)}, u32[]{:S(2)}) collective-permute-start(f32[8,1536]{1,0:T(8,128)S(1)} %fusion), channel_id=1, source_target_pairs={{0,8},{1,9},{2,10},{3,11},{4,12},{5,13},{6,14},{7,15},{8,16},{9,17... | collective-permute-start | bytes 147464
  1382.1 66.3 %collective-permute-start.10 = (f32[8,1536]{1,0:T(8,128)S(1)}, f32[8,1536]{1,0:T(8,128)S(1)}, u32[]{:S(2)}, u32[]{:S(2)}) collective-permute-start(f32[8,1536]{1,0:T(8,128)S(1)} %fusion), channel_id=1, source_target_pairs={{0,7},{1,8},{2,9},{3,10},{4,11},{5,12},{6,13},{7,14},{8,15},{9,16}... | collective-permute-start | bytes 147464
  1395.2 66.3 %collective-permute-start.9 = (f32[8,1536]{1,0:T(8,128)S(1)}, f32[8,1536]{1,0:T(8,128)S(1)}, u32[]{:S(2)}, u32[]{:S(2)}) collective-permute-start(f32[8,1536]{1,0:T(8,128)S(1)} %fusion), channel_id=1, source_target_pairs={{0,6},{1,7},{2,8},{3,9},{4,10},{5,11},{6,12},{7,13},{8,14},{9,15},... | collective-permute-start | bytes 147464
  1408.4 56.6 %collective-permute-start.8 = (f32[8,1536]{1,0:T(8,128)S(1)}, f32[8,1536]{1,0:T(8,128)}, u32[]{:S(2)}, u32[]{:S(2)}) collective-permute-start(f32[8,1536]{1,0:T(8,128)S(1)} %fusion), channel_id=1, source_target_pairs={{0,5},{1,6},{2,7},{3,8},{4,9},{5,10},{6,11},{7,12},{8,13},{9,14},{... | collective-permute-start | bytes 147464
  (126 other events, 11473.5 us)
Sparse Core Ops, SparseCore 0:
  11.9 120.5 all-gather.3
  1677.9 246.9 all-reduce.7
where the time goes:
time: 1950 us; the launch traced here: 1930 us
  blocking collectives  1010 us (52%)
  starting transfers between devices  502 us (26%)
  waiting for transfers between devices  239 us (12%)
  local copies, waits for them, and re-layouts  129 us (7%)
  other arithmetic  27.6 us (1%)
    unnamed x1, blocking collectives  710 us
    unnamed x65, starting transfers between devices  489 us
    unnamed x67, waiting for transfers between devices  239 us
    unnamed x183, local copies, waits for them, and re-layouts  109 us
    psum x1, blocking collectives, local(): lax.psum((jnp.sum(grad_pre * normed, axis=0), jnp.sum(grad_pre, axis=0)),...  79.5 us
    psum x1, blocking collectives, local(): lax.psum((jnp.sum(weight_col * conv, axis=0), jnp.sum(weight_col)), ('dp'...  75.7 us
    psum x1, blocking collectives, local(): lax.psum(jnp.sum(weight_col * centred * centred, axis=0), ('dp', 'pair'))  74.2 us
    all_gather x1, blocking collectives, local(): params_full = lax.all_gather(stacked, ('dp', 'pair'), axis=1, tiled=True)  68 us
  transfers between devices with their start and end apart: 70, of which 3 were waited for; matrix products, arithmetic and copies ran while one was open for 44% of the time, Pallas kernels for 0%

commit v1 on v0

v1 whole, which is shorter than its diff:
```python
import jax
import jax.numpy as jnp
from jax import lax
from jax.experimental import pallas as pl
from jax.experimental.pallas import tpu as pltpu
from jax.sharding import Mesh, PartitionSpec as P

Z, X, Y, CORES = 8, 4, 4, 2
GROUP = Z * CORES
SETS = X * Y
KERNEL = 31
HALF = KERNEL // 2
D = 1536
ROWS = 128
OWN = D // (GROUP * SETS)
CHAN = OWN * SETS
HALO = 16
LANES = 128
BLOCK = CORES * ROWS
SPAN = BLOCK + 2 * HALO
SENT = ROWS + HALO
CHUNK = 64
MASK_LANE, HIGH_LANE, LOW_LANE, KEEP_LANE = CHAN, CHAN + 1, CHAN + 2, CHAN + 3
ALL = ("z", "x", "y", "core")
IN_GROUP = ("z", "core")
OVER_SETS = ("x", "y")
F32, BF16 = jnp.float32, jnp.bfloat16


def call(body, outs, ins, scratch, name, **more):
    return pl.pallas_call(
        body,
        out_shape=outs,
        scratch_shapes=scratch,
        name=name,
        compiler_params=pltpu.CompilerParams(vmem_limit_bytes=24 * 2**20),
        **more,
    )(*ins)


def vmem():
    return pl.BlockSpec(memory_space=pltpu.VMEM)


def smem():
    return pl.BlockSpec(memory_space=pltpu.SMEM)


def one_hot():
    col = lax.broadcasted_iota(jnp.int32, (1, 4 * LANES), 1)
    lane = col % LANES
    piece = col // LANES
    source = (
        (piece // 2) * (D // Z) + (lane // OWN) * (CORES * OWN) + (piece % 2) * OWN + lane % OWN
    )
    source = jnp.where(lane < CHAN, source, -1)
    row = lax.broadcasted_iota(jnp.int32, (2 * D // Z, 4 * LANES), 0)
    return jnp.where(row == source, 1.0, 0.0).astype(BF16)


def split_body(core_ref, own_ref, halo_ref, ext_ref, out_ref, rows_ref):
    @pl.when(core_ref[0] == 0)
    def _():
        rows_ref[0:HALO] = halo_ref[...]
        rows_ref[HALO:SENT] = own_ref[...]

    @pl.when(core_ref[0] != 0)
    def _():
        rows_ref[0:ROWS] = own_ref[...]
        rows_ref[ROWS:SENT] = halo_ref[...]

    ext = ext_ref[...].astype(F32)
    keep = ext[:, KEEP_LANE : KEEP_LANE + 1] > 0.5
    permute = one_hot()
    width = 2 * D // Z
    for part in range(Z // 2):
        piece = rows_ref[:, part * width : (part + 1) * width].astype(F32)
        piece = jnp.where(keep, piece, 0.0).astype(BF16)
        moved = jnp.dot(piece, permute, preferred_element_type=F32)
        for i in range(4):
            out_ref[4 * part + i] = (moved[:, i * LANES : (i + 1) * LANES] + ext).astype(BF16)


def segment_rows(x):
    seg = x[:, HIGH_LANE : HIGH_LANE + 1] * 256.0 + x[:, LOW_LANE : LOW_LANE + 1]
    return jnp.broadcast_to(seg, x.shape)


def mask_rows(x):
    return jnp.broadcast_to(x[:, MASK_LANE : MASK_LANE + 1], x.shape)


def conv_body(x_ref, wp_ref, conv_ref, stat_ref, par_ref, w_ref, wide_ref, xf_ref, seg_ref, m_ref, tmp_ref, wf_ref):
    tmp_ref[...] = jnp.zeros_like(tmp_ref)
    wf_ref[...] = jnp.zeros_like(wf_ref)
    for d in range(SETS):
        piece = wp_ref[d].astype(F32)
        high, mid, low = (piece[:, D + i * LANES : D + (i + 1) * LANES] for i in range(3))
        tmp_ref[d * OWN : (d + 1) * OWN] = high + mid + low
        wf_ref[d * OWN : (d + 1) * OWN] = piece[:, :D]
    wide = wf_ref[...].astype(BF16)
    wide_ref[...] = wide
    w_ref[...] = wide[:CHAN]
    par_ref[...] = tmp_ref[...].T[: par_ref.shape[0]]

    def block(b, carry):
        x = x_ref[b].astype(F32)
        xf_ref[...] = x
        seg_ref[...] = segment_rows(x)
        m_ref[b] = mask_rows(x[HALO : HALO + BLOCK])
        for chunk in range(BLOCK // CHUNK):
            base = HALO + chunk * CHUNK
            here = seg_ref[base : base + CHUNK]
            total = jnp.zeros((CHUNK, LANES), F32)
            for k in range(KERNEL):
                at = base + k - HALF
                near = jnp.where(seg_ref[at : at + CHUNK] == here, xf_ref[at : at + CHUNK], 0.0)
                total = total + par_ref[k : k + 1] * near
            conv_ref[b, chunk * CHUNK : (chunk + 1) * CHUNK] = total
        return carry

    lax.fori_loop(0, Z, block, 0)

    def first(b, carry):
        count, total = carry
        m = m_ref[b]
        return (
            count + jnp.sum(m.reshape(-1, 8, LANES), axis=0),
            total + jnp.sum((m * conv_ref[b]).reshape(-1, 8, LANES), axis=0),
        )

    zero = jnp.zeros((8, LANES), F32)
    count, total = lax.fori_loop(0, Z, first, (zero, zero))
    count = jnp.sum(count, axis=0, keepdims=True)
    total = jnp.sum(total, axis=0, keepdims=True)
    mean = total / count

    def second(b, spread):
        off = conv_ref[b] - mean
        return spread + jnp.sum((m_ref[b] * off * off).reshape(-1, 8, LANES), axis=0)

    spread = jnp.sum(lax.fori_loop(0, Z, second, zero), axis=0, keepdims=True)
    pad = jnp.zeros((5, LANES), F32)
    rows = jnp.concatenate([count, total, spread, pad], axis=0)
    for d in range(SETS):
        stat_ref[d] = rows


def moments(stat_ref):
    each = [stat_ref[d] for d in range(SETS)]
    count = sum(e[0:1] for e in each)
    mean = sum(e[1:2] for e in each) / count
    spread = sum(e[2:3] for e in each)
    for e in each:
        off = e[1:2] / e[0:1] - mean
        spread = spread + e[0:1] * off * off
    inv_std = lax.rsqrt(spread / count + 1e-05)
    return count, mean, inv_std


def grad_body(
    conv_ref, x_ref, cot_ref, wide_ref, par_ref, stat_ref,
    act_ref, gp_ref, nm_ref, first_ref, last_ref, sum_ref, gw_ref,
    total_ref, acc_ref,
):
    step = pl.program_id(0)
    count, mean, inv_std = moments(stat_ref)
    m = mask_rows(x_ref[0, HALO : HALO + BLOCK].astype(F32))
    scale = par_ref[KERNEL : KERNEL + 1]
    shift = par_ref[KERNEL + 1 : KERNEL + 2]
    normed = (conv_ref[0] - mean) * inv_std
    pre = scale * normed + shift
    sig = jax.nn.sigmoid(pre)
    act = (m * pre * sig).astype(BF16)
    act_ref[0] = act[:ROWS]
    act_ref[1] = act[ROWS:]
    cot = cot_ref[...].reshape(BLOCK, D)
    grad_act = lax.dot_general(
        cot, wide_ref[...], (((1,), (1,)), ((), ())), preferred_element_type=F32
    )
    gp = m * grad_act * sig * (1.0 + pre * (1.0 - sig))
    nm = m * normed
    gp_ref[0] = gp
    nm_ref[0] = nm
    lane = lax.broadcasted_iota(jnp.int32, (HALO, LANES), 1)
    for ref, at in ((first_ref, 0), (last_ref, BLOCK - HALO)):
        ref[0, 0] = gp[at : at + HALO].astype(BF16)
        ref[0, 1] = jnp.where(
            lane == MASK_LANE, m[at : at + HALO], nm[at : at + HALO]
        ).astype(BF16)

    @pl.when(step == 0)
    def _():
        total_ref[...] = jnp.zeros_like(total_ref)
        acc_ref[...] = jnp.zeros_like(acc_ref)

    acc_ref[0] += jnp.sum((gp * normed).reshape(-1, 8, LANES), axis=0)
    acc_ref[1] += jnp.sum(gp.reshape(-1, 8, LANES), axis=0)
    total_ref[...] += lax.dot_general(
        act, cot, (((0,), (0,)), ((), ())), preferred_element_type=F32
    )

    @pl.when(step == Z - 1)
    def _():
        rows = jnp.concatenate(
            [
                jnp.sum(acc_ref[0], axis=0, keepdims=True),
                jnp.sum(acc_ref[1], axis=0, keepdims=True),
                jnp.zeros((6, LANES), F32),
            ],
            axis=0,
        )
        for d in range(SETS):
            sum_ref[d] = rows
            gw_ref[d] = total_ref[d * OWN : (d + 1) * OWN].astype(BF16)


def back_body(
    set_ref, gp_ref, nm_ref, x_ref, par_ref, stat_ref, sum_ref, left_ref, right_ref, act_ref, gw_ref,
    pack_ref, gwp_ref, sums_ref,
    gc_ref, xf_ref, seg_ref, tap_ref, tmp_ref,
):
    count, mean, inv_std = moments(stat_ref)
    both = sum_ref[0]
    for d in range(1, SETS):
        both = both + sum_ref[d]
    sums_ref[...] = both
    gain = par_ref[KERNEL : KERNEL + 1] * inv_std
    by_norm = both[0:1] / count
    by_one = both[1:2] / count
    tap_ref[...] = jnp.zeros_like(tap_ref)
    where_am_i = set_ref[0]

    def outside(ref, b):
        gp = ref[b, 0].astype(F32)
        nm = ref[b, 1].astype(F32)
        return gain * (gp - by_one * mask_rows(nm) - by_norm * nm)

    def block(b, carry):
        x = x_ref[b].astype(F32)
        xf_ref[...] = x
        seg_ref[...] = segment_rows(x)
        before = jnp.where(where_am_i == 0, jnp.maximum(b - 1, 0), b)
        after = jnp.where(where_am_i == SETS - 1, jnp.minimum(b + 1, Z - 1), b)
        gc_ref[0:HALO] = outside(left_ref, before)
        gc_ref[HALO + BLOCK : SPAN] = outside(right_ref, after)
        m = mask_rows(x[HALO : HALO + BLOCK])
        gc_ref[HALO : HALO + BLOCK] = gain * (gp_ref[b] - by_one * m - by_norm * nm_ref[b])
        pieces = []
        for chunk in range(BLOCK // CHUNK):
            base = HALO + chunk * CHUNK
            here = seg_ref[base : base + CHUNK]
            centre = xf_ref[base : base + CHUNK]
            total = jnp.zeros((CHUNK, LANES), F32)
            for k in range(KERNEL):
                at = base + HALF - k
                near = jnp.where(seg_ref[at : at + CHUNK] == here, gc_ref[at : at + CHUNK], 0.0)
                total = total + par_ref[k : k + 1] * near
                tap_ref[k] += jnp.sum((centre * near).reshape(-1, 8, LANES), axis=0)
            pieces.append(total)
        for core in range(CORES):
            half = jnp.concatenate(
                pieces[core * (ROWS // CHUNK) : (core + 1) * (ROWS // CHUNK)], axis=0
            )
            half = half * m[core * ROWS : (core + 1) * ROWS]
            turned = pltpu.roll(half, CHAN, 1)
            at = CORES * b + core
            lane = lax.broadcasted_iota(jnp.int32, (ROWS, LANES), 1)
            pack_ref[at, 0:ROWS] = jnp.where(
                lane < CHAN, act_ref[at].astype(F32), turned
            ).astype(BF16)
            lane = lane[: ROWS // 2]
            pack_ref[at, ROWS : ROWS + ROWS // 2] = jnp.where(
                lane < LANES // 2, turned[: ROWS // 2], pltpu.roll(turned[ROWS // 2 :], LANES // 2, 1)
            ).astype(BF16)
        return carry

    lax.fori_loop(0, Z, block, 0)
    tmp_ref[...] = jnp.zeros_like(tmp_ref)
    tmp_ref[0:32] = jnp.sum(tap_ref[...], axis=1)
    tmp_ref[...] = tmp_ref[...].T
    for d in range(SETS):
        gwp_ref[d, :, :D] = gw_ref[d]
        taps = tmp_ref[d * OWN : (d + 1) * OWN]
        high = taps.astype(BF16)
        gwp_ref[d, :, D : D + LANES] = high
        gwp_ref[d, :, D + LANES : D + 2 * LANES] = (taps - high.astype(F32)).astype(BF16)


def join_body(pack_ref, w_ref, out_ref, gh_ref, four_ref):
    permute = one_hot()
    lane = lax.broadcasted_iota(jnp.int32, (ROWS // 2, LANES), 1)
    width = 2 * D // Z
    total = jnp.zeros((ROWS, D), F32)
    for part in range(Z // 2):
        for i in range(4):
            at = 4 * part + i
            main = pack_ref[at, 0:ROWS]
            total = total + jnp.dot(
                main[:, :CHAN], w_ref[at * CHAN : (at + 1) * CHAN], preferred_element_type=F32
            )
            main = main.astype(F32)
            rest = pack_ref[at, ROWS : ROWS + ROWS // 2].astype(F32)
            upper = jnp.where(lane < LANES // 2, rest, main[: ROWS // 2])
            lower = jnp.where(lane < LANES // 2, pltpu.roll(rest, LANES // 2, 1), main[ROWS // 2 :])
            turned = jnp.concatenate([upper, lower], axis=0)
            four_ref[:, i * LANES : (i + 1) * LANES] = pltpu.roll(turned, LANES - CHAN, 1).astype(BF16)
        gh_ref[:, part * width : (part + 1) * width] = lax.dot_general(
            four_ref[...], permute, (((1,), (1,)), ((), ())), preferred_element_type=F32
        ).astype(BF16)
    out_ref[...] = total.astype(BF16)


def shape(dims, kind):
    return jax.ShapeDtypeStruct(dims, kind)


def local(hidden_in, segment_ids, frame_mask, dw_kernel, norm_scale, norm_shift, out_weight, cotangent):
    core = lax.axis_index("core")
    here = lax.axis_index(ALL)
    this_set = lax.axis_index(OVER_SETS)

    with jax.named_scope("cotangent_of_group"):
        cot_all = lax.all_gather(cotangent, IN_GROUP)

    with jax.named_scope("rows_and_params"):
        params = jnp.concatenate([dw_kernel, norm_scale[None], norm_shift[None]], axis=0).T
        params = jnp.pad(params, ((0, 0), (0, LANES - params.shape[1])))
        high = lax.reduce_precision(params, 8, 7)
        rest = params - high
        mid = lax.reduce_precision(rest, 8, 7)
        low = rest - mid
        sent = jnp.concatenate([out_weight] + [p.astype(BF16) for p in (high, mid, low)], axis=1)
        sent = lax.optimization_barrier(jnp.broadcast_to(sent[None], (SETS,) + sent.shape))
        wp = lax.all_to_all(sent, OVER_SETS, 0, 0)

    with jax.named_scope("edge_frames"):
        edge = jnp.where(core == 1, hidden_in[ROWS - HALO :], hidden_in[:HALO])
        edge_mask = jnp.where(core == 1, frame_mask[ROWS - HALO :], frame_mask[:HALO])
        edge = jnp.where(edge_mask[:, None] == 1, edge, jnp.zeros_like(edge))
        last = Z * SETS * CORES - 1
        pairs = [(i, i + 1) for i in range(1, last, 2)] + [(i + 1, i) for i in range(1, last, 2)]
        halo = lax.ppermute(edge, ALL, pairs)

    with jax.named_scope("frames_to_channels"):
        mask = frame_mask.astype(F32)
        zeros, ones = jnp.zeros((HALO,), F32), jnp.ones((HALO,), F32)
        mask_col = jnp.where(
            core == 1, jnp.concatenate([mask, zeros]), jnp.concatenate([zeros, mask])
        )
        keep_col = jnp.where(core == 1, jnp.concatenate([mask, ones]), jnp.concatenate([ones, mask]))
        seg_pad = jnp.pad(segment_ids, (HALO, HALO), constant_values=-1)
        seg = lax.dynamic_slice_in_dim(seg_pad, here * ROWS + core * HALO, SENT)
        columns = (
            (MASK_LANE, mask_col),
            (HIGH_LANE, (seg >> 8).astype(F32)),
            (LOW_LANE, (seg & 255).astype(F32)),
            (KEEP_LANE, keep_col),
        )
        lane = lax.broadcasted_iota(jnp.int32, (SENT, LANES), 1)
        ext = jnp.zeros((SENT, LANES), F32)
        for at, column in columns:
            ext = jnp.where(lane == at, column[:, None], ext)
        frames = call(
            split_body,
            shape((GROUP, SENT, LANES), BF16),
            (core.reshape(1), hidden_in, halo, ext.astype(BF16)),
            [pltpu.VMEM((SENT, D), BF16)],
            "split",
            in_specs=[smem(), vmem(), vmem(), vmem()],
            out_specs=vmem(),
        )
        x = lax.all_to_all(frames, IN_GROUP, 0, 0).reshape(Z, SPAN, LANES)

    with jax.named_scope("conv"):
        conv, stat, par, rows, wide = call(
            conv_body,
            (
                shape((Z, BLOCK, LANES), F32),
                shape((SETS, 8, LANES), F32),
                shape((40, LANES), F32),
                shape((CHAN, D), BF16),
                shape((LANES, D), BF16),
            ),
            (x, wp),
            [
                pltpu.VMEM((SPAN, LANES), F32),
                pltpu.VMEM((SPAN, LANES), F32),
                pltpu.VMEM((Z, BLOCK, LANES), F32),
                pltpu.VMEM((LANES, LANES), F32),
                pltpu.VMEM((LANES, D), F32),
            ],
            "conv",
            in_specs=[vmem()] * 2,
            out_specs=[vmem()] * 5,
        )

    with jax.named_scope("weights_of_group"):
        w_all = lax.all_gather(rows, IN_GROUP, tiled=True)

    with jax.named_scope("norm_sums"):
        stat = lax.all_to_all(stat, OVER_SETS, 0, 0)

    with jax.named_scope("activation_grad"):
        whole = lambda *dims: pl.BlockSpec(dims, lambda i: (0,) * len(dims))
        act, gp, nm, first, last_rows, sums, gw = call(
            grad_body,
            (
                shape((GROUP, ROWS, LANES), BF16),
                shape((Z, BLOCK, LANES), F32),
                shape((Z, BLOCK, LANES), F32),
                shape((Z, 2, HALO, LANES), BF16),
                shape((Z, 2, HALO, LANES), BF16),
                shape((SETS, 8, LANES), F32),
                shape((SETS, OWN, D), BF16),
            ),
            (conv, x, cot_all, wide, par, stat),
            [pltpu.VMEM((LANES, D), F32), pltpu.VMEM((2, 8, LANES), F32)],
            "activation",
            grid=(Z,),
            in_specs=[
                pl.BlockSpec((1, BLOCK, LANES), lambda i: (i, 0, 0)),
                pl.BlockSpec((1, SPAN, LANES), lambda i: (i, 0, 0)),
                pl.BlockSpec((CORES, ROWS, D), lambda i: (i, 0, 0)),
                whole(LANES, D),
                whole(40, LANES),
                whole(SETS, 8, LANES),
            ],
            out_specs=[
                pl.BlockSpec((CORES, ROWS, LANES), lambda i: (i, 0, 0)),
                pl.BlockSpec((1, BLOCK, LANES), lambda i: (i, 0, 0)),
                pl.BlockSpec((1, BLOCK, LANES), lambda i: (i, 0, 0)),
                pl.BlockSpec((1, 2, HALO, LANES), lambda i: (i, 0, 0, 0)),
                pl.BlockSpec((1, 2, HALO, LANES), lambda i: (i, 0, 0, 0)),
                whole(SETS, 8, LANES),
                whole(SETS, OWN, D),
            ],
        )

    with jax.named_scope("edge_grads"):
        up = [(i, (i + 1) % SETS) for i in range(SETS)]
        down = [((i + 1) % SETS, i) for i in range(SETS)]
        left = lax.ppermute(last_rows, OVER_SETS, up)
        right = lax.ppermute(first, OVER_SETS, down)

    with jax.named_scope("norm_grad_sums"):
        sums = lax.all_to_all(sums, OVER_SETS, 0, 0)

    with jax.named_scope("conv_grad"):
        pack, gwp, both = call(
            back_body,
            (
                shape((GROUP, ROWS + ROWS // 2, LANES), BF16),
                shape((SETS, OWN, D + 2 * LANES), BF16),
                shape((8, LANES), F32),
            ),
            (this_set.reshape(1), gp, nm, x, par, stat, sums, left, right, act, gw),
            [
                pltpu.VMEM((SPAN, LANES), F32),
                pltpu.VMEM((SPAN, LANES), F32),
                pltpu.VMEM((SPAN, LANES), F32),
                pltpu.VMEM((32, 8, LANES), F32),
                pltpu.VMEM((LANES, LANES), F32),
            ],
            "conv_grad",
            in_specs=[smem()] + [vmem()] * 10,
            out_specs=[vmem()] * 3,
        )

    with jax.named_scope("weight_grad_sums"):
        gathered = lax.all_to_all(gwp, OVER_SETS, 0, 0)
        own = jnp.sum(gathered.astype(F32), axis=0)
        grad_weight = own[:, :D]
        grad_kernel = (own[:, D : D + KERNEL] + own[:, D + LANES : D + LANES + KERNEL]).T
        grad_scale = lax.dynamic_slice(both, (0, this_set * OWN), (1, OWN))[0]
        grad_shift = lax.dynamic_slice(both, (1, this_set * OWN), (1, OWN))[0]

    with jax.named_scope("channels_to_frames"):
        back = lax.all_to_all(pack, IN_GROUP, 0, 0)
        module_out, grad_hidden = call(
            join_body,
            (shape((ROWS, D), BF16), shape((ROWS, D), BF16)),
            (back, w_all),
            [pltpu.VMEM((ROWS, 4 * LANES), BF16)],
            "join",
            in_specs=[vmem()] * 2,
            out_specs=[vmem()] * 2,
        )
    return (module_out, grad_hidden, grad_kernel, grad_scale, grad_shift, grad_weight)


def solution(mesh):
    grid = Mesh(mesh.devices.reshape(Z, X, Y, CORES), ALL)
    return jax.shard_map(
        local,
        mesh=grid,
        in_specs=(P(ALL, None), P(), P(ALL), P(None, ALL), P(ALL), P(ALL), P(ALL, None), P(ALL, None)),
        out_specs=(P(ALL, None), P(ALL, None), P(None, ALL), P(ALL), P(ALL), P(ALL, None)),
        check_vma=False,
    )
```

time: 1950 us -> 185 us (0.09)
  blocking collectives: 1010 us -> 56 us
  starting transfers between devices: 502 us -> 27.2 us
  waiting for transfers between devices: 239 us -> 36.1 us
  local copies, waits for them, and re-layouts: 129 us -> 14.7 us
  Pallas kernels: 0 us -> 30.8 us
  other arithmetic: 27.6 us -> 5.62 us
    unnamed x1 -> x0, blocking collectives: 710 us -> none
    unnamed x65 -> x0, starting transfers between devices: 489 us -> none
    unnamed x67 -> x2, waiting for transfers between devices: 239 us -> 0.7 us
    psum x3 -> x0, blocking collectives: 229 us -> none  [the longest x1 79.5 us: local(): lax.psum((jnp.sum(grad_pre * normed, axis=0), jnp.sum(grad_pre, axis=0)),...]
    unnamed x183 -> x20, local copies, waits for them, and re-layouts: 109 us -> 11.1 us
    all_gather x1 -> x0, blocking collectives: 68 us -> none  [local(): params_full = lax.all_gather(stacked, ('dp', 'pair'), axis=1, tiled=True)]
    all_to_all x0 -> x3, blocking collectives: none -> 56 us  [the longest x1 34.4 us: local(): x = lax.all_to_all(frames, IN_GROUP, 0, 0).reshape(Z, SPAN, LANES)]
    all_to_all x0 -> x3, waiting for transfers between devices: none -> 35.4 us  [the longest x1 20.8 us: local(): back = lax.all_to_all(pack, IN_GROUP, 0, 0)]
  transfers between devices with their start and end apart: 70 -> 8, of which waited for: 3 -> 3; matrix products, arithmetic and copies ran while one was open for 44% -> 5% of each run, Pallas kernels for 0% -> 15%
where the time goes in v1:
time: 185 us; the launch traced here: 184 us
  blocking collectives  56 us (30%)
  waiting for transfers between devices  36.1 us (20%)
  Pallas kernels  30.8 us (17%)
  starting transfers between devices  27.2 us (15%)
  local copies, waits for them, and re-layouts  14.7 us (8%)
  between operations  14.2 us (8%)
  other arithmetic  5.62 us (3%)
    all_to_all x1, blocking collectives, local(): x = lax.all_to_all(frames, IN_GROUP, 0, 0).reshape(Z, SPAN, LANES)  34.4 us
    pallas_call x5, Pallas kernels, call(): pl.pallas_call(body, out_shape=outs, scratch_shapes=scratch, name=name, c...  30.8 us
    all_to_all x1, waiting for transfers between devices, local(): back = lax.all_to_all(pack, IN_GROUP, 0, 0)  20.8 us
    all_to_all x1, blocking collectives, local(): gathered = lax.all_to_all(gwp, OVER_SETS, 0, 0)  12 us
    unnamed x20, local copies, waits for them, and re-layouts  11.1 us
    all_to_all x1, blocking collectives, local(): stat = lax.all_to_all(stat, OVER_SETS, 0, 0)  9.5 us
    all_to_all x1, waiting for transfers between devices, local(): wp = lax.all_to_all(sent, OVER_SETS, 0, 0)  8.08 us
    all_to_all x1, starting transfers between devices, local(): back = lax.all_to_all(pack, IN_GROUP, 0, 0)  7.77 us
  transfers between devices with their start and end apart: 8, of which 3 were waited for; matrix products, arithmetic and copies ran while one was open for 5% of the time, Pallas kernels for 15%

profile of v1, /device:TPU:1, one launch (start us, length us, event | category | flops | bytes accessed | tf_op | source)
XLA Modules:
  0.0 184.4 jit_solution(9743825314945657026)
XLA Ops:
  7.2 0.7 all-gather.6.cloned.1.call-update
  7.9 0.8 fusion.2
  8.7 0.9 select_select_fusion
  9.6 4.6 %collective-permute-start = (bf16[16,1536]{1,0:T(8,128)(2,1)S(1)}, bf16[16,1536]{1,0:T(8,128)(2,1)S(1)}, u32[]{:S(2)}, u32[]{:S(2)}) collective-permute-start(bf16[16,1536]{1,0:T(8,128)(2,1)S(1)} %select_select_fusion), channel_id=1, source_target_pairs={{1,2},{3,4},{5,6},{7,8},{9,10},{11,12},{13,14},{15,16},{17,18},{19... | collective-permute-start | bytes 147464 | tf_op jit(solution)/shard_map/edge_frames/ppermute | solution.py:343
  14.2 0.7 copy.15
  14.9 0.7 copy.14
  15.7 0.8 maximum_bitcast_fusion
  16.5 0.7 pad_maximum_fusion
  17.2 0.8 broadcast_in_dim.63
  18.0 6.5 %all-to-all-start.1 = ((bf16[16,6,1920]{2,1,0:T(8,128)(2,1)}), bf16[16,6,1920]{2,1,0:T(8,128)(2,1)S(1)}, u32[]{:S(2)}, u32[]{:S(2)}) async-start(bf16[16,6,1920]{2,1,0:T(8,128)(2,1)} %broadcast_in_dim.63), calls=%async_computation.1 | async-start | bytes 983040 | tf_op jit(solution)/shard_map/rows_and_params/all_to_all | solution.py:335
  24.6 0.8 and_convert_fusion
  26.3 1.0 copy-done.4
  27.9 8.1 %all-to-all-done.1.wp_ref = bf16[16,6,1920]{2,1,0:T(8,128)(2,1)S(1)} async-done(((bf16[16,6,1920]{2,1,0:T(8,128)(2,1)}), bf16[16,6,1920]{2,1,0:T(8,128)(2,1)S(1)}, u32[]{:S(2)}, u32[]{:S(2)}) %all-to-all-start.1) | async-done | bytes 368672 | tf_op jit(solution)/shard_map/rows_and_params/all_to_all | solution.py:335
  35.9 34.4 %all_to_all.30 = bf16[16,144,128]{2,1,0:T(8,128)(2,1)S(1)} all-to-all(bf16[16,144,128]{2,1,0:T(8,128)(2,1)S(1)} %split.1), channel_id=1, replica_groups=mesh['z'=8,'x'=4,'y'=4,'core'=2] {'z','core'}, dimensions={0} | all-to-all | bytes 1179648 | tf_op jit(solution)/shard_map/frames_to_channels/all_to_all | solution.py:373
  70.4 6.9 %conv.1 = (f32[8,256,128]{2,1,0:T(8,128)S(1)}, f32[16,8,128]{2,1,0:T(8,128)S(1)}, f32[40,128]{1,0:T(8,128)S(1)}, bf16[96,1536]{1,0:T(8,128)(2,1)}, bf16[128,1536]{1,0:T(8,128)(2,1)S(1)}) custom-call(bf16[8,288,128]{2,1,0:T(8,128)(2,1)S(1)} %bitcast.14, bf16[16,6,1920]{2,1,0:T(8,128)(2,1)S(1)} %all-to-all-done.1.wp_ref), custom_call_target="tpu_custom_call" | custom-call | tf_op jit(solution)/shard_map/conv/conv/pallas_call | solution.py:31
  77.3 1.0 copy-done.2
  78.3 9.5 %all_to_all.31.stat_ref = f32[16,8,128]{2,1,0:T(8,128)S(1)} all-to-all(f32[16,8,128]{2,1,0:T(8,128)S(1)} %get-tuple-element.26), channel_id=1, replica_groups=mesh['z'=8,'x'=4,'y'=4,'core'=2] {'x','y'}, dimensions={0} | all-to-all | bytes 131072 | tf_op jit(solution)/shard_map/norm_sums/all_to_all | solution.py:402
  87.8 2.8 %copy-done = bf16[2048,1536]{1,0:T(8,128)(2,1)S(1)} copy-done((bf16[2048,1536]{1,0:T(8,128)(2,1)S(1)}, bf16[2048,1536]{1,0:T(8,128)(2,1)}, u32[]{:S(2)}) %copy-start) | copy-done | bytes 6291480
  90.6 1.2 copy-done.3
  91.9 1.0 copy-done.8
  92.9 7.5 %activation.1 = (bf16[16,128,128]{2,1,0:T(8,128)(2,1)S(1)}, f32[8,256,128]{2,1,0:T(8,128)S(1)}, f32[8,256,128]{2,1,0:T(8,128)S(1)}, bf16[8,2,16,128]{3,2,1,0:T(8...) custom-call(f32[8,256,128]{2,1,0:T(8,128)S(1)} %copy-done.3, ...), custom_call_target="tpu_custom_call" | custom-call | tf_op jit(solution)/shard_map/activation_grad/activation/pallas_call | solution.py:31
  100.4 0.7 copy-done.5
  101.4 4.6 %collective-permute-start.2 = (bf16[8,2,16,128]{3,2,1,0:T(8,128)(2,1)}, bf16[8,2,16,128]{3,2,1,0:T(8,128)(2,1)S(1)}, u32[]{:S(2)}, u32[]{:S(2)}) collective-permute-start(bf16[8,2,16,128]{3,2,1,0:T(8,128)(2,1)} %get-tuple-element.31), channel_id=1, source_target_pairs={{2,0},{4,2},{6,4},{8,6},{10,8},{12,10},{14,12},{16,14},{18,16},{20... | collective-permute-start | bytes 196616 | tf_op jit(solution)/shard_map/edge_grads/ppermute | solution.py:444
  105.9 3.5 %all-to-all-start.3 = ((f32[16,8,128]{2,1,0:T(8,128)}), f32[16,8,128]{2,1,0:T(8,128)S(1)}, u32[]{:S(2)}, u32[]{:S(2)}) async-start(f32[16,8,128]{2,1,0:T(8,128)} %copy-done.9), calls=%async_computation.3 | async-start | bytes 131072 | tf_op jit(solution)/shard_map/norm_grad_sums/all_to_all | solution.py:447
  109.4 6.5 %all-to-all-done.3.sum_ref = f32[16,8,128]{2,1,0:T(8,128)S(1)} async-done(((f32[16,8,128]{2,1,0:T(8,128)}), f32[16,8,128]{2,1,0:T(8,128)S(1)}, u32[]{:S(2)}, u32[]{:S(2)}) %all-to-all-start.3) | async-done | bytes 65568 | tf_op jit(solution)/shard_map/norm_grad_sums/all_to_all | solution.py:447
  115.9 1.0 copy-done.6
  116.9 12.8 %conv_grad.1 = (bf16[16,192,128]{2,1,0:T(8,128)(2,1)}, bf16[16,6,1792]{2,1,0:T(8,128)(2,1)S(1)}, f32[8,128]{1,0:T(8,128)S(1)}) custom-call(s32[1]{0:T(128)} %bitcast.set_ref, f32[8,256,128]{2,1,0:T(8,128)S(1)} %get-tuple-element.27.gp_ref, f32[8,256,128]{2,1,0:T(8,128)S(1)} %get-tuple-element.28.nm_ref, bf16[8,288,128]{2,1,0:T(8,128)(2,1)S(1)} %bitcast.16, ...), custom_call_target="tpu_custom_call" | custom-call | tf_op jit(solution)/shard_map/conv_grad/conv_grad/pallas_call | solution.py:31
  129.7 12.0 %all_to_all.32 = bf16[16,6,1792]{2,1,0:T(8,128)(2,1)S(1)} all-to-all(bf16[16,6,1792]{2,1,0:T(8,128)(2,1)S(1)} %get-tuple-element.38), channel_id=1, replica_groups=mesh['z'=8,'x'=4,'y'=4,'core'=2] {'x','y'}, dimensions={0} | all-to-all | bytes 688128 | tf_op jit(solution)/shard_map/weight_grad_sums/all_to_all | solution.py:471
  141.8 7.8 %all-to-all-start.4 = ((bf16[16,192,128]{2,1,0:T(8,128)(2,1)}), bf16[16,192,128]{2,1,0:T(8,128)(2,1)S(1)}, u32[]{:S(2)}, u32[]{:S(2)}) async-start(bf16[16,192,128]{2,1,0:T(8,128)(2,1)} %get-tuple-element.34), calls=%async_computation.4 | async-start | bytes 1572864 | tf_op jit(solution)/shard_map/channels_to_frames/all_to_all | solution.py:479
  151.4 20.8 %all-to-all-done.4.pack_ref = bf16[16,192,128]{2,1,0:T(8,128)(2,1)S(1)} async-done(((bf16[16,192,128]{2,1,0:T(8,128)(2,1)}), bf16[16,192,128]{2,1,0:T(8,128)(2,1)S(1)}, u32[]{:S(2)}, u32[]{:S(2)}) %all-to-all-start.4) | async-done | bytes 786464 | tf_op jit(solution)/shard_map/channels_to_frames/all_to_all | solution.py:479
  172.2 2.3 %copy-done.1 = bf16[1536,1536]{1,0:T(8,128)(2,1)S(1)} copy-done((bf16[1536,1536]{1,0:T(8,128)(2,1)S(1)}, bf16[1536,1536]{1,0:T(8,128)(2,1)}, u32[]{:S(2)}) %copy-start.1) | copy-done | bytes 4718616
  174.6 3.0 %join.1 = (bf16[128,1536]{1,0:T(8,128)(2,1)}, bf16[128,1536]{1,0:T(8,128)(2,1)}) custom-call(bf16[16,192,128]{2,1,0:T(8,128)(2,1)S(1)} %all-to-all-done.4.pack_ref, bf16[1536,1536]{1,0:T(8,128)(2,1)S(1)} %copy-done.1), custom_call_target="tpu_custom_call" | custom-call | tf_op jit(solution)/shard_map/channels_to_frames/join/pallas_call | solution.py:31
  (33 shorter events, 3.7 us)
Async XLA Ops:
  7.2 80.6 %all-gather.6.cloned.1.call-start = ((), (), s32[]{:S(2)}) async-start(), calls=%async_computation.7 | async-start | bytes 6684672 | tf_op jit(solution)/shard_map/cotangent_of_group/all_gather | solution.py:324
  9.6 16.7 %collective-permute-start = (bf16[16,1536]{1,0:T(8,128)(2,1)S(1)}, bf16[16,1536]{1,0:T(8,128)(2,1)S(1)}, u32[]{:S(2)}, u32[]{:S(2)}) collective-permute-start(bf16[16,1536]{1,0:T(8,128)(2,1)S(1)} %select_select_fusion), channel_id=1, source_target_pairs={{1,2},{3,4},{5,6},{7,8},{9,10},{11,12},{13,14},{15,16},{17,18},{19... | collective-permute-start | bytes 147464 | tf_op jit(solution)/shard_map/edge_frames/ppermute | solution.py:343
  18.0 17.9 %all-to-all-start.1 = ((bf16[16,6,1920]{2,1,0:T(8,128)(2,1)}), bf16[16,6,1920]{2,1,0:T(8,128)(2,1)S(1)}, u32[]{:S(2)}, u32[]{:S(2)}) async-start(bf16[16,6,1920]{2,1,0:T(8,128)(2,1)} %broadcast_in_dim.63), calls=%async_computation.1 | async-start | bytes 983040 | tf_op jit(solution)/shard_map/rows_and_params/all_to_all | solution.py:335
  24.5 126.9 %all-gather.4.cloned.1.call-start = ((), (), s32[]{:S(2)}) async-start(), calls=%async_computation.6 | async-start | bytes 5013504 | tf_op jit(solution)/shard_map/weights_of_group/all_gather | solution.py:399
  26.3 1.0 copy-start.4
  77.3 1.0 copy-start.2
  78.3 9.5 %copy-start.7 = (bf16[128,1536]{1,0:T(8,128)(2,1)}, bf16[128,1536]{1,0:T(8,128)(2,1)S(1)}, u32[]{:S(2)}) copy-start(bf16[128,1536]{1,0:T(8,128)(2,1)S(1)} %get-tuple-element.24.wide_ref) | copy-start | bytes 1179652
  87.8 2.8 %copy-start = (bf16[2048,1536]{1,0:T(8,128)(2,1)S(1)}, bf16[2048,1536]{1,0:T(8,128)(2,1)}, u32[]{:S(2)}) copy-start(bf16[2048,1536]{1,0:T(8,128)(2,1)} %all-gather.6.cloned.1.call-done) | copy-start | bytes 18874372
  90.6 1.2 copy-start.3
  91.9 1.0 copy-start.8
  100.4 0.7 copy-start.5
  101.1 4.8 %copy-start.9 = (f32[16,8,128]{2,1,0:T(8,128)}, f32[16,8,128]{2,1,0:T(8,128)S(1)}, u32[]{:S(2)}) copy-start(f32[16,8,128]{2,1,0:T(8,128)S(1)} %get-tuple-element.29) | copy-start | bytes 196612
  101.1 14.8 %collective-permute-start.1 = (bf16[8,2,16,128]{3,2,1,0:T(8,128)(2,1)}, bf16[8,2,16,128]{3,2,1,0:T(8,128)(2,1)S(1)}, u32[]{:S(2)}, u32[]{:S(2)}) collective-permute-start(bf16[8,2,16,128]{3,2,1,0:T(8,128)(2,1)} %get-tuple-element.30), channel_id=1, source_target_pairs={{0,2},{2,4},{4,6},{6,8},{8,10},{10,12},{12,14},{14,16},{16,18},{18... | collective-permute-start | bytes 196616 | tf_op jit(solution)/shard_map/edge_grads/ppermute | solution.py:443
  101.4 14.5 %collective-permute-start.2 = (bf16[8,2,16,128]{3,2,1,0:T(8,128)(2,1)}, bf16[8,2,16,128]{3,2,1,0:T(8,128)(2,1)S(1)}, u32[]{:S(2)}, u32[]{:S(2)}) collective-permute-start(bf16[8,2,16,128]{3,2,1,0:T(8,128)(2,1)} %get-tuple-element.31), channel_id=1, source_target_pairs={{2,0},{4,2},{6,4},{8,6},{10,8},{12,10},{14,12},{16,14},{18,16},{20... | collective-permute-start | bytes 196616 | tf_op jit(solution)/shard_map/edge_grads/ppermute | solution.py:444
  105.9 10.0 %all-to-all-start.3 = ((f32[16,8,128]{2,1,0:T(8,128)}), f32[16,8,128]{2,1,0:T(8,128)S(1)}, u32[]{:S(2)}, u32[]{:S(2)}) async-start(f32[16,8,128]{2,1,0:T(8,128)} %copy-done.9), calls=%async_computation.3 | async-start | bytes 131072 | tf_op jit(solution)/shard_map/norm_grad_sums/all_to_all | solution.py:447
  115.9 1.0 copy-start.6
  141.8 30.5 %all-to-all-start.4 = ((bf16[16,192,128]{2,1,0:T(8,128)(2,1)}), bf16[16,192,128]{2,1,0:T(8,128)(2,1)S(1)}, u32[]{:S(2)}, u32[]{:S(2)}) async-start(bf16[16,192,128]{2,1,0:T(8,128)(2,1)} %get-tuple-element.34), calls=%async_computation.4 | async-start | bytes 1572864 | tf_op jit(solution)/shard_map/channels_to_frames/all_to_all | solution.py:479
  172.2 2.3 %copy-start.1 = (bf16[1536,1536]{1,0:T(8,128)(2,1)S(1)}, bf16[1536,1536]{1,0:T(8,128)(2,1)}, u32[]{:S(2)}) copy-start(bf16[1536,1536]{1,0:T(8,128)(2,1)} %all-gather.4.cloned.1.call-done.w_ref) | copy-start | bytes 14155780
Sparse Core Ops, SparseCore 0:
  9.8 62.8 all-gather.5
  78.4 37.9 all-gather.3

commit v2 on v1

v2 whole, which is shorter than its diff:
```python
import jax
import jax.numpy as jnp
from jax import lax
from jax.experimental import pallas as pl
from jax.experimental.pallas import tpu as pltpu
from jax.sharding import Mesh, PartitionSpec as P

Z, X, Y, CORES = 8, 4, 4, 2
GROUP = Z * CORES
SETS = X * Y
KERNEL = 31
HALF = KERNEL // 2
D = 1536
ROWS = 128
OWN = D // (GROUP * SETS)
CHAN = OWN * SETS
HALO = 16
LANES = 128
BLOCK = CORES * ROWS
SPAN = BLOCK + 2 * HALO
SENT = ROWS + HALO
CHUNK = 64
WIDE = D + LANES
PART = 40
MASK_LANE, PREV_LANE, NEXT_LANE = CHAN, CHAN + 1, CHAN + 2
ALL = ("z", "x", "y", "core")
IN_GROUP = ("z", "core")
OVER_SETS = ("x", "y")
F32, BF16 = jnp.float32, jnp.bfloat16


def call(body, outs, ins, scratch, name, work=0, **more):
    if work:
        more["cost_estimate"] = pl.CostEstimate(flops=work, bytes_accessed=2**20, transcendentals=0)
    return pl.pallas_call(
        body,
        out_shape=outs,
        scratch_shapes=scratch,
        name=name,
        compiler_params=pltpu.CompilerParams(vmem_limit_bytes=64 * 2**20),
        **more,
    )(*ins)


def vmem():
    return pl.BlockSpec(memory_space=pltpu.VMEM)


def hbm():
    return pl.BlockSpec(memory_space=pltpu.HBM)


def parts(x):
    high = x.astype(BF16).astype(F32)
    mid = (x - high).astype(BF16).astype(F32)
    return high, mid, (x - high - mid).astype(BF16).astype(F32)


def smem():
    return pl.BlockSpec(memory_space=pltpu.SMEM)


def one_hot():
    col = lax.broadcasted_iota(jnp.int32, (1, 4 * LANES), 1)
    lane = col % LANES
    piece = col // LANES
    source = (
        (piece // 2) * (D // Z) + (lane // OWN) * (CORES * OWN) + (piece % 2) * OWN + lane % OWN
    )
    source = jnp.where(lane < CHAN, source, -1)
    row = lax.broadcasted_iota(jnp.int32, (2 * D // Z, 4 * LANES), 0)
    return jnp.where(row == source, 1.0, 0.0).astype(BF16)


def prep_body(
    core_ref, seg_ref, taps_hbm, scale_hbm, shift_hbm, mask_hbm, w_hbm, own_hbm,
    wp_ref, ext_ref, own_ref, edge_ref,
    tmp_ref, taps_ref, scale_ref, shift_ref, mask_ref, w_ref, sem,
):
    pairs = (
        (taps_hbm, taps_ref), (scale_hbm, scale_ref), (shift_hbm, shift_ref),
        (mask_hbm, mask_ref), (w_hbm, w_ref), (own_hbm, own_ref),
    )
    copies = [pltpu.make_async_copy(a, b, sem.at[i]) for i, (a, b) in enumerate(pairs)]
    for copy in copies:
        copy.start()
    tmp_ref[...] = jnp.zeros_like(tmp_ref)
    for copy in copies:
        copy.wait()
    tmp_ref[KERNEL : KERNEL + 1, 0:OWN] = scale_ref[...]
    tmp_ref[KERNEL + 1 : KERNEL + 2, 0:OWN] = shift_ref[...]
    rows = tmp_ref[...].T
    tmp_ref[0:8] = rows[0:8]
    tmp_ref[0:OWN, 0:KERNEL] = taps_ref[...]
    high, mid, low = parts(tmp_ref[0:8])
    side = high + pltpu.roll(mid, PART, 1) + pltpu.roll(low, 2 * PART, 1)
    side = side[0:OWN].astype(BF16)
    for d in range(SETS):
        wp_ref[d, :, 0:D] = w_ref[...]
        wp_ref[d, :, D:WIDE] = side
    seg = seg_ref[...]
    own = seg[:, HALO : HALO + ROWS]
    before = jnp.zeros((1, ROWS), F32)
    after = jnp.zeros((1, ROWS), F32)
    for j in range(1, HALF + 1):
        before = before + jnp.where(seg[:, HALO - j : HALO - j + ROWS] == own, 1.0, 0.0)
        after = after + jnp.where(seg[:, HALO + j : HALO + j + ROWS] == own, 1.0, 0.0)
    tmp_ref[...] = jnp.zeros_like(tmp_ref)
    tmp_ref[MASK_LANE : MASK_LANE + 1] = mask_ref[...].astype(F32)
    tmp_ref[PREV_LANE : PREV_LANE + 1] = before
    tmp_ref[NEXT_LANE : NEXT_LANE + 1] = after
    ext = tmp_ref[...].T
    ext_ref[...] = ext
    keep = ext[:, MASK_LANE : MASK_LANE + 1] > 0.5
    own = jnp.where(keep, own_ref[...].astype(F32), 0.0).astype(BF16)
    own_ref[...] = own
    edge_ref[...] = jnp.where(core_ref[0] == 0, own[0:HALO].astype(F32), own[ROWS - HALO :].astype(F32)).astype(BF16)


def split_body(core_ref, own_ref, halo_ref, ext_ref, out_ref, rows_ref, side_ref):
    own = own_ref[...]
    none = jnp.zeros((HALO, LANES), F32)

    @pl.when(core_ref[0] == 0)
    def _():
        rows_ref[0:HALO] = halo_ref[...]
        rows_ref[HALO:SENT] = own
        side_ref[0:HALO] = none
        side_ref[HALO:SENT] = ext_ref[...]

    @pl.when(core_ref[0] != 0)
    def _():
        rows_ref[0:ROWS] = own
        rows_ref[ROWS:SENT] = halo_ref[...]
        side_ref[0:ROWS] = ext_ref[...]
        side_ref[ROWS:SENT] = none

    ext = side_ref[...]
    permute = one_hot()
    width = 2 * D // Z
    for part in range(Z // 2):
        piece = rows_ref[:, part * width : (part + 1) * width]
        moved = jnp.dot(piece, permute, preferred_element_type=F32)
        for i in range(4):
            out_ref[4 * part + i] = (moved[:, i * LANES : (i + 1) * LANES] + ext).astype(BF16)


def lane_rows(x, lane):
    return jnp.broadcast_to(x[:, lane : lane + 1], x.shape)


def mask_rows(x):
    return lane_rows(x, MASK_LANE)


def near_rows(ref, base, offset, before, after):
    rows = ref[base + offset : base + offset + CHUNK]
    if offset == 0:
        return rows
    same = before >= -offset if offset < 0 else after >= offset
    return jnp.where(same, rows, 0.0)


def conv_body(
    x_ref, wp_ref, conv_ref, stat_ref, par_ref, w_ref, wide_ref,
    xf_ref, prev_ref, next_ref, tmp_ref, wf_ref, run_ref,
):
    step = pl.program_id(0)

    @pl.when(step == 0)
    def _():
        wf_ref[CHAN:] = jnp.zeros((LANES - CHAN, WIDE), F32)
        for d in range(SETS):
            wf_ref[d * OWN : (d + 1) * OWN] = wp_ref[d].astype(F32)
        wide = wf_ref[:, 0:D].astype(BF16)
        wide_ref[...] = wide
        w_ref[...] = wide[:CHAN]
        tmp_ref[...] = wf_ref[:, D:WIDE].T
        par_ref[...] = tmp_ref[0:PART] + tmp_ref[PART : 2 * PART] + tmp_ref[2 * PART : 3 * PART]
        run_ref[...] = jnp.zeros_like(run_ref)

    x = x_ref[0].astype(F32)
    xf_ref[...] = x
    inside = x[HALO : HALO + BLOCK]
    prev_ref[...] = lane_rows(inside, PREV_LANE)
    next_ref[...] = lane_rows(inside, NEXT_LANE)
    for chunk in range(BLOCK // CHUNK):
        at = slice(chunk * CHUNK, (chunk + 1) * CHUNK)
        before, after = prev_ref[at], next_ref[at]
        total = jnp.zeros((CHUNK, LANES), F32)
        for k in range(KERNEL):
            near = near_rows(xf_ref, HALO + chunk * CHUNK, k - HALF, before, after)
            total = total + par_ref[k : k + 1] * near
        conv_ref[0, at] = total

    rows = lambda v: jnp.sum(jnp.sum(v.reshape(-1, 8, LANES), axis=0), axis=0, keepdims=True)
    m = mask_rows(inside)
    conv = conv_ref[0]
    here = rows(m)
    mean_here = rows(m * conv) / here
    off = conv - mean_here
    count, mean, spread = run_ref[0:1], run_ref[1:2], run_ref[2:3]
    both = count + here
    apart = mean_here - mean
    run_ref[0:1] = both
    run_ref[1:2] = mean + apart * (here / both)
    run_ref[2:3] = spread + rows(m * off * off) + apart * apart * (count * here / both)

    @pl.when(step == Z - 1)
    def _():
        for d in range(SETS):
            stat_ref[d] = run_ref[...]


def moments(stat_ref):
    each = [stat_ref[d] for d in range(SETS)]
    count = sum(e[0:1] for e in each)
    mean = sum(e[0:1] * e[1:2] for e in each) / count
    spread = sum(e[2:3] for e in each)
    for e in each:
        off = e[1:2] - mean
        spread = spread + e[0:1] * off * off
    inv_std = lax.rsqrt(spread / count + 1e-05)
    return count, mean, inv_std


def grad_body(
    conv_ref, x_ref, wide_ref, par_ref, stat_ref, cot_hbm,
    act_ref, gp_ref, nm_ref, first_ref, last_ref, gw_ref,
    total_ref, acc_ref, mom_ref, cot_ref, sem,
):
    step = pl.program_id(0)

    def fetch(i):
        rows = pl.ds(i * CORES, CORES)
        return pltpu.make_async_copy(cot_hbm.at[rows], cot_ref.at[rows], sem.at[i])

    @pl.when(step == 0)
    def _():
        for i in range(Z):
            fetch(i).start()

    @pl.when(step == 0)
    def _():
        total_ref[...] = jnp.zeros_like(total_ref)
        acc_ref[...] = jnp.zeros_like(acc_ref)
        count, mean, inv_std = moments(stat_ref)
        mom_ref[0:1] = mean
        mom_ref[1:2] = inv_std

    mean, inv_std = mom_ref[0:1], mom_ref[1:2]
    m = mask_rows(x_ref[0, HALO : HALO + BLOCK].astype(F32))
    scale = par_ref[KERNEL : KERNEL + 1]
    shift = par_ref[KERNEL + 1 : KERNEL + 2]
    normed = (conv_ref[0] - mean) * inv_std
    pre = scale * normed + shift
    sig = jax.nn.sigmoid(pre)
    act = (m * pre * sig).astype(BF16)
    act_ref[0] = act[:ROWS]
    act_ref[1] = act[ROWS:]
    fetch(step).wait()
    cot = cot_ref[pl.ds(step * CORES, CORES)].reshape(BLOCK, D)
    grad_act = lax.dot_general(
        cot, wide_ref[...], (((1,), (1,)), ((), ())), preferred_element_type=F32
    )
    gp = m * grad_act * sig * (1.0 + pre * (1.0 - sig))
    nm = m * normed
    gp_ref[0] = gp
    nm_ref[0] = nm
    lane = lax.broadcasted_iota(jnp.int32, (HALO, LANES), 1)
    for ref, at in ((first_ref, 0), (last_ref, BLOCK - HALO)):
        ref[0, 0] = gp[at : at + HALO].astype(BF16)
        ref[0, 1] = jnp.where(
            lane == MASK_LANE, m[at : at + HALO], nm[at : at + HALO]
        ).astype(BF16)

    acc_ref[0] += jnp.sum((gp * normed).reshape(-1, 8, LANES), axis=0)
    acc_ref[1] += jnp.sum(gp.reshape(-1, 8, LANES), axis=0)
    total_ref[...] += lax.dot_general(
        act, cot, (((0,), (0,)), ((), ())), preferred_element_type=F32
    )

    @pl.when(step == Z - 1)
    def _():
        sums = [jnp.sum(acc_ref[i], axis=0, keepdims=True) for i in range(2)]
        rows = jnp.concatenate(list(parts(sums[0])) + list(parts(sums[1])), axis=0).astype(BF16)
        for d in range(SETS):
            gw_ref[d, :, 0:D] = total_ref[d * OWN : (d + 1) * OWN].astype(BF16)
            gw_ref[d, :, D:WIDE] = rows


def back_body(
    set_ref, gp_ref, nm_ref, x_ref, act_ref, par_ref, stat_ref, sum_ref, left_ref, right_ref,
    pack_ref, taps_ref, sums_ref,
    gc_ref, xf_ref, prev_ref, next_ref, tap_ref, run_ref,
):
    b = pl.program_id(0)

    @pl.when(b == 0)
    def _():
        count, mean, inv_std = moments(stat_ref)
        each = sum_ref[0, :, D:WIDE].astype(F32)
        for d in range(1, SETS):
            each = each + sum_ref[d, :, D:WIDE].astype(F32)
        scale_sum = each[0:1] + each[1:2] + each[2:3]
        shift_sum = each[3:4] + each[4:5] + each[5:6]
        sums_ref[...] = jnp.concatenate([scale_sum, shift_sum, jnp.zeros((6, LANES), F32)], axis=0)
        run_ref[0:1] = par_ref[KERNEL : KERNEL + 1] * inv_std
        run_ref[1:2] = scale_sum / count
        run_ref[2:3] = shift_sum / count
        tap_ref[...] = jnp.zeros_like(tap_ref)

    gain, by_norm, by_one = run_ref[0:1], run_ref[1:2], run_ref[2:3]
    where_am_i = set_ref[0]

    def outside(ref, at):
        gp = ref[at, 0].astype(F32)
        nm = ref[at, 1].astype(F32)
        return gain * (gp - by_one * mask_rows(nm) - by_norm * nm)

    x = x_ref[0, HALO : HALO + BLOCK].astype(F32)
    xf_ref[...] = x
    prev_ref[...] = lane_rows(x, PREV_LANE)
    next_ref[...] = lane_rows(x, NEXT_LANE)
    gc_ref[0:HALO] = outside(left_ref, jnp.where(where_am_i == 0, jnp.maximum(b - 1, 0), b))
    gc_ref[HALO + BLOCK : SPAN] = outside(
        right_ref, jnp.where(where_am_i == SETS - 1, jnp.minimum(b + 1, Z - 1), b)
    )
    m = mask_rows(x)
    gc_ref[HALO : HALO + BLOCK] = gain * (gp_ref[0] - by_one * m - by_norm * nm_ref[0])
    pieces = []
    for chunk in range(BLOCK // CHUNK):
        at = slice(chunk * CHUNK, (chunk + 1) * CHUNK)
        before, after, centre = prev_ref[at], next_ref[at], xf_ref[at]
        total = jnp.zeros((CHUNK, LANES), F32)
        for k in range(KERNEL):
            near = near_rows(gc_ref, HALO + chunk * CHUNK, HALF - k, before, after)
            total = total + par_ref[k : k + 1] * near
            tap_ref[k] += jnp.sum((centre * near).reshape(-1, 8, LANES), axis=0)
        pieces.append(total)
    for core in range(CORES):
        half = jnp.concatenate(
            pieces[core * (ROWS // CHUNK) : (core + 1) * (ROWS // CHUNK)], axis=0
        )
        half = half * m[core * ROWS : (core + 1) * ROWS]
        turned = pltpu.roll(half, CHAN, 1)
        lane = lax.broadcasted_iota(jnp.int32, (ROWS, LANES), 1)
        pack_ref[core, 0:ROWS] = jnp.where(
            lane < CHAN, act_ref[core].astype(F32), turned
        ).astype(BF16)
        lane = lane[: ROWS // 2]
        pack_ref[core, ROWS : ROWS + ROWS // 2] = jnp.where(
            lane < LANES // 2, turned[: ROWS // 2], pltpu.roll(turned[ROWS // 2 :], LANES // 2, 1)
        ).astype(BF16)

    @pl.when(b == Z - 1)
    def _():
        taps_ref[...] = jnp.sum(tap_ref[...], axis=1)


def join_body(pack_ref, w_hbm, out_ref, gh_ref, four_ref, total_ref, w_ref, sem):
    step = pl.program_id(0)
    width = 4 * CHAN

    def fetch(i):
        rows = pl.ds(pl.multiple_of(i * width, width), width)
        return pltpu.make_async_copy(w_hbm.at[rows], w_ref.at[i], sem.at[i])

    @pl.when(step == 0)
    def _():
        for i in range(Z // 2):
            fetch(i).start()

    fetch(step).wait()
    lane = lax.broadcasted_iota(jnp.int32, (ROWS // 2, LANES), 1)

    @pl.when(step == 0)
    def _():
        total_ref[...] = jnp.zeros_like(total_ref)

    total = total_ref[...]
    for i in range(4):
        main = pack_ref[i, 0:ROWS]
        total = total + jnp.dot(
            main[:, :CHAN], w_ref[step, i * CHAN : (i + 1) * CHAN], preferred_element_type=F32
        )
        main = main.astype(F32)
        rest = pack_ref[i, ROWS : ROWS + ROWS // 2].astype(F32)
        upper = jnp.where(lane < LANES // 2, rest, main[: ROWS // 2])
        lower = jnp.where(lane < LANES // 2, pltpu.roll(rest, LANES // 2, 1), main[ROWS // 2 :])
        turned = jnp.concatenate([upper, lower], axis=0)
        four_ref[:, i * LANES : (i + 1) * LANES] = pltpu.roll(turned, LANES - CHAN, 1).astype(BF16)
    total_ref[...] = total
    gh_ref[...] = lax.dot_general(
        four_ref[...], one_hot(), (((1,), (1,)), ((), ())), preferred_element_type=F32
    ).astype(BF16)

    @pl.when(step == Z // 2 - 1)
    def _():
        out_ref[...] = total.astype(BF16)


def shape(dims, kind):
    return jax.ShapeDtypeStruct(dims, kind)


def local(hidden_in, segment_ids, frame_mask, dw_kernel, norm_scale, norm_shift, out_weight, cotangent):
    core = lax.axis_index("core")
    here = lax.axis_index(ALL)
    this_set = lax.axis_index(OVER_SETS)

    with jax.named_scope("cotangent_of_group"):
        cot_all = lax.all_gather(cotangent, IN_GROUP)

    with jax.named_scope("prepare"):
        seg = lax.dynamic_slice_in_dim(
            jnp.pad(segment_ids, (HALO, LANES - HALO), constant_values=-1), here * ROWS, 2 * LANES
        )
        row = lambda v: v.reshape(1, -1)
        wp, ext, own, edge = call(
            prep_body,
            (
                shape((SETS, OWN, WIDE), BF16),
                shape((ROWS, LANES), F32),
                shape((ROWS, D), BF16),
                shape((HALO, D), BF16),
            ),
            (core.reshape(1), row(seg), dw_kernel.T, row(norm_scale), row(norm_shift), row(frame_mask), out_weight, hidden_in),
            [
                pltpu.VMEM((LANES, LANES), F32),
                pltpu.VMEM((OWN, KERNEL), F32),
                pltpu.VMEM((1, OWN), F32),
                pltpu.VMEM((1, OWN), F32),
                pltpu.VMEM((1, ROWS), jnp.int32),
                pltpu.VMEM((OWN, D), BF16),
                pltpu.SemaphoreType.DMA((6,)),
            ],
            "prepare",
            in_specs=[smem(), vmem()] + [hbm()] * 6,
            out_specs=[vmem()] * 4,
        )

    with jax.named_scope("edge_frames"):
        last = Z * SETS * CORES - 1
        pairs = [(i, i + 1) for i in range(1, last, 2)] + [(i + 1, i) for i in range(1, last, 2)]
        halo = lax.ppermute(edge, ALL, pairs)

    with jax.named_scope("rows_and_params"):
        wp = lax.all_to_all(wp, OVER_SETS, 0, 0)

    with jax.named_scope("frames_to_channels"):
        frames = call(
            split_body,
            shape((GROUP, SENT, LANES), BF16),
            (core.reshape(1), own, halo, ext),
            [pltpu.VMEM((SENT, D), BF16), pltpu.VMEM((SENT, LANES), F32)],
            "split",
            in_specs=[smem(), vmem(), vmem(), vmem()],
            out_specs=vmem(),
        )
        frames, wp = lax.optimization_barrier((frames, wp))
        x = lax.all_to_all(frames, IN_GROUP, 0, 0).reshape(Z, SPAN, LANES)

    whole = lambda *dims: pl.BlockSpec(dims, lambda i: (0,) * len(dims))
    each = lambda *dims: pl.BlockSpec(dims, lambda i: (i,) + (0,) * (len(dims) - 1))

    with jax.named_scope("conv"):
        conv, stat, par, rows, wide = call(
            conv_body,
            (
                shape((Z, BLOCK, LANES), F32),
                shape((SETS, 8, LANES), F32),
                shape((PART, LANES), F32),
                shape((CHAN, D), BF16),
                shape((LANES, D), BF16),
            ),
            (x, wp),
            [
                pltpu.VMEM((SPAN, LANES), F32),
                pltpu.VMEM((BLOCK, LANES), F32),
                pltpu.VMEM((BLOCK, LANES), F32),
                pltpu.VMEM((LANES, LANES), F32),
                pltpu.VMEM((LANES, WIDE), F32),
                pltpu.VMEM((8, LANES), F32),
            ],
            "conv",
            work=6 * 10**9,
            grid=(Z,),
            in_specs=[each(1, SPAN, LANES), whole(SETS, OWN, WIDE)],
            out_specs=[
                each(1, BLOCK, LANES),
                whole(SETS, 8, LANES),
                whole(PART, LANES),
                whole(CHAN, D),
                whole(LANES, D),
            ],
        )

    with jax.named_scope("weights_of_group"):
        w_all = lax.all_gather(rows, IN_GROUP, tiled=True)

    with jax.named_scope("norm_sums"):
        stat = lax.all_to_all(stat, OVER_SETS, 0, 0)

    with jax.named_scope("activation_grad"):
        act, gp, nm, first, last_rows, gw = call(
            grad_body,
            (
                shape((GROUP, ROWS, LANES), BF16),
                shape((Z, BLOCK, LANES), F32),
                shape((Z, BLOCK, LANES), F32),
                shape((Z, 2, HALO, LANES), BF16),
                shape((Z, 2, HALO, LANES), BF16),
                shape((SETS, OWN, WIDE), BF16),
            ),
            (conv, x, wide, par, stat, cot_all),
            [
                pltpu.VMEM((LANES, D), F32),
                pltpu.VMEM((2, 8, LANES), F32),
                pltpu.VMEM((8, LANES), F32),
                pltpu.VMEM((GROUP, ROWS, D), BF16),
                pltpu.SemaphoreType.DMA((Z,)),
            ],
            "activation",
            grid=(Z,),
            in_specs=[
                pl.BlockSpec((1, BLOCK, LANES), lambda i: (i, 0, 0)),
                pl.BlockSpec((1, SPAN, LANES), lambda i: (i, 0, 0)),
                whole(LANES, D),
                whole(PART, LANES),
                whole(SETS, 8, LANES),
                hbm(),
            ],
            out_specs=[
                pl.BlockSpec((CORES, ROWS, LANES), lambda i: (i, 0, 0)),
                pl.BlockSpec((1, BLOCK, LANES), lambda i: (i, 0, 0)),
                pl.BlockSpec((1, BLOCK, LANES), lambda i: (i, 0, 0)),
                pl.BlockSpec((1, 2, HALO, LANES), lambda i: (i, 0, 0, 0)),
                pl.BlockSpec((1, 2, HALO, LANES), lambda i: (i, 0, 0, 0)),
                whole(SETS, OWN, WIDE),
            ],
        )

    with jax.named_scope("edge_grads"):
        up = [(i, (i + 1) % SETS) for i in range(SETS)]
        down = [((i + 1) % SETS, i) for i in range(SETS)]
        left = lax.ppermute(last_rows, OVER_SETS, up)
        right = lax.ppermute(first, OVER_SETS, down)

    with jax.named_scope("norm_grad_sums"):
        gw = lax.all_to_all(gw, OVER_SETS, 0, 0)

    with jax.named_scope("conv_grad"):
        pack, taps, both = call(
            back_body,
            (
                shape((GROUP, ROWS + ROWS // 2, LANES), BF16),
                shape((32, LANES), F32),
                shape((8, LANES), F32),
            ),
            (this_set.reshape(1), gp, nm, x, act, par, stat, gw, left, right),
            [
                pltpu.VMEM((SPAN, LANES), F32),
                pltpu.VMEM((BLOCK, LANES), F32),
                pltpu.VMEM((BLOCK, LANES), F32),
                pltpu.VMEM((BLOCK, LANES), F32),
                pltpu.VMEM((32, 8, LANES), F32),
                pltpu.VMEM((8, LANES), F32),
            ],
            "conv_grad",
            work=10**10,
            grid=(Z,),
            in_specs=[
                smem(),
                each(1, BLOCK, LANES),
                each(1, BLOCK, LANES),
                each(1, SPAN, LANES),
                each(CORES, ROWS, LANES),
                whole(PART, LANES),
                whole(SETS, 8, LANES),
                whole(SETS, OWN, WIDE),
                whole(Z, 2, HALO, LANES),
                whole(Z, 2, HALO, LANES),
            ],
            out_specs=[each(CORES, ROWS + ROWS // 2, LANES), whole(32, LANES), whole(8, LANES)],
        )

    with jax.named_scope("channels_to_frames"):
        back = lax.all_to_all(pack, IN_GROUP, 0, 0)

    with jax.named_scope("sums_of_taps"):
        for axis, size in (("x", X), ("y", Y)):
            moved = [
                lax.ppermute(taps, axis, [(i, (i + by) % size) for i in range(size)])
                for by in range(1, size)
            ]
            taps = taps + sum(moved)
        at = this_set * OWN
        grad_kernel = lax.dynamic_slice(taps, (0, at), (KERNEL, OWN))
        grad_scale = lax.dynamic_slice(both, (0, at), (1, OWN))[0]
        grad_shift = lax.dynamic_slice(both, (1, at), (1, OWN))[0]

    with jax.named_scope("weight_grad_sums"):
        grad_weight = jnp.sum(gw[:, :, :D].astype(F32), axis=0)

    with jax.named_scope("join"):
        width = 2 * D // Z
        module_out, grad_hidden = call(
            join_body,
            (shape((ROWS, D), BF16), shape((ROWS, D), BF16)),
            (back, w_all),
            [
                pltpu.VMEM((ROWS, 4 * LANES), BF16),
                pltpu.VMEM((ROWS, D), F32),
                pltpu.VMEM((Z // 2, width, D), BF16),
                pltpu.SemaphoreType.DMA((Z // 2,)),
            ],
            "join",
            grid=(Z // 2,),
            in_specs=[
                pl.BlockSpec((4, ROWS + ROWS // 2, LANES), lambda i: (i, 0, 0)),
                hbm(),
            ],
            out_specs=[
                pl.BlockSpec((ROWS, D), lambda i: (0, 0)),
                pl.BlockSpec((ROWS, width), lambda i: (0, i)),
            ],
        )
    return (module_out, grad_hidden, grad_kernel, grad_scale, grad_shift, grad_weight)


def solution(mesh):
    grid = Mesh(mesh.devices.reshape(Z, X, Y, CORES), ALL)
    return jax.shard_map(
        local,
        mesh=grid,
        in_specs=(P(ALL, None), P(), P(ALL), P(None, ALL), P(ALL), P(ALL), P(ALL, None), P(ALL, None)),
        out_specs=(P(ALL, None), P(ALL, None), P(None, ALL), P(ALL), P(ALL), P(ALL, None)),
        check_vma=False,
    )
```

time: 185 us -> 168 us (0.908)
  local copies, waits for them, and re-layouts: 14.7 us -> 3.39 us
  waiting for transfers between devices: 36.1 us -> 24.9 us
  Pallas kernels: 30.8 us -> 41.6 us
  blocking collectives: 56 us -> 48.8 us
  starting transfers between devices: 27.2 us -> 31.3 us
  other arithmetic: 5.62 us -> 2.5 us
    all_to_all x2, waiting for transfers between devices: 14.5 us -> 0.01 us  [the longest x1 0.01 us: local(): wp = lax.all_to_all(wp, OVER_SETS, 0, 0)]
    all_to_all x1 -> x0, blocking collectives: 12 us -> none  [local(): gathered = lax.all_to_all(gwp, OVER_SETS, 0, 0)]
    all_to_all x1, waiting for transfers between devices: 20.8 us -> 9.31 us  [local(): back = lax.all_to_all(pack, IN_GROUP, 0, 0)]
    pallas_call x5 -> x6, Pallas kernels: 30.8 us -> 41.6 us  [call(): pl.pallas_call(body, out_shape=outs, scratch_shapes=scratch, name=name, c...]
    unnamed x20 -> x1, local copies, waits for them, and re-layouts: 11.1 us -> 0.69 us
    ppermute x1, waiting for transfers between devices: 0.01 us -> 5.5 us  [local(): left = lax.ppermute(last_rows, OVER_SETS, up)]
    ppermute x0 -> x6, waiting for transfers between devices: none -> 4.96 us  [local(): lax.ppermute(taps, axis, [(i, (i + by) % size) for i in range(size)])]
    ppermute x1, waiting for transfers between devices: 0.01 us -> 4.39 us  [local(): halo = lax.ppermute(edge, ALL, pairs)]
  transfers between devices with their start and end apart: 8 -> 14, of which waited for: 3 -> 7; matrix products, arithmetic and copies ran while one was open for 5% -> 4% of each run, Pallas kernels for 15% -> 21%
where the time goes in v2:
time: 168 us; the launch traced here: 167 us
  blocking collectives  48.8 us (29%)
  Pallas kernels  41.6 us (25%)
  starting transfers between devices  31.3 us (19%)
  waiting for transfers between devices  24.9 us (15%)
  between operations  14.1 us (8%)
  local copies, waits for them, and re-layouts  3.39 us (2%)
  other arithmetic  2.5 us (1%)
    pallas_call x6, Pallas kernels, call(): pl.pallas_call(body, out_shape=outs, scratch_shapes=scratch, name=name, c...  41.6 us
    all_to_all x1, blocking collectives, local(): x = lax.all_to_all(frames, IN_GROUP, 0, 0).reshape(Z, SPAN, LANES)  38.2 us
    all_to_all x1, blocking collectives, local(): stat = lax.all_to_all(stat, OVER_SETS, 0, 0)  10.6 us
    all_to_all x1, waiting for transfers between devices, local(): back = lax.all_to_all(pack, IN_GROUP, 0, 0)  9.31 us
    all_to_all x1, starting transfers between devices, local(): wp = lax.all_to_all(wp, OVER_SETS, 0, 0)  7.64 us
    all_to_all x1, starting transfers between devices, local(): back = lax.all_to_all(pack, IN_GROUP, 0, 0)  6.19 us
    ppermute x1, waiting for transfers between devices, local(): left = lax.ppermute(last_rows, OVER_SETS, up)  5.5 us
    ppermute x6, waiting for transfers between devices, local(): lax.ppermute(taps, axis, [(i, (i + by) % size) for i in range(size)])  4.96 us
  transfers between devices with their start and end apart: 14, of which 7 were waited for; matrix products, arithmetic and copies ran while one was open for 4% of the time, Pallas kernels for 21%

profile of v2, /device:TPU:1, one launch (start us, length us, event | category | flops | bytes accessed | tf_op | source)
XLA Modules:
  0.0 166.7 jit_solution(13271538327829514625)
XLA Ops:
  7.2 0.7 all-gather.6.cloned.1.call-update
  7.9 1.4 pad_dynamic-slice_fusion
  9.3 3.1 %prepare.1 = (bf16[16,6,1664]{2,1,0:T(8,128)(2,1)}, f32[128,128]{1,0:T(8,128)}, bf16[128,1536]{1,0:T(8,128)(2,1)}, bf16[16,1536]{1,0:T(8,128)(2,1)}) custom-call(s32[1]{0:T(128)} %bitcast.1.core_ref, s32[1,256]{1,0:T(1,128)} %bitcast.18, f32[6,31]{1,0:T(8,128)} %bitcast.17, f32[1,6]{1,0:T(1,128)} %bitcast.19, f32[1,6]{1,0:T(1,128)} %bitcast.20, ...), custom_call_target="tpu_custom_call" | custom-call | tf_op jit(solution)/shard_map/prepare/prepare/pallas_call | solution.py:35
  12.3 7.6 %all-to-all-start = ((bf16[16,6,1664]{2,1,0:T(8,128)(2,1)}), bf16[16,6,1664]{2,1,0:T(8,128)(2,1)}, u32[]{:S(2)}, u32[]{:S(2)}) async-start(bf16[16,6,1664]{2,1,0:T(8,128)(2,1)} %get-tuple-element.31), calls=%async_computation | async-start | bytes 851968 | tf_op jit(solution)/shard_map/rows_and_params/all_to_all | solution.py:449
  20.0 4.3 %collective-permute-start = (bf16[16,1536]{1,0:T(8,128)(2,1)}, bf16[16,1536]{1,0:T(8,128)(2,1)}, u32[]{:S(2)}, u32[]{:S(2)}) collective-permute-start(bf16[16,1536]{1,0:T(8,128)(2,1)} %get-tuple-element.29), channel_id=1, source_target_pairs={{1,2},{3,4},{5,6},{7,8},{9,10},{11,12},{13,14},{15,16},{17,18},{19... | collective-permute-start | bytes 147464 | tf_op jit(solution)/shard_map/edge_frames/ppermute | solution.py:446
  24.4 4.4 %collective-permute-done.halo_ref = bf16[16,1536]{1,0:T(8,128)(2,1)} collective-permute-done((bf16[16,1536]{1,0:T(8,128)(2,1)}, bf16[16,1536]{1,0:T(8,128)(2,1)}, u32[]{:S(2)}, u32[]{:S(2)}) %collective-permute-start) | collective-permute-done | bytes 49184 | tf_op jit(solution)/shard_map/edge_frames/ppermute | solution.py:446
  28.8 2.4 %split.1 = bf16[16,144,128]{2,1,0:T(8,128)(2,1)} custom-call(s32[1]{0:T(128)} %bitcast.1.core_ref, bf16[128,1536]{1,0:T(8,128)(2,1)} %get-tuple-element.28.own_ref, bf16[16,1536]{1,0:T(8,128)(2,1)} %collective-permute-done.halo_ref, f32[128,128]{1,0:T(8,128)} %get-tuple-element.30.ext_ref), custom_call_target="tpu_custom_call" | custom-call | tf_op jit(solution)/shard_map/frames_to_channels/split/pallas_call | solution.py:35
  31.2 38.2 %all_to_all.25 = bf16[16,144,128]{2,1,0:T(8,128)(2,1)} all-to-all(bf16[16,144,128]{2,1,0:T(8,128)(2,1)} %split.1), channel_id=1, replica_groups=mesh['z'=8,'x'=4,'y'=4,'core'=2] {'z','core'}, dimensions={0} | all-to-all | bytes 1179648 | tf_op jit(solution)/shard_map/frames_to_channels/all_to_all | solution.py:462
  69.4 8.5 %conv.1 = (f32[8,256,128]{2,1,0:T(8,128)}, f32[16,8,128]{2,1,0:T(8,128)}, f32[40,128]{1,0:T(8,128)}, bf16[96,1536]{1,0:T(8,128)(2,1)}, bf16[128,1536]{1,0:T(8,128)(2,1)}) custom-call(bf16[8,288,128]{2,1,0:T(8,128)(2,1)} %bitcast.14, bf16[16,6,1664]{2,1,0:T(8,128)(2,1)} %all-to-all-done.wp_ref), custom_call_target="tpu_custom_call" | custom-call | flops 6000000000 | bytes 1048576 | tf_op jit(solution)/shard_map/conv/conv/pallas_call | solution.py:35
  77.9 10.6 %all_to_all.26.stat_ref = f32[16,8,128]{2,1,0:T(8,128)} all-to-all(f32[16,8,128]{2,1,0:T(8,128)} %get-tuple-element.37), channel_id=1, replica_groups=mesh['z'=8,'x'=4,'y'=4,'core'=2] {'x','y'}, dimensions={0} | all-to-all | bytes 131072 | tf_op jit(solution)/shard_map/norm_sums/all_to_all | solution.py:503
  88.5 10.1 %activation.1 = (bf16[16,128,128]{2,1,0:T(8,128)(2,1)}, f32[8,256,128]{2,1,0:T(8,128)}, f32[8,256,128]{2,1,0:T(8,128)}, bf16[8,2,16,128]{3,2,1,0:T(8,128)(2,1)},...) custom-call(f32[8,256,128]{2,1,0:T(8,128)} %get-tuple-element.34.conv_ref, bf16[8,288,128]{2,1,0:T(8,128)(2,1)} %bitcast.15, ...), custom_call_target="tpu_custom_call" | custom-call | tf_op jit(solution)/shard_map/activation_grad/activation/pallas_call | solution.py:35
  98.6 4.2 %all-to-all-start.3 = ((bf16[16,6,1664]{2,1,0:T(8,128)(2,1)}), bf16[16,6,1664]{2,1,0:T(8,128)(2,1)}, u32[]{:S(2)}, u32[]{:S(2)}) async-start(bf16[16,6,1664]{2,1,0:T(8,128)(2,1)} %get-tuple-element.41), calls=%async_computation.3 | async-start | bytes 851968 | tf_op jit(solution)/shard_map/norm_grad_sums/all_to_all | solution.py:551
  102.8 1.2 collective-permute-start.1
  104.0 3.7 %collective-permute-start.2 = (bf16[8,2,16,128]{3,2,1,0:T(8,128)(2,1)}, bf16[8,2,16,128]{3,2,1,0:T(8,128)(2,1)}, u32[]{:S(2)}, u32[]{:S(2)}) collective-permute-start(bf16[8,2,16,128]{3,2,1,0:T(8,128)(2,1)} %get-tuple-element.43), channel_id=1, source_target_pairs={{2,0},{4,2},{6,4},{8,6},{10,8},{12,10},{14,12},{16,14},{18,16},{20... | collective-permute-start | bytes 196616 | tf_op jit(solution)/shard_map/edge_grads/ppermute | solution.py:548
  107.7 5.5 %collective-permute-done.1.left_ref = bf16[8,2,16,128]{3,2,1,0:T(8,128)(2,1)} collective-permute-done((bf16[8,2,16,128]{3,2,1,0:T(8,128)(2,1)}, bf16[8,2,16,128]{3,2,1,0:T(8,128)(2,1)}, u32[]{:S(2)}, u32[]{:S(2)}) %collective-permute-start.1) | collective-permute-done | bytes 65568 | tf_op jit(solution)/shard_map/edge_grads/ppermute | solution.py:547
  113.2 11.4 %conv_grad.1 = (bf16[16,192,128]{2,1,0:T(8,128)(2,1)}, f32[32,128]{1,0:T(8,128)}, f32[8,128]{1,0:T(8,128)}) custom-call(s32[1]{0:T(128)} %bitcast.set_ref, f32[8,256,128]{2,1,0:T(8,128)} %get-tuple-element.38.gp_ref, f32[8,256,128]{2,1,0:T(8,128)} %get-tuple-element.39.nm_ref, bf16[8,288,128]{2,1,0:T(8,128)(2,1)} %bitcast.16, ...), custom_call_target="tpu_custom_call" | custom-call | flops 10000000000 | bytes 1048576 | tf_op jit(solution)/shard_map/conv_grad/conv_grad/pallas_call | solution.py:35
  124.6 6.2 %all-to-all-start.4 = ((bf16[16,192,128]{2,1,0:T(8,128)(2,1)}), bf16[16,192,128]{2,1,0:T(8,128)(2,1)}, u32[]{:S(2)}, u32[]{:S(2)}) async-start(bf16[16,192,128]{2,1,0:T(8,128)(2,1)} %get-tuple-element.44), calls=%async_computation.4 | async-start | bytes 1572864 | tf_op jit(solution)/shard_map/channels_to_frames/all_to_all | solution.py:589
  130.8 0.6 collective-permute-start.5
  131.4 0.9 collective-permute-start.3
  132.3 0.9 collective-permute-start.4
  133.2 1.7 %convert_reduce_fusion = f32[6,1536]{1,0:T(8,128)} fusion(bf16[16,6,1664]{2,1,0:T(8,128)(2,1)} %all-to-all-done.3.sum_ref), kind=kLoop, calls=%fused_computation | loop fusion | flops 285696 | bytes 331776 | tf_op jit(solution)/shard_map/weight_grad_sums/reduce_sum | solution.py:604
  134.9 0.5 collective-permute-done.3
  135.4 1.6 collective-permute-done.4
  137.0 0.7 add_add_fusion
  137.7 1.0 collective-permute-start.8
  138.7 0.7 collective-permute-start.7
  139.3 1.3 dynamic-slice_bitcast_fusion
  140.7 2.5 %collective-permute-done.7 = f32[32,128]{1,0:T(8,128)S(1)} collective-permute-done((f32[32,128]{1,0:T(8,128)S(1)}, f32[32,128]{1,0:T(8,128)S(1)}, u32[]{:S(2)}, u32[]{:S(2)}) %collective-permute-start.7) | collective-permute-done | bytes 16416 | tf_op jit(solution)/shard_map/sums_of_taps/ppermute | solution.py:594
  143.2 0.4 collective-permute-done.6
  143.6 0.7 copy.14
  144.3 9.3 %all-to-all-done.4.pack_ref = bf16[16,192,128]{2,1,0:T(8,128)(2,1)} async-done(((bf16[16,192,128]{2,1,0:T(8,128)(2,1)}), bf16[16,192,128]{2,1,0:T(8,128)(2,1)}, u32[]{:S(2)}, u32[]{:S(2)}) %all-to-all-start.4) | async-done | bytes 786464 | tf_op jit(solution)/shard_map/channels_to_frames/all_to_all | solution.py:589
  153.6 6.2 %join.1 = (bf16[128,1536]{1,0:T(8,128)(2,1)}, bf16[128,1536]{1,0:T(8,128)(2,1)}) custom-call(bf16[16,192,128]{2,1,0:T(8,128)(2,1)} %all-to-all-done.4.pack_ref, bf16[1536,1536]{1,0:T(8,128)(2,1)} %all-gather.4.cloned.1.call-done.w_hbm), custom_call_target="tpu_custom_call" | custom-call | tf_op jit(solution)/shard_map/join/join/pallas_call | solution.py:35
  (12 shorter events, 0.2 us)
Async XLA Ops:
  7.2 81.4 %all-gather.6.cloned.1.call-start = ((), (), s32[]{:S(2)}) async-start(), calls=%async_computation.6 | async-start | bytes 6684672 | tf_op jit(solution)/shard_map/cotangent_of_group/all_gather | solution.py:413
  12.3 18.9 %all-to-all-start = ((bf16[16,6,1664]{2,1,0:T(8,128)(2,1)}), bf16[16,6,1664]{2,1,0:T(8,128)(2,1)}, u32[]{:S(2)}, u32[]{:S(2)}) async-start(bf16[16,6,1664]{2,1,0:T(8,128)(2,1)} %get-tuple-element.31), calls=%async_computation | async-start | bytes 851968 | tf_op jit(solution)/shard_map/rows_and_params/all_to_all | solution.py:449
  20.0 124.3 %all-gather.4.cloned.1.call-start = ((), (), s32[]{:S(2)}) async-start(), calls=%async_computation.5 | async-start | bytes 5013504 | tf_op jit(solution)/shard_map/weights_of_group/all_gather | solution.py:500
  20.0 8.7 %collective-permute-start = (bf16[16,1536]{1,0:T(8,128)(2,1)}, bf16[16,1536]{1,0:T(8,128)(2,1)}, u32[]{:S(2)}, u32[]{:S(2)}) collective-permute-start(bf16[16,1536]{1,0:T(8,128)(2,1)} %get-tuple-element.29), channel_id=1, source_target_pairs={{1,2},{3,4},{5,6},{7,8},{9,10},{11,12},{13,14},{15,16},{17,18},{19... | collective-permute-start | bytes 147464 | tf_op jit(solution)/shard_map/edge_frames/ppermute | solution.py:446
  98.6 14.6 %all-to-all-start.3 = ((bf16[16,6,1664]{2,1,0:T(8,128)(2,1)}), bf16[16,6,1664]{2,1,0:T(8,128)(2,1)}, u32[]{:S(2)}, u32[]{:S(2)}) async-start(bf16[16,6,1664]{2,1,0:T(8,128)(2,1)} %get-tuple-element.41), calls=%async_computation.3 | async-start | bytes 851968 | tf_op jit(solution)/shard_map/norm_grad_sums/all_to_all | solution.py:551
  102.8 10.4 %collective-permute-start.1 = (bf16[8,2,16,128]{3,2,1,0:T(8,128)(2,1)}, bf16[8,2,16,128]{3,2,1,0:T(8,128)(2,1)}, u32[]{:S(2)}, u32[]{:S(2)}) collective-permute-start(bf16[8,2,16,128]{3,2,1,0:T(8,128)(2,1)} %get-tuple-element.42), channel_id=1, source_target_pairs={{0,2},{2,4},{4,6},{6,8},{8,10},{10,12},{12,14},{14,16},{16,18},{18... | collective-permute-start | bytes 196616 | tf_op jit(solution)/shard_map/edge_grads/ppermute | solution.py:547
  104.0 9.2 %collective-permute-start.2 = (bf16[8,2,16,128]{3,2,1,0:T(8,128)(2,1)}, bf16[8,2,16,128]{3,2,1,0:T(8,128)(2,1)}, u32[]{:S(2)}, u32[]{:S(2)}) collective-permute-start(bf16[8,2,16,128]{3,2,1,0:T(8,128)(2,1)} %get-tuple-element.43), channel_id=1, source_target_pairs={{2,0},{4,2},{6,4},{8,6},{10,8},{12,10},{14,12},{16,14},{18,16},{20... | collective-permute-start | bytes 196616 | tf_op jit(solution)/shard_map/edge_grads/ppermute | solution.py:548
  124.6 29.0 %all-to-all-start.4 = ((bf16[16,192,128]{2,1,0:T(8,128)(2,1)}), bf16[16,192,128]{2,1,0:T(8,128)(2,1)}, u32[]{:S(2)}, u32[]{:S(2)}) async-start(bf16[16,192,128]{2,1,0:T(8,128)(2,1)} %get-tuple-element.44), calls=%async_computation.4 | async-start | bytes 1572864 | tf_op jit(solution)/shard_map/channels_to_frames/all_to_all | solution.py:589
  130.8 4.1 %collective-permute-start.5 = (f32[32,128]{1,0:T(8,128)}, f32[32,128]{1,0:T(8,128)S(1)}, u32[]{:S(2)}, u32[]{:S(2)}) collective-permute-start(f32[32,128]{1,0:T(8,128)} %get-tuple-element.48), channel_id=1, source_target_pairs={{0,24},{8,0},{16,8},{24,16},{1,25},{9,1},{17,9},{25,17},{2,26},{10... | collective-permute-start | bytes 49160 | tf_op jit(solution)/shard_map/sums_of_taps/ppermute | solution.py:594
  131.4 4.0 %collective-permute-start.3 = (f32[32,128]{1,0:T(8,128)}, f32[32,128]{1,0:T(8,128)S(1)}, u32[]{:S(2)}, u32[]{:S(2)}) collective-permute-start(f32[32,128]{1,0:T(8,128)} %get-tuple-element.48), channel_id=1, source_target_pairs={{0,8},{8,16},{16,24},{24,0},{1,9},{9,17},{17,25},{25,1},{2,10},{10... | collective-permute-start | bytes 49160 | tf_op jit(solution)/shard_map/sums_of_taps/ppermute | solution.py:594
  132.3 4.7 %collective-permute-start.4 = (f32[32,128]{1,0:T(8,128)}, f32[32,128]{1,0:T(8,128)S(1)}, u32[]{:S(2)}, u32[]{:S(2)}) collective-permute-start(f32[32,128]{1,0:T(8,128)} %get-tuple-element.48), channel_id=1, source_target_pairs={{0,16},{8,24},{16,0},{24,8},{1,17},{9,25},{17,1},{25,9},{2,18},{10... | collective-permute-start | bytes 49160 | tf_op jit(solution)/shard_map/sums_of_taps/ppermute | solution.py:594
  137.7 3.0 %collective-permute-start.8 = (f32[32,128]{1,0:T(8,128)S(1)}, f32[32,128]{1,0:T(8,128)S(1)}, u32[]{:S(2)}, u32[]{:S(2)}) collective-permute-start(f32[32,128]{1,0:T(8,128)S(1)} %add_add_fusion), channel_id=1, source_target_pairs={{0,6},{2,0},{4,2},{6,4},{1,7},{3,1},{5,3},{7,5},{8,14},{10,8},{12,... | collective-permute-start | bytes 49160 | tf_op jit(solution)/shard_map/sums_of_taps/ppermute | solution.py:594
  138.7 4.5 %collective-permute-start.7 = (f32[32,128]{1,0:T(8,128)S(1)}, f32[32,128]{1,0:T(8,128)S(1)}, u32[]{:S(2)}, u32[]{:S(2)}) collective-permute-start(f32[32,128]{1,0:T(8,128)S(1)} %add_add_fusion), channel_id=1, source_target_pairs={{0,4},{2,6},{4,0},{6,2},{1,5},{3,7},{5,1},{7,3},{8,12},{10,14},{12... | collective-permute-start | bytes 49160 | tf_op jit(solution)/shard_map/sums_of_taps/ppermute | solution.py:594
  139.3 4.2 %collective-permute-start.6 = (f32[32,128]{1,0:T(8,128)S(1)}, f32[32,128]{1,0:T(8,128)S(1)}, u32[]{:S(2)}, u32[]{:S(2)}) collective-permute-start(f32[32,128]{1,0:T(8,128)S(1)} %add_add_fusion), channel_id=1, source_target_pairs={{0,2},{2,4},{4,6},{6,0},{1,3},{3,5},{5,7},{7,1},{8,10},{10,12},{12... | collective-permute-start | bytes 49160 | tf_op jit(solution)/shard_map/sums_of_taps/ppermute | solution.py:594
Sparse Core Ops, SparseCore 0:
  9.8 62.9 all-gather.5
  78.0 38.6 all-gather.3

commit v3 on v2

--- a/solution.py
+++ b/solution.py
@@ -29,7 +29,7 @@
 F32, BF16 = jnp.float32, jnp.bfloat16
 
 
-def call(body, outs, ins, scratch, name, work=0, **more):
+def call(body, outs, ins, scratch, name, limit=64, work=0, **more):
     if work:
         more["cost_estimate"] = pl.CostEstimate(flops=work, bytes_accessed=2**20, transcendentals=0)
     return pl.pallas_call(
@@ -37,7 +37,7 @@
         out_shape=outs,
         scratch_shapes=scratch,
         name=name,
-        compiler_params=pltpu.CompilerParams(vmem_limit_bytes=64 * 2**20),
+        compiler_params=pltpu.CompilerParams(vmem_limit_bytes=limit * 2**20),
         **more,
     )(*ins)
 
@@ -226,7 +226,7 @@
 
 def grad_body(
     conv_ref, x_ref, wide_ref, par_ref, stat_ref, cot_hbm,
-    act_ref, gp_ref, nm_ref, first_ref, last_ref, gw_ref,
+    act_ref, gp_ref, first_ref, last_ref, gw_ref,
     total_ref, acc_ref, mom_ref, cot_ref, sem,
 ):
     step = pl.program_id(0)
@@ -266,7 +266,6 @@
     gp = m * grad_act * sig * (1.0 + pre * (1.0 - sig))
     nm = m * normed
     gp_ref[0] = gp
-    nm_ref[0] = nm
     lane = lax.broadcasted_iota(jnp.int32, (HALO, LANES), 1)
     for ref, at in ((first_ref, 0), (last_ref, BLOCK - HALO)):
         ref[0, 0] = gp[at : at + HALO].astype(BF16)
@@ -290,7 +289,7 @@
 
 
 def back_body(
-    set_ref, gp_ref, nm_ref, x_ref, act_ref, par_ref, stat_ref, sum_ref, left_ref, right_ref,
+    set_ref, gp_ref, conv_ref, x_ref, act_ref, par_ref, stat_ref, sum_ref, left_ref, right_ref,
     pack_ref, taps_ref, sums_ref,
     gc_ref, xf_ref, prev_ref, next_ref, tap_ref, run_ref,
 ):
@@ -308,6 +307,8 @@
         run_ref[0:1] = par_ref[KERNEL : KERNEL + 1] * inv_std
         run_ref[1:2] = scale_sum / count
         run_ref[2:3] = shift_sum / count
+        run_ref[3:4] = mean
+        run_ref[4:5] = inv_std
         tap_ref[...] = jnp.zeros_like(tap_ref)
 
     gain, by_norm, by_one = run_ref[0:1], run_ref[1:2], run_ref[2:3]
@@ -327,7 +328,8 @@
         right_ref, jnp.where(where_am_i == SETS - 1, jnp.minimum(b + 1, Z - 1), b)
     )
     m = mask_rows(x)
-    gc_ref[HALO : HALO + BLOCK] = gain * (gp_ref[0] - by_one * m - by_norm * nm_ref[0])
+    normed = (conv_ref[0] - run_ref[3:4]) * run_ref[4:5]
+    gc_ref[HALO : HALO + BLOCK] = gain * (gp_ref[0] - m * (by_one + by_norm * normed))
     pieces = []
     for chunk in range(BLOCK // CHUNK):
         at = slice(chunk * CHUNK, (chunk + 1) * CHUNK)
@@ -358,20 +360,8 @@
         taps_ref[...] = jnp.sum(tap_ref[...], axis=1)
 
 
-def join_body(pack_ref, w_hbm, out_ref, gh_ref, four_ref, total_ref, w_ref, sem):
+def join_body(pack_ref, w_ref, out_ref, gh_ref, four_ref, total_ref):
     step = pl.program_id(0)
-    width = 4 * CHAN
-
-    def fetch(i):
-        rows = pl.ds(pl.multiple_of(i * width, width), width)
-        return pltpu.make_async_copy(w_hbm.at[rows], w_ref.at[i], sem.at[i])
-
-    @pl.when(step == 0)
-    def _():
-        for i in range(Z // 2):
-            fetch(i).start()
-
-    fetch(step).wait()
     lane = lax.broadcasted_iota(jnp.int32, (ROWS // 2, LANES), 1)
 
     @pl.when(step == 0)
@@ -382,7 +372,7 @@
     for i in range(4):
         main = pack_ref[i, 0:ROWS]
         total = total + jnp.dot(
-            main[:, :CHAN], w_ref[step, i * CHAN : (i + 1) * CHAN], preferred_element_type=F32
+            main[:, :CHAN], w_ref[i * CHAN : (i + 1) * CHAN], preferred_element_type=F32
         )
         main = main.astype(F32)
         rest = pack_ref[i, ROWS : ROWS + ROWS // 2].astype(F32)
@@ -436,6 +426,7 @@
                 pltpu.SemaphoreType.DMA((6,)),
             ],
             "prepare",
+            limit=64,
             in_specs=[smem(), vmem()] + [hbm()] * 6,
             out_specs=[vmem()] * 4,
         )
@@ -455,6 +446,7 @@
             (core.reshape(1), own, halo, ext),
             [pltpu.VMEM((SENT, D), BF16), pltpu.VMEM((SENT, LANES), F32)],
             "split",
+            limit=64,
             in_specs=[smem(), vmem(), vmem(), vmem()],
             out_specs=vmem(),
         )
@@ -484,6 +476,7 @@
                 pltpu.VMEM((8, LANES), F32),
             ],
             "conv",
+            limit=24,
             work=6 * 10**9,
             grid=(Z,),
             in_specs=[each(1, SPAN, LANES), whole(SETS, OWN, WIDE)],
@@ -503,11 +496,10 @@
         stat = lax.all_to_all(stat, OVER_SETS, 0, 0)
 
     with jax.named_scope("activation_grad"):
-        act, gp, nm, first, last_rows, gw = call(
+        act, gp, first, last_rows, gw = call(
             grad_body,
             (
                 shape((GROUP, ROWS, LANES), BF16),
-                shape((Z, BLOCK, LANES), F32),
                 shape((Z, BLOCK, LANES), F32),
                 shape((Z, 2, HALO, LANES), BF16),
                 shape((Z, 2, HALO, LANES), BF16),
@@ -522,6 +514,7 @@
                 pltpu.SemaphoreType.DMA((Z,)),
             ],
             "activation",
+            limit=48,
             grid=(Z,),
             in_specs=[
                 pl.BlockSpec((1, BLOCK, LANES), lambda i: (i, 0, 0)),
@@ -534,7 +527,6 @@
             out_specs=[
                 pl.BlockSpec((CORES, ROWS, LANES), lambda i: (i, 0, 0)),
                 pl.BlockSpec((1, BLOCK, LANES), lambda i: (i, 0, 0)),
-                pl.BlockSpec((1, BLOCK, LANES), lambda i: (i, 0, 0)),
                 pl.BlockSpec((1, 2, HALO, LANES), lambda i: (i, 0, 0, 0)),
                 pl.BlockSpec((1, 2, HALO, LANES), lambda i: (i, 0, 0, 0)),
                 whole(SETS, OWN, WIDE),
@@ -558,7 +550,7 @@
                 shape((32, LANES), F32),
                 shape((8, LANES), F32),
             ),
-            (this_set.reshape(1), gp, nm, x, act, par, stat, gw, left, right),
+            (this_set.reshape(1), gp, conv, x, act, par, stat, gw, left, right),
             [
                 pltpu.VMEM((SPAN, LANES), F32),
                 pltpu.VMEM((BLOCK, LANES), F32),
@@ -568,6 +560,7 @@
                 pltpu.VMEM((8, LANES), F32),
             ],
             "conv_grad",
+            limit=24,
             work=10**10,
             grid=(Z,),
             in_specs=[
@@ -589,6 +582,7 @@
         back = lax.all_to_all(pack, IN_GROUP, 0, 0)
 
     with jax.named_scope("sums_of_taps"):
+        taps, w_all = lax.optimization_barrier((taps, w_all))
         for axis, size in (("x", X), ("y", Y)):
             moved = [
                 lax.ppermute(taps, axis, [(i, (i + by) % size) for i in range(size)])
@@ -612,14 +606,13 @@
             [
                 pltpu.VMEM((ROWS, 4 * LANES), BF16),
                 pltpu.VMEM((ROWS, D), F32),
-                pltpu.VMEM((Z // 2, width, D), BF16),
-                pltpu.SemaphoreType.DMA((Z // 2,)),
             ],
             "join",
+            limit=24,
             grid=(Z // 2,),
             in_specs=[
                 pl.BlockSpec((4, ROWS + ROWS // 2, LANES), lambda i: (i, 0, 0)),
-                hbm(),
+                pl.BlockSpec((width, D), lambda i: (i, 0)),
             ],
             out_specs=[
                 pl.BlockSpec((ROWS, D), lambda i: (0, 0)),

time: 168 us -> 161 us (0.958)
  Pallas kernels: 41.6 us -> 33.1 us
  local copies, waits for them, and re-layouts: 3.39 us -> 6.81 us
  waiting for transfers between devices: 24.9 us -> 27 us
  other arithmetic: 2.5 us -> 0.79 us
    pallas_call x6, Pallas kernels: 41.6 us -> 33.1 us  [call(): pl.pallas_call(body, out_shape=outs, scratch_shapes=scratch, name=name, c...]
    unnamed x1 -> x7, local copies, waits for them, and re-layouts: 0.69 us -> 4.87 us
  transfers between devices with their start and end apart: 14 -> 14, of which waited for: 7 -> 8; matrix products, arithmetic and copies ran while one was open for 4% -> 2% of each run, Pallas kernels for 21% -> 18%
where the time goes in v3:
time: 161 us; the launch traced here: 160 us
  blocking collectives  48.4 us (30%)
  Pallas kernels  33.1 us (21%)
  starting transfers between devices  30.2 us (19%)
  waiting for transfers between devices  27 us (17%)
  between operations  14.1 us (9%)
  local copies, waits for them, and re-layouts  6.81 us (4%)
    all_to_all x1, blocking collectives, local(): x = lax.all_to_all(frames, IN_GROUP, 0, 0).reshape(Z, SPAN, LANES)  38.1 us
    pallas_call x6, Pallas kernels, call(): pl.pallas_call(body, out_shape=outs, scratch_shapes=scratch, name=name, c...  33.1 us
    all_to_all x1, blocking collectives, local(): stat = lax.all_to_all(stat, OVER_SETS, 0, 0)  10.3 us
    all_to_all x1, waiting for transfers between devices, local(): back = lax.all_to_all(pack, IN_GROUP, 0, 0)  10.2 us
    all_to_all x1, starting transfers between devices, local(): wp = lax.all_to_all(wp, OVER_SETS, 0, 0)  7.64 us
    ppermute x6, waiting for transfers between devices, local(): lax.ppermute(taps, axis, [(i, (i + by) % size) for i in range(size)])  6.29 us
    all_to_all x1, starting transfers between devices, local(): back = lax.all_to_all(pack, IN_GROUP, 0, 0)  5.56 us
    ppermute x1, waiting for transfers between devices, local(): left = lax.ppermute(last_rows, OVER_SETS, up)  5.45 us
  transfers between devices with their start and end apart: 14, of which 8 were waited for; matrix products, arithmetic and copies ran while one was open for 2% of the time, Pallas kernels for 18%

profile of v3, /device:TPU:1, one launch (start us, length us, event | category | flops | bytes accessed | tf_op | source)
XLA Modules:
  0.0 160.4 jit_solution(1764797497034871143)
XLA Ops:
  7.2 0.7 all-gather.6.cloned.1.call-update
  7.9 1.4 pad_dynamic-slice_fusion
  9.3 3.1 %prepare.1 = (bf16[16,6,1664]{2,1,0:T(8,128)(2,1)}, f32[128,128]{1,0:T(8,128)}, bf16[128,1536]{1,0:T(8,128)(2,1)}, bf16[16,1536]{1,0:T(8,128)(2,1)}) custom-call(s32[1]{0:T(128)} %bitcast.1.core_ref, s32[1,256]{1,0:T(1,128)} %bitcast.18, f32[6,31]{1,0:T(8,128)} %bitcast.17, f32[1,6]{1,0:T(1,128)} %bitcast.19, f32[1,6]{1,0:T(1,128)} %bitcast.20, ...), custom_call_target="tpu_custom_call" | custom-call | tf_op jit(solution)/shard_map/prepare/prepare/pallas_call | solution.py:35
  12.3 7.6 %all-to-all-start = ((bf16[16,6,1664]{2,1,0:T(8,128)(2,1)}), bf16[16,6,1664]{2,1,0:T(8,128)(2,1)}, u32[]{:S(2)}, u32[]{:S(2)}) async-start(bf16[16,6,1664]{2,1,0:T(8,128)(2,1)} %get-tuple-element.32), calls=%async_computation | async-start | bytes 851968 | tf_op jit(solution)/shard_map/rows_and_params/all_to_all | solution.py:440
  20.0 4.3 %collective-permute-start = (bf16[16,1536]{1,0:T(8,128)(2,1)}, bf16[16,1536]{1,0:T(8,128)(2,1)}, u32[]{:S(2)}, u32[]{:S(2)}) collective-permute-start(bf16[16,1536]{1,0:T(8,128)(2,1)} %get-tuple-element.30), channel_id=1, source_target_pairs={{1,2},{3,4},{5,6},{7,8},{9,10},{11,12},{13,14},{15,16},{17,18},{19... | collective-permute-start | bytes 147464 | tf_op jit(solution)/shard_map/edge_frames/ppermute | solution.py:437
  24.4 4.4 %collective-permute-done.halo_ref = bf16[16,1536]{1,0:T(8,128)(2,1)} collective-permute-done((bf16[16,1536]{1,0:T(8,128)(2,1)}, bf16[16,1536]{1,0:T(8,128)(2,1)}, u32[]{:S(2)}, u32[]{:S(2)}) %collective-permute-start) | collective-permute-done | bytes 49184 | tf_op jit(solution)/shard_map/edge_frames/ppermute | solution.py:437
  28.8 2.4 %split.1 = bf16[16,144,128]{2,1,0:T(8,128)(2,1)} custom-call(s32[1]{0:T(128)} %bitcast.1.core_ref, bf16[128,1536]{1,0:T(8,128)(2,1)} %get-tuple-element.29.own_ref, bf16[16,1536]{1,0:T(8,128)(2,1)} %collective-permute-done.halo_ref, f32[128,128]{1,0:T(8,128)} %get-tuple-element.31.ext_ref), custom_call_target="tpu_custom_call" | custom-call | tf_op jit(solution)/shard_map/frames_to_channels/split/pallas_call | solution.py:35
  31.2 38.1 %all_to_all.25 = bf16[16,144,128]{2,1,0:T(8,128)(2,1)S(1)} all-to-all(bf16[16,144,128]{2,1,0:T(8,128)(2,1)} %split.1), channel_id=1, replica_groups=mesh['z'=8,'x'=4,'y'=4,'core'=2] {'z','core'}, dimensions={0} | all-to-all | bytes 1179648 | tf_op jit(solution)/shard_map/frames_to_channels/all_to_all | solution.py:454
  69.3 7.4 %conv.1 = (f32[8,256,128]{2,1,0:T(8,128)S(1)}, f32[16,8,128]{2,1,0:T(8,128)S(1)}, f32[40,128]{1,0:T(8,128)S(1)}, bf16[96,1536]{1,0:T(8,128)(2,1)}, bf16[128,1536]{1,0:T(8,128)(2,1)S(1)}) custom-call(bf16[8,288,128]{2,1,0:T(8,128)(2,1)S(1)} %bitcast.13, bf16[16,6,1664]{2,1,0:T(8,128)(2,1)} %all-to-all-done.wp_ref), custom_call_target="tpu_custom_call" | custom-call | flops 6000000000 | bytes 1048576 | tf_op jit(solution)/shard_map/conv/conv/pallas_call | solution.py:35
  76.7 10.3 %all_to_all.26.stat_ref = f32[16,8,128]{2,1,0:T(8,128)S(1)} all-to-all(f32[16,8,128]{2,1,0:T(8,128)S(1)} %get-tuple-element.38), channel_id=1, replica_groups=mesh['z'=8,'x'=4,'y'=4,'core'=2] {'x','y'}, dimensions={0} | all-to-all | bytes 131072 | tf_op jit(solution)/shard_map/norm_sums/all_to_all | solution.py:496
  87.0 6.7 %activation.1 = (bf16[16,128,128]{2,1,0:T(8,128)(2,1)S(1)}, f32[8,256,128]{2,1,0:T(8,128)S(1)}, bf16[8,2,16,128]{3,2,1,0:T(8,128)(2,1)S(1)}, bf16[8,2,16,128]{3,2,1,0:T(8,128)(2,1)S(1)}, bf16[16,6,1664]{2,1,0:T(8,128)(2,1)}) custom-call(f32[8,256,128]{2,1,0:T(8,128)S(1)} %get-tuple-element.35.conv_ref, bf16[8,288,128]{2,1,0:T(8,128)(2,1)S(1)} %bitcast.14, ...), custom_call_target="tpu_custom_call" | custom-call | tf_op jit(solution)/shard_map/activation_grad/activation/pallas_call | solution.py:35
  93.7 0.8 copy-done.1
  94.5 3.6 %all-to-all-start.3 = ((bf16[16,6,1664]{2,1,0:T(8,128)(2,1)}), bf16[16,6,1664]{2,1,0:T(8,128)(2,1)S(1)}, u32[]{:S(2)}, u32[]{:S(2)}) async-start(bf16[16,6,1664]{2,1,0:T(8,128)(2,1)} %get-tuple-element.41), calls=%async_computation.3 | async-start | bytes 851968 | tf_op jit(solution)/shard_map/norm_grad_sums/all_to_all | solution.py:543
  98.0 1.2 collective-permute-start.1
  99.3 3.6 %collective-permute-start.2 = (bf16[8,2,16,128]{3,2,1,0:T(8,128)(2,1)S(1)}, bf16[8,2,16,128]{3,2,1,0:T(8,128)(2,1)S(1)}, u32[]{:S(2)}, u32[]{:S(2)}) collective-permute-start(bf16[8,2,16,128]{3,2,1,0:T(8,128)(2,1)S(1)} %get-tuple-element.43), channel_id=1, source_target_pairs={{2,0},{4,2},{6,4},{8,6},{10,8},{12,10},{14,12},{16,14},{18,16},{20... | collective-permute-start | bytes 196616 | tf_op jit(solution)/shard_map/edge_grads/ppermute | solution.py:540
  102.9 5.5 %collective-permute-done.1.left_ref = bf16[8,2,16,128]{3,2,1,0:T(8,128)(2,1)S(1)} collective-permute-done((bf16[8,2,16,128]{3,2,1,0:T(8,128)(2,1)S(1)}, bf16[8,2,16,128]{3,2,1,0:T(8,128)(2,1)S(1)}, u32[]{:S(2)}, u32[]{:S(2)}) %collective-permute-start.1) | collective-permute-done | bytes 65568 | tf_op jit(solution)/shard_map/edge_grads/ppermute | solution.py:539
  108.4 1.0 copy-done.2
  109.4 10.0 %conv_grad.1 = (bf16[16,192,128]{2,1,0:T(8,128)(2,1)}, f32[32,128]{1,0:T(8,128)S(1)}, f32[8,128]{1,0:T(8,128)S(1)}) custom-call(s32[1]{0:T(128)} %bitcast.set_ref, f32[8,256,128]{2,1,0:T(8,128)S(1)} %get-tuple-element.39.gp_ref, f32[8,256,128]{2,1,0:T(8,128)S(1)} %get-tuple-element.35.conv_ref, bf16[8,288,128]{2,1,0:T(8,128)(2,1)S(1)} %bitcast.15, ...), custom_call_target="tpu_custom_call" | custom-call | flops 10000000000 | bytes 1048576 | tf_op jit(solution)/shard_map/conv_grad/conv_grad/pallas_call | solution.py:35
  119.4 5.6 %all-to-all-start.4 = ((bf16[16,192,128]{2,1,0:T(8,128)(2,1)}), bf16[16,192,128]{2,1,0:T(8,128)(2,1)S(1)}, u32[]{:S(2)}, u32[]{:S(2)}) async-start(bf16[16,192,128]{2,1,0:T(8,128)(2,1)} %get-tuple-element.44), calls=%async_computation.4 | async-start | bytes 1572864 | tf_op jit(solution)/shard_map/channels_to_frames/all_to_all | solution.py:582
  125.0 0.7 collective-permute-start.5
  125.7 0.9 collective-permute-start.3
  126.6 0.9 collective-permute-start.4
  127.5 0.7 convert_reduce_fusion
  128.2 1.3 collective-permute-done.3
  129.5 1.5 collective-permute-done.4
  131.6 1.0 collective-permute-start.7
  133.8 2.2 %collective-permute-done.7 = f32[32,128]{1,0:T(8,128)S(1)} collective-permute-done((f32[32,128]{1,0:T(8,128)S(1)}, f32[32,128]{1,0:T(8,128)S(1)}, u32[]{:S(2)}, u32[]{:S(2)}) %collective-permute-start.7) | collective-permute-done | bytes 16416 | tf_op jit(solution)/shard_map/sums_of_taps/ppermute | solution.py:588
  136.0 0.7 collective-permute-done.6
  136.8 0.7 copy.14
  137.5 10.2 %all-to-all-done.4.pack_ref = bf16[16,192,128]{2,1,0:T(8,128)(2,1)S(1)} async-done(((bf16[16,192,128]{2,1,0:T(8,128)(2,1)}), bf16[16,192,128]{2,1,0:T(8,128)(2,1)S(1)}, u32[]{:S(2)}, u32[]{:S(2)}) %all-to-all-start.4) | async-done | bytes 786464 | tf_op jit(solution)/shard_map/channels_to_frames/all_to_all | solution.py:582
  147.7 2.3 %copy-done = bf16[1536,1536]{1,0:T(8,128)(2,1)S(1)} copy-done((bf16[1536,1536]{1,0:T(8,128)(2,1)S(1)}, bf16[1536,1536]{1,0:T(8,128)(2,1)}, u32[]{:S(2)}) %copy-start) | copy-done | bytes 4718616
  150.0 3.6 %join.1 = (bf16[128,1536]{1,0:T(8,128)(2,1)}, bf16[128,1536]{1,0:T(8,128)(2,1)}) custom-call(bf16[16,192,128]{2,1,0:T(8,128)(2,1)S(1)} %all-to-all-done.4.pack_ref, bf16[1536,1536]{1,0:T(8,128)(2,1)S(1)} %copy-done), custom_call_target="tpu_custom_call" | custom-call | tf_op jit(solution)/shard_map/join/join/pallas_call | solution.py:35
  (18 shorter events, 2.1 us)
Async XLA Ops:
  7.2 79.8 %all-gather.6.cloned.1.call-start = ((), (), s32[]{:S(2)}) async-start(), calls=%async_computation.6 | async-start | bytes 6684672 | tf_op jit(solution)/shard_map/cotangent_of_group/all_gather | solution.py:403
  12.3 18.9 %all-to-all-start = ((bf16[16,6,1664]{2,1,0:T(8,128)(2,1)}), bf16[16,6,1664]{2,1,0:T(8,128)(2,1)}, u32[]{:S(2)}, u32[]{:S(2)}) async-start(bf16[16,6,1664]{2,1,0:T(8,128)(2,1)} %get-tuple-element.32), calls=%async_computation | async-start | bytes 851968 | tf_op jit(solution)/shard_map/rows_and_params/all_to_all | solution.py:440
  20.0 105.0 %all-gather.4.cloned.1.call-start = ((), (), s32[]{:S(2)}) async-start(), calls=%async_computation.5 | async-start | bytes 5013504 | tf_op jit(solution)/shard_map/weights_of_group/all_gather | solution.py:493
  20.0 8.7 %collective-permute-start = (bf16[16,1536]{1,0:T(8,128)(2,1)}, bf16[16,1536]{1,0:T(8,128)(2,1)}, u32[]{:S(2)}, u32[]{:S(2)}) collective-permute-start(bf16[16,1536]{1,0:T(8,128)(2,1)} %get-tuple-element.30), channel_id=1, source_target_pairs={{1,2},{3,4},{5,6},{7,8},{9,10},{11,12},{13,14},{15,16},{17,18},{19... | collective-permute-start | bytes 147464 | tf_op jit(solution)/shard_map/edge_frames/ppermute | solution.py:437
  93.7 0.8 copy-start.1
  94.5 13.9 %all-to-all-start.3 = ((bf16[16,6,1664]{2,1,0:T(8,128)(2,1)}), bf16[16,6,1664]{2,1,0:T(8,128)(2,1)S(1)}, u32[]{:S(2)}, u32[]{:S(2)}) async-start(bf16[16,6,1664]{2,1,0:T(8,128)(2,1)} %get-tuple-element.41), calls=%async_computation.3 | async-start | bytes 851968 | tf_op jit(solution)/shard_map/norm_grad_sums/all_to_all | solution.py:543
  98.0 10.3 %collective-permute-start.1 = (bf16[8,2,16,128]{3,2,1,0:T(8,128)(2,1)S(1)}, bf16[8,2,16,128]{3,2,1,0:T(8,128)(2,1)S(1)}, u32[]{:S(2)}, u32[]{:S(2)}) collective-permute-start(bf16[8,2,16,128]{3,2,1,0:T(8,128)(2,1)S(1)} %get-tuple-element.42), channel_id=1, source_target_pairs={{0,2},{2,4},{4,6},{6,8},{8,10},{10,12},{12,14},{14,16},{16,18},{18... | collective-permute-start | bytes 196616 | tf_op jit(solution)/shard_map/edge_grads/ppermute | solution.py:539
  99.3 9.1 %collective-permute-start.2 = (bf16[8,2,16,128]{3,2,1,0:T(8,128)(2,1)S(1)}, bf16[8,2,16,128]{3,2,1,0:T(8,128)(2,1)S(1)}, u32[]{:S(2)}, u32[]{:S(2)}) collective-permute-start(bf16[8,2,16,128]{3,2,1,0:T(8,128)(2,1)S(1)} %get-tuple-element.43), channel_id=1, source_target_pairs={{2,0},{4,2},{6,4},{8,6},{10,8},{12,10},{14,12},{16,14},{18,16},{20... | collective-permute-start | bytes 196616 | tf_op jit(solution)/shard_map/edge_grads/ppermute | solution.py:540
  108.4 1.0 copy-start.2
  119.4 28.3 %all-to-all-start.4 = ((bf16[16,192,128]{2,1,0:T(8,128)(2,1)}), bf16[16,192,128]{2,1,0:T(8,128)(2,1)S(1)}, u32[]{:S(2)}, u32[]{:S(2)}) async-start(bf16[16,192,128]{2,1,0:T(8,128)(2,1)} %get-tuple-element.44), calls=%async_computation.4 | async-start | bytes 1572864 | tf_op jit(solution)/shard_map/channels_to_frames/all_to_all | solution.py:582
  125.0 3.1 %collective-permute-start.5 = (f32[32,128]{1,0:T(8,128)S(1)}, f32[32,128]{1,0:T(8,128)S(1)}, u32[]{:S(2)}, u32[]{:S(2)}) collective-permute-start(f32[32,128]{1,0:T(8,128)S(1)} %get-tuple-element.50), channel_id=1, source_target_pairs={{0,24},{8,0},{16,8},{24,16},{1,25},{9,1},{17,9},{25,17},{2,26},{10... | collective-permute-start | bytes 49160 | tf_op jit(solution)/shard_map/sums_of_taps/ppermute | solution.py:588
  125.7 3.8 %collective-permute-start.3 = (f32[32,128]{1,0:T(8,128)S(1)}, f32[32,128]{1,0:T(8,128)S(1)}, u32[]{:S(2)}, u32[]{:S(2)}) collective-permute-start(f32[32,128]{1,0:T(8,128)S(1)} %get-tuple-element.50), channel_id=1, source_target_pairs={{0,8},{8,16},{16,24},{24,0},{1,9},{9,17},{17,25},{25,1},{2,10},{10... | collective-permute-start | bytes 49160 | tf_op jit(solution)/shard_map/sums_of_taps/ppermute | solution.py:588
  126.6 4.4 %collective-permute-start.4 = (f32[32,128]{1,0:T(8,128)S(1)}, f32[32,128]{1,0:T(8,128)S(1)}, u32[]{:S(2)}, u32[]{:S(2)}) collective-permute-start(f32[32,128]{1,0:T(8,128)S(1)} %get-tuple-element.50), channel_id=1, source_target_pairs={{0,16},{8,24},{16,0},{24,8},{1,17},{9,25},{17,1},{25,9},{2,18},{10... | collective-permute-start | bytes 49160 | tf_op jit(solution)/shard_map/sums_of_taps/ppermute | solution.py:588
  131.0 2.9 %collective-permute-start.8 = (f32[32,128]{1,0:T(8,128)S(1)}, f32[32,128]{1,0:T(8,128)S(1)}, u32[]{:S(2)}, u32[]{:S(2)}) collective-permute-start(f32[32,128]{1,0:T(8,128)S(1)} %add_add_fusion), channel_id=1, source_target_pairs={{0,6},{2,0},{4,2},{6,4},{1,7},{3,1},{5,3},{7,5},{8,14},{10,8},{12,... | collective-permute-start | bytes 49160 | tf_op jit(solution)/shard_map/sums_of_taps/ppermute | solution.py:588
  131.6 4.4 %collective-permute-start.7 = (f32[32,128]{1,0:T(8,128)S(1)}, f32[32,128]{1,0:T(8,128)S(1)}, u32[]{:S(2)}, u32[]{:S(2)}) collective-permute-start(f32[32,128]{1,0:T(8,128)S(1)} %add_add_fusion), channel_id=1, source_target_pairs={{0,4},{2,6},{4,0},{6,2},{1,5},{3,7},{5,1},{7,3},{8,12},{10,14},{12... | collective-permute-start | bytes 49160 | tf_op jit(solution)/shard_map/sums_of_taps/ppermute | solution.py:588
  132.6 4.1 %collective-permute-start.6 = (f32[32,128]{1,0:T(8,128)S(1)}, f32[32,128]{1,0:T(8,128)S(1)}, u32[]{:S(2)}, u32[]{:S(2)}) collective-permute-start(f32[32,128]{1,0:T(8,128)S(1)} %add_add_fusion), channel_id=1, source_target_pairs={{0,2},{2,4},{4,6},{6,0},{1,3},{3,5},{5,7},{7,1},{8,10},{10,12},{12... | collective-permute-start | bytes 49160 | tf_op jit(solution)/shard_map/sums_of_taps/ppermute | solution.py:588
  147.7 2.3 %copy-start = (bf16[1536,1536]{1,0:T(8,128)(2,1)S(1)}, bf16[1536,1536]{1,0:T(8,128)(2,1)}, u32[]{:S(2)}) copy-start(bf16[1536,1536]{1,0:T(8,128)(2,1)} %all-gather.4.cloned.1.call-done.w_ref) | copy-start | bytes 14155780
Sparse Core Ops, SparseCore 0:
  9.8 62.9 all-gather.5
  76.8 39.8 all-gather.3

commit v4 on v3

--- a/solution.py
+++ b/solution.py
@@ -32,10 +32,11 @@
 def call(body, outs, ins, scratch, name, limit=64, work=0, **more):
     if work:
         more["cost_estimate"] = pl.CostEstimate(flops=work, bytes_accessed=2**20, transcendentals=0)
+    if scratch:
+        more["scratch_shapes"] = scratch
     return pl.pallas_call(
         body,
         out_shape=outs,
-        scratch_shapes=scratch,
         name=name,
         compiler_params=pltpu.CompilerParams(vmem_limit_bytes=limit * 2**20),
         **more,
@@ -161,22 +162,24 @@
     return jnp.where(same, rows, 0.0)
 
 
+def rows_body(wp_ref, par_ref, w_ref, wide_ref, tmp_ref, wf_ref):
+    wf_ref[CHAN:] = jnp.zeros((LANES - CHAN, WIDE), F32)
+    for d in range(SETS):
+        wf_ref[d * OWN : (d + 1) * OWN] = wp_ref[d].astype(F32)
+    wide = wf_ref[:, 0:D].astype(BF16)
+    wide_ref[...] = wide
+    w_ref[...] = wide[:CHAN]
+    tmp_ref[...] = wf_ref[:, D:WIDE].T
+    par_ref[...] = tmp_ref[0:PART] + tmp_ref[PART : 2 * PART] + tmp_ref[2 * PART : 3 * PART]
+
+
 def conv_body(
-    x_ref, wp_ref, conv_ref, stat_ref, par_ref, w_ref, wide_ref,
-    xf_ref, prev_ref, next_ref, tmp_ref, wf_ref, run_ref,
+    x_ref, par_ref, conv_ref, stat_ref, xf_ref, prev_ref, next_ref, run_ref
 ):
     step = pl.program_id(0)
 
     @pl.when(step == 0)
     def _():
-        wf_ref[CHAN:] = jnp.zeros((LANES - CHAN, WIDE), F32)
-        for d in range(SETS):
-            wf_ref[d * OWN : (d + 1) * OWN] = wp_ref[d].astype(F32)
-        wide = wf_ref[:, 0:D].astype(BF16)
-        wide_ref[...] = wide
-        w_ref[...] = wide[:CHAN]
-        tmp_ref[...] = wf_ref[:, D:WIDE].T
-        par_ref[...] = tmp_ref[0:PART] + tmp_ref[PART : 2 * PART] + tmp_ref[2 * PART : 3 * PART]
         run_ref[...] = jnp.zeros_like(run_ref)
 
     x = x_ref[0].astype(F32)
@@ -289,7 +292,7 @@
 
 
 def back_body(
-    set_ref, gp_ref, conv_ref, x_ref, act_ref, par_ref, stat_ref, sum_ref, left_ref, right_ref,
+    set_ref, gp_ref, conv_ref, x_ref, par_ref, stat_ref, sum_ref, left_ref, right_ref,
     pack_ref, taps_ref, sums_ref,
     gc_ref, xf_ref, prev_ref, next_ref, tap_ref, run_ref,
 ):
@@ -345,49 +348,31 @@
             pieces[core * (ROWS // CHUNK) : (core + 1) * (ROWS // CHUNK)], axis=0
         )
         half = half * m[core * ROWS : (core + 1) * ROWS]
-        turned = pltpu.roll(half, CHAN, 1)
-        lane = lax.broadcasted_iota(jnp.int32, (ROWS, LANES), 1)
-        pack_ref[core, 0:ROWS] = jnp.where(
-            lane < CHAN, act_ref[core].astype(F32), turned
+        pack_ref[core] = half.astype(BF16)
+
+    @pl.when(b == Z - 1)
+    def _():
+        taps_ref[...] = jnp.sum(tap_ref[...], axis=1)
+
+
+def out_body(act_ref, w_ref, out_ref):
+    total = jnp.zeros((ROWS, D), F32)
+    for at in range(GROUP):
+        total = total + jnp.dot(
+            act_ref[at][:, :CHAN], w_ref[at * CHAN : (at + 1) * CHAN], preferred_element_type=F32
+        )
+    out_ref[...] = total.astype(BF16)
+
+
+def join_body(back_ref, gh_ref, four_ref):
+    width = 4 * CHAN
+    permute = one_hot()
+    for part in range(Z // 2):
+        for i in range(4):
+            four_ref[:, i * LANES : (i + 1) * LANES] = back_ref[4 * part + i]
+        gh_ref[:, part * width : (part + 1) * width] = lax.dot_general(
+            four_ref[...], permute, (((1,), (1,)), ((), ())), preferred_element_type=F32
         ).astype(BF16)
-        lane = lane[: ROWS // 2]
-        pack_ref[core, ROWS : ROWS + ROWS // 2] = jnp.where(
-            lane < LANES // 2, turned[: ROWS // 2], pltpu.roll(turned[ROWS // 2 :], LANES // 2, 1)
-        ).astype(BF16)
-
-    @pl.when(b == Z - 1)
-    def _():
-        taps_ref[...] = jnp.sum(tap_ref[...], axis=1)
-
-
-def join_body(pack_ref, w_ref, out_ref, gh_ref, four_ref, total_ref):
-    step = pl.program_id(0)
-    lane = lax.broadcasted_iota(jnp.int32, (ROWS // 2, LANES), 1)
-
-    @pl.when(step == 0)
-    def _():
-        total_ref[...] = jnp.zeros_like(total_ref)
-
-    total = total_ref[...]
-    for i in range(4):
-        main = pack_ref[i, 0:ROWS]
-        total = total + jnp.dot(
-            main[:, :CHAN], w_ref[i * CHAN : (i + 1) * CHAN], preferred_element_type=F32
-        )
-        main = main.astype(F32)
-        rest = pack_ref[i, ROWS : ROWS + ROWS // 2].astype(F32)
-        upper = jnp.where(lane < LANES // 2, rest, main[: ROWS // 2])
-        lower = jnp.where(lane < LANES // 2, pltpu.roll(rest, LANES // 2, 1), main[ROWS // 2 :])
-        turned = jnp.concatenate([upper, lower], axis=0)
-        four_ref[:, i * LANES : (i + 1) * LANES] = pltpu.roll(turned, LANES - CHAN, 1).astype(BF16)
-    total_ref[...] = total
-    gh_ref[...] = lax.dot_general(
-        four_ref[...], one_hot(), (((1,), (1,)), ((), ())), preferred_element_type=F32
-    ).astype(BF16)
-
-    @pl.when(step == Z // 2 - 1)
-    def _():
-        out_ref[...] = total.astype(BF16)
 
 
 def shape(dims, kind):
@@ -456,40 +441,40 @@
     whole = lambda *dims: pl.BlockSpec(dims, lambda i: (0,) * len(dims))
     each = lambda *dims: pl.BlockSpec(dims, lambda i: (i,) + (0,) * (len(dims) - 1))
 
+    with jax.named_scope("unpack_rows"):
+        par, rows, wide = call(
+            rows_body,
+            (shape((PART, LANES), F32), shape((CHAN, D), BF16), shape((LANES, D), BF16)),
+            (wp,),
+            [pltpu.VMEM((LANES, LANES), F32), pltpu.VMEM((LANES, WIDE), F32)],
+            "rows",
+            limit=24,
+            work=2 * 10**9,
+            in_specs=[vmem()],
+            out_specs=[vmem()] * 3,
+        )
+
     with jax.named_scope("conv"):
-        conv, stat, par, rows, wide = call(
+        conv, stat = call(
             conv_body,
-            (
-                shape((Z, BLOCK, LANES), F32),
-                shape((SETS, 8, LANES), F32),
-                shape((PART, LANES), F32),
-                shape((CHAN, D), BF16),
-                shape((LANES, D), BF16),
-            ),
-            (x, wp),
+            (shape((Z, BLOCK, LANES), F32), shape((SETS, 8, LANES), F32)),
+            (x, par),
             [
                 pltpu.VMEM((SPAN, LANES), F32),
                 pltpu.VMEM((BLOCK, LANES), F32),
                 pltpu.VMEM((BLOCK, LANES), F32),
-                pltpu.VMEM((LANES, LANES), F32),
-                pltpu.VMEM((LANES, WIDE), F32),
                 pltpu.VMEM((8, LANES), F32),
             ],
             "conv",
             limit=24,
             work=6 * 10**9,
             grid=(Z,),
-            in_specs=[each(1, SPAN, LANES), whole(SETS, OWN, WIDE)],
-            out_specs=[
-                each(1, BLOCK, LANES),
-                whole(SETS, 8, LANES),
-                whole(PART, LANES),
-                whole(CHAN, D),
-                whole(LANES, D),
-            ],
+            in_specs=[each(1, SPAN, LANES), whole(PART, LANES)],
+            out_specs=[each(1, BLOCK, LANES), whole(SETS, 8, LANES)],
         )
 
     with jax.named_scope("weights_of_group"):
+        rows, conv = lax.optimization_barrier((rows, conv))
         w_all = lax.all_gather(rows, IN_GROUP, tiled=True)
 
     with jax.named_scope("norm_sums"):
@@ -542,15 +527,19 @@
     with jax.named_scope("norm_grad_sums"):
         gw = lax.all_to_all(gw, OVER_SETS, 0, 0)
 
+    with jax.named_scope("act_to_frames"):
+        act, gw = lax.optimization_barrier((act, gw))
+        act = lax.all_to_all(act, IN_GROUP, 0, 0)
+
     with jax.named_scope("conv_grad"):
         pack, taps, both = call(
             back_body,
             (
-                shape((GROUP, ROWS + ROWS // 2, LANES), BF16),
+                shape((GROUP, ROWS, LANES), BF16),
                 shape((32, LANES), F32),
                 shape((8, LANES), F32),
             ),
-            (this_set.reshape(1), gp, conv, x, act, par, stat, gw, left, right),
+            (this_set.reshape(1), gp, conv, x, par, stat, gw, left, right),
             [
                 pltpu.VMEM((SPAN, LANES), F32),
                 pltpu.VMEM((BLOCK, LANES), F32),
@@ -568,26 +557,39 @@
                 each(1, BLOCK, LANES),
                 each(1, BLOCK, LANES),
                 each(1, SPAN, LANES),
-                each(CORES, ROWS, LANES),
                 whole(PART, LANES),
                 whole(SETS, 8, LANES),
                 whole(SETS, OWN, WIDE),
                 whole(Z, 2, HALO, LANES),
                 whole(Z, 2, HALO, LANES),
             ],
-            out_specs=[each(CORES, ROWS + ROWS // 2, LANES), whole(32, LANES), whole(8, LANES)],
+            out_specs=[each(CORES, ROWS, LANES), whole(32, LANES), whole(8, LANES)],
         )
 
     with jax.named_scope("channels_to_frames"):
         back = lax.all_to_all(pack, IN_GROUP, 0, 0)
 
+    with jax.named_scope("module_out"):
+        taps, w_all, act = lax.optimization_barrier((taps, w_all, act))
+        module_out = call(
+            out_body,
+            shape((ROWS, D), BF16),
+            (act, w_all),
+            [],
+            "module_out",
+            limit=24,
+            work=4 * 10**9,
+            in_specs=[vmem()] * 2,
+            out_specs=vmem(),
+        )
+
     with jax.named_scope("sums_of_taps"):
-        taps, w_all = lax.optimization_barrier((taps, w_all))
         for axis, size in (("x", X), ("y", Y)):
             moved = [
                 lax.ppermute(taps, axis, [(i, (i + by) % size) for i in range(size)])
                 for by in range(1, size)
             ]
+            *moved, module_out = lax.optimization_barrier((*moved, module_out))
             taps = taps + sum(moved)
         at = this_set * OWN
         grad_kernel = lax.dynamic_slice(taps, (0, at), (KERNEL, OWN))
@@ -598,26 +600,15 @@
         grad_weight = jnp.sum(gw[:, :, :D].astype(F32), axis=0)
 
     with jax.named_scope("join"):
-        width = 2 * D // Z
-        module_out, grad_hidden = call(
+        grad_hidden = call(
             join_body,
-            (shape((ROWS, D), BF16), shape((ROWS, D), BF16)),
-            (back, w_all),
-            [
-                pltpu.VMEM((ROWS, 4 * LANES), BF16),
-                pltpu.VMEM((ROWS, D), F32),
-            ],
+            shape((ROWS, D), BF16),
+            (back,),
+            [pltpu.VMEM((ROWS, 4 * LANES), BF16)],
             "join",
             limit=24,
-            grid=(Z // 2,),
-            in_specs=[
-                pl.BlockSpec((4, ROWS + ROWS // 2, LANES), lambda i: (i, 0, 0)),
-                pl.BlockSpec((width, D), lambda i: (i, 0)),
-            ],
-            out_specs=[
-                pl.BlockSpec((ROWS, D), lambda i: (0, 0)),
-                pl.BlockSpec((ROWS, width), lambda i: (0, i)),
-            ],
+            in_specs=[vmem()],
+            out_specs=vmem(),
         )
     return (module_out, grad_hidden, grad_kernel, grad_scale, grad_shift, grad_weight)
 

time: 161 us -> 158 us (0.981)
  blocking collectives: 48.4 us -> 10.3 us
  starting transfers between devices: 30.2 us -> 51.6 us
  waiting for transfers between devices: 27 us -> 40.9 us
    all_to_all x1 -> x0, blocking collectives: 38.1 us -> none  [local(): x = lax.all_to_all(frames, IN_GROUP, 0, 0).reshape(Z, SPAN, LANES)]
    all_to_all x0 -> x2, waiting for transfers between devices: none -> 28.9 us  [the longest x1 22 us: local(): x = lax.all_to_all(frames, IN_GROUP, 0, 0).reshape(Z, SPAN, LANES)]
    all_to_all x0 -> x2, starting transfers between devices: none -> 19.2 us  [the longest x1 12.8 us: local(): x = lax.all_to_all(frames, IN_GROUP, 0, 0).reshape(Z, SPAN, LANES)]
    all_to_all x1, waiting for transfers between devices: 10.2 us -> 3.14 us  [local(): back = lax.all_to_all(pack, IN_GROUP, 0, 0)]
    ppermute x6, waiting for transfers between devices: 6.29 us -> 0.02 us  [local(): lax.ppermute(taps, axis, [(i, (i + by) % size) for i in range(size)])]
    ppermute x1, waiting for transfers between devices: 5.45 us -> 0.01 us  [local(): left = lax.ppermute(last_rows, OVER_SETS, up)]
    ppermute x6, starting transfers between devices: 4.13 us -> 8.01 us  [local(): lax.ppermute(taps, axis, [(i, (i + by) % size) for i in range(size)])]
    all_to_all x1, waiting for transfers between devices: 0.01 us -> 3.69 us  [local(): gw = lax.all_to_all(gw, OVER_SETS, 0, 0)]
  transfers between devices with their start and end apart: 14 -> 16, of which waited for: 8 -> 5; matrix products, arithmetic and copies ran while one was open for 2% -> 2% of each run, Pallas kernels for 18% -> 20%
where the time goes in v4:
time: 158 us; the launch traced here: 157 us
  starting transfers between devices  51.6 us (33%)
  waiting for transfers between devices  40.9 us (26%)
  Pallas kernels  32.1 us (20%)
  between operations  14.2 us (9%)
  blocking collectives  10.3 us (7%)
  local copies, waits for them, and re-layouts  7.15 us (5%)
    pallas_call x8, Pallas kernels, call(): pl.pallas_call(body, out_shape=outs, name=name, compiler_params=pltpu.Com...  32.1 us
    all_to_all x1, waiting for transfers between devices, local(): x = lax.all_to_all(frames, IN_GROUP, 0, 0).reshape(Z, SPAN, LANES)  22 us
    all_to_all x1, starting transfers between devices, local(): x = lax.all_to_all(frames, IN_GROUP, 0, 0).reshape(Z, SPAN, LANES)  12.8 us
    all_to_all x1, blocking collectives, local(): stat = lax.all_to_all(stat, OVER_SETS, 0, 0)  10.3 us
    ppermute x6, starting transfers between devices, local(): lax.ppermute(taps, axis, [(i, (i + by) % size) for i in range(size)])  8.01 us
    all_to_all x1, starting transfers between devices, local(): wp = lax.all_to_all(wp, OVER_SETS, 0, 0)  7.64 us
    all_to_all x1, waiting for transfers between devices, local(): act = lax.all_to_all(act, IN_GROUP, 0, 0)  6.91 us
    all_to_all x1, starting transfers between devices, local(): act = lax.all_to_all(act, IN_GROUP, 0, 0)  6.37 us
  transfers between devices with their start and end apart: 16, of which 5 were waited for; matrix products, arithmetic and copies ran while one was open for 2% of the time, Pallas kernels for 20%

profile of v4, /device:TPU:1, one launch (start us, length us, event | category | flops | bytes accessed | tf_op | source)
XLA Modules:
  0.0 156.9 jit_solution(8190201920084056035)
XLA Ops:
  7.9 1.4 pad_dynamic-slice_fusion
  9.3 3.1 %prepare.1 = (bf16[16,6,1664]{2,1,0:T(8,128)(2,1)}, f32[128,128]{1,0:T(8,128)}, bf16[128,1536]{1,0:T(8,128)(2,1)}, bf16[16,1536]{1,0:T(8,128)(2,1)}) custom-call(s32[1]{0:T(128)} %bitcast.1.core_ref, s32[1,256]{1,0:T(1,128)} %bitcast.18, f32[6,31]{1,0:T(8,128)} %bitcast.17, f32[1,6]{1,0:T(1,128)} %bitcast.19, f32[1,6]{1,0:T(1,128)} %bitcast.20, ...), custom_call_target="tpu_custom_call" | custom-call | tf_op jit(solution)/shard_map/prepare/prepare/pallas_call | solution.py:37
  12.3 7.6 %all-to-all-start = ((bf16[16,6,1664]{2,1,0:T(8,128)(2,1)}), bf16[16,6,1664]{2,1,0:T(8,128)(2,1)}, u32[]{:S(2)}, u32[]{:S(2)}) async-start(bf16[16,6,1664]{2,1,0:T(8,128)(2,1)} %get-tuple-element.43), calls=%async_computation | async-start | bytes 851968 | tf_op jit(solution)/shard_map/rows_and_params/all_to_all | solution.py:425
  20.0 4.3 %collective-permute-start = (bf16[16,1536]{1,0:T(8,128)(2,1)}, bf16[16,1536]{1,0:T(8,128)(2,1)}, u32[]{:S(2)}, u32[]{:S(2)}) collective-permute-start(bf16[16,1536]{1,0:T(8,128)(2,1)} %get-tuple-element.41), channel_id=1, source_target_pairs={{1,2},{3,4},{5,6},{7,8},{9,10},{11,12},{13,14},{15,16},{17,18},{19... | collective-permute-start | bytes 147464 | tf_op jit(solution)/shard_map/edge_frames/ppermute | solution.py:422
  24.3 4.4 %collective-permute-done.halo_ref = bf16[16,1536]{1,0:T(8,128)(2,1)} collective-permute-done((bf16[16,1536]{1,0:T(8,128)(2,1)}, bf16[16,1536]{1,0:T(8,128)(2,1)}, u32[]{:S(2)}, u32[]{:S(2)}) %collective-permute-start) | collective-permute-done | bytes 49184 | tf_op jit(solution)/shard_map/edge_frames/ppermute | solution.py:422
  28.7 2.4 %split.1 = bf16[16,144,128]{2,1,0:T(8,128)(2,1)} custom-call(s32[1]{0:T(128)} %bitcast.1.core_ref, bf16[128,1536]{1,0:T(8,128)(2,1)} %get-tuple-element.40.own_ref, bf16[16,1536]{1,0:T(8,128)(2,1)} %collective-permute-done.halo_ref, f32[128,128]{1,0:T(8,128)} %get-tuple-element.42.ext_ref), custom_call_target="tpu_custom_call" | custom-call | tf_op jit(solution)/shard_map/frames_to_channels/split/pallas_call | solution.py:37
  31.2 12.8 %all-to-all-start.1 = ((bf16[16,144,128]{2,1,0:T(8,128)(2,1)}), bf16[16,144,128]{2,1,0:T(8,128)(2,1)S(1)}, u32[]{:S(2)}, u32[]{:S(2)}) async-start(bf16[16,144,128]{2,1,0:T(8,128)(2,1)} %split.1), calls=%async_computation.1 | async-start | bytes 1179648 | tf_op jit(solution)/shard_map/frames_to_channels/all_to_all | solution.py:439
  44.1 1.9 %rows.1 = (f32[40,128]{1,0:T(8,128)S(1)}, bf16[96,1536]{1,0:T(8,128)(2,1)}, bf16[128,1536]{1,0:T(8,128)(2,1)S(1)}) custom-call(bf16[16,6,1664]{2,1,0:T(8,128)(2,1)} %all-to-all-done.wp_ref), custom_call_target="tpu_custom_call" | custom-call | flops 2000000000 | bytes 1048576 | tf_op jit(solution)/shard_map/unpack_rows/rows/pallas_call | solution.py:37
  45.9 22.0 %all-to-all-done.1 = bf16[16,144,128]{2,1,0:T(8,128)(2,1)S(1)} async-done(((bf16[16,144,128]{2,1,0:T(8,128)(2,1)}), bf16[16,144,128]{2,1,0:T(8,128)(2,1)S(1)}, u32[]{:S(2)}, u32[]{:S(2)}) %all-to-all-start.1) | async-done | bytes 589856 | tf_op jit(solution)/shard_map/frames_to_channels/all_to_all | solution.py:439
  67.9 5.4 %conv.1 = (f32[8,256,128]{2,1,0:T(8,128)S(1)}, f32[16,8,128]{2,1,0:T(8,128)S(1)}) custom-call(bf16[8,288,128]{2,1,0:T(8,128)(2,1)S(1)} %bitcast.13, f32[40,128]{1,0:T(8,128)S(1)} %get-tuple-element.47.par_ref), custom_call_target="tpu_custom_call" | custom-call | flops 6000000000 | bytes 1048576 | tf_op jit(solution)/shard_map/conv/conv/pallas_call | solution.py:37
  73.4 10.3 %all_to_all.30.stat_ref = f32[16,8,128]{2,1,0:T(8,128)S(1)} all-to-all(f32[16,8,128]{2,1,0:T(8,128)S(1)} %get-tuple-element.51), channel_id=1, replica_groups=mesh['z'=8,'x'=4,'y'=4,'core'=2] {'x','y'}, dimensions={0} | all-to-all | bytes 131072 | tf_op jit(solution)/shard_map/norm_sums/all_to_all | solution.py:481
  83.7 6.8 %activation.1 = (bf16[16,128,128]{2,1,0:T(8,128)(2,1)}, f32[8,256,128]{2,1,0:T(8,128)S(1)}, bf16[8,2,16,128]{3,2,1,0:T(8,128)(2,1)S(1)}, bf16[8,2,16,128]{3,2,1,0:T(8,128)(2,1)S(1)}, bf16[16,6,1664]{2,1,0:T(8,128)(2,1)}) custom-call(f32[8,256,128]{2,1,0:T(8,128)S(1)} %get-tuple-element.49.conv_ref, bf16[8,288,128]{2,1,0:T(8,128)(2,1)S(1)} %bitcast.14, ...), custom_call_target="tpu_custom_call" | custom-call | tf_op jit(solution)/shard_map/activation_grad/activation/pallas_call | solution.py:37
  90.5 1.0 copy-done.1
  91.5 3.6 %all-to-all-start.3 = ((bf16[16,6,1664]{2,1,0:T(8,128)(2,1)}), bf16[16,6,1664]{2,1,0:T(8,128)(2,1)S(1)}, u32[]{:S(2)}, u32[]{:S(2)}) async-start(bf16[16,6,1664]{2,1,0:T(8,128)(2,1)} %get-tuple-element.54), calls=%async_computation.3 | async-start | bytes 851968 | tf_op jit(solution)/shard_map/norm_grad_sums/all_to_all | solution.py:528
  95.0 1.3 collective-permute-start.1
  96.3 3.6 %collective-permute-start.2 = (bf16[8,2,16,128]{3,2,1,0:T(8,128)(2,1)S(1)}, bf16[8,2,16,128]{3,2,1,0:T(8,128)(2,1)S(1)}, u32[]{:S(2)}, u32[]{:S(2)}) collective-permute-start(bf16[8,2,16,128]{3,2,1,0:T(8,128)(2,1)S(1)} %get-tuple-element.57), channel_id=1, source_target_pairs={{2,0},{4,2},{6,4},{8,6},{10,8},{12,10},{14,12},{16,14},{18,16},{20... | collective-permute-start | bytes 196616 | tf_op jit(solution)/shard_map/edge_grads/ppermute | solution.py:525
  99.9 3.7 %all-to-all-done.3.sum_ref = bf16[16,6,1664]{2,1,0:T(8,128)(2,1)S(1)} async-done(((bf16[16,6,1664]{2,1,0:T(8,128)(2,1)}), bf16[16,6,1664]{2,1,0:T(8,128)(2,1)S(1)}, u32[]{:S(2)}, u32[]{:S(2)}) %all-to-all-start.3) | async-done | bytes 319520 | tf_op jit(solution)/shard_map/norm_grad_sums/all_to_all | solution.py:528
  103.6 6.4 %all-to-all-start.4 = ((bf16[16,128,128]{2,1,0:T(8,128)(2,1)}), bf16[16,128,128]{2,1,0:T(8,128)(2,1)S(1)}, u32[]{:S(2)}, u32[]{:S(2)}) async-start(bf16[16,128,128]{2,1,0:T(8,128)(2,1)} %get-tuple-element.60), calls=%async_computation.4 | async-start | bytes 1048576 | tf_op jit(solution)/shard_map/act_to_frames/all_to_all | solution.py:532
  110.0 1.2 copy-done.2
  111.2 8.6 %conv_grad.1 = (bf16[16,128,128]{2,1,0:T(8,128)(2,1)}, f32[32,128]{1,0:T(8,128)S(1)}, f32[8,128]{1,0:T(8,128)S(1)}) custom-call(s32[1]{0:T(128)} %bitcast.set_ref, f32[8,256,128]{2,1,0:T(8,128)S(1)} %copy-done.2, f32[8,256,128]{2,1,0:T(8,128)S(1)} %get-tuple-element.49.conv_ref, bf16[8,288,128]{2,1,0:T(8,128)(2,1)S(1)} %bitcast.15, ...), custom_call_target="tpu_custom_call" | custom-call | flops 10000000000 | bytes 1048576 | tf_op jit(solution)/shard_map/conv_grad/conv_grad/pallas_call | solution.py:37
  119.8 6.9 %all-to-all-done.4.act_ref = bf16[16,128,128]{2,1,0:T(8,128)(2,1)S(1)} async-done(((bf16[16,128,128]{2,1,0:T(8,128)(2,1)}), bf16[16,128,128]{2,1,0:T(8,128)(2,1)S(1)}, u32[]{:S(2)}, u32[]{:S(2)}) %all-to-all-start.4) | async-done | bytes 524320 | tf_op jit(solution)/shard_map/act_to_frames/all_to_all | solution.py:532
  126.7 3.9 %all-to-all-start.5 = ((bf16[16,128,128]{2,1,0:T(8,128)(2,1)}), bf16[16,128,128]{2,1,0:T(8,128)(2,1)S(1)}, u32[]{:S(2)}, u32[]{:S(2)}) async-start(bf16[16,128,128]{2,1,0:T(8,128)(2,1)} %get-tuple-element.69), calls=%async_computation.5 | async-start | bytes 1048576 | tf_op jit(solution)/shard_map/channels_to_frames/all_to_all | solution.py:570
  130.6 0.7 convert_reduce_fusion
  132.0 2.4 %collective-permute-start.4 = (f32[32,128]{1,0:T(8,128)S(1)}, f32[32,128]{1,0:T(8,128)S(1)}, u32[]{:S(2)}, u32[]{:S(2)}) collective-permute-start(f32[32,128]{1,0:T(8,128)S(1)} %get-tuple-element.61), channel_id=1, source_target_pairs={{0,16},{8,24},{16,0},{24,8},{1,17},{9,25},{17,1},{25,9},{2,18},{10... | collective-permute-start | bytes 49160 | tf_op jit(solution)/shard_map/sums_of_taps/ppermute | solution.py:589
  134.4 1.2 collective-permute-start.5
  135.5 2.3 %copy-done = bf16[1536,1536]{1,0:T(8,128)(2,1)S(1)} copy-done((bf16[1536,1536]{1,0:T(8,128)(2,1)S(1)}, bf16[1536,1536]{1,0:T(8,128)(2,1)}, u32[]{:S(2)}) %copy-start) | copy-done | bytes 4718616
  137.9 2.5 %module_out.1 = bf16[128,1536]{1,0:T(8,128)(2,1)} custom-call(bf16[16,128,128]{2,1,0:T(8,128)(2,1)S(1)} %all-to-all-done.4.act_ref, bf16[1536,1536]{1,0:T(8,128)(2,1)S(1)} %copy-done), custom_call_target="tpu_custom_call" | custom-call | flops 4000000000 | bytes 1048576 | tf_op jit(solution)/shard_map/module_out/module_out/pallas_call | solution.py:37
  140.9 2.2 %collective-permute-start.7 = (f32[32,128]{1,0:T(8,128)S(1)}, f32[32,128]{1,0:T(8,128)S(1)}, u32[]{:S(2)}, u32[]{:S(2)}) collective-permute-start(f32[32,128]{1,0:T(8,128)S(1)} %add_add_fusion), channel_id=1, source_target_pairs={{0,4},{2,6},{4,0},{6,2},{1,5},{3,7},{5,1},{7,3},{8,12},{10,14},{12... | collective-permute-start | bytes 49160 | tf_op jit(solution)/shard_map/sums_of_taps/ppermute | solution.py:589
  143.0 1.1 collective-permute-start.8
  144.8 3.1 %all-to-all-done.5.back_ref = bf16[16,128,128]{2,1,0:T(8,128)(2,1)S(1)} async-done(((bf16[16,128,128]{2,1,0:T(8,128)(2,1)}), bf16[16,128,128]{2,1,0:T(8,128)(2,1)S(1)}, u32[]{:S(2)}, u32[]{:S(2)}) %all-to-all-start.5) | async-done | bytes 524320 | tf_op jit(solution)/shard_map/channels_to_frames/all_to_all | solution.py:570
  147.9 1.4 join.1
  149.4 0.7 copy.14
  (23 shorter events, 2.6 us)
Async XLA Ops:
  7.2 76.5 %all-gather.6.cloned.1.call-start = ((), (), s32[]{:S(2)}) async-start(), calls=%async_computation.7 | async-start | bytes 6684672 | tf_op jit(solution)/shard_map/cotangent_of_group/all_gather | solution.py:388
  12.3 18.8 %all-to-all-start = ((bf16[16,6,1664]{2,1,0:T(8,128)(2,1)}), bf16[16,6,1664]{2,1,0:T(8,128)(2,1)}, u32[]{:S(2)}, u32[]{:S(2)}) async-start(bf16[16,6,1664]{2,1,0:T(8,128)(2,1)} %get-tuple-element.43), calls=%async_computation | async-start | bytes 851968 | tf_op jit(solution)/shard_map/rows_and_params/all_to_all | solution.py:425
  20.0 8.8 %collective-permute-start = (bf16[16,1536]{1,0:T(8,128)(2,1)}, bf16[16,1536]{1,0:T(8,128)(2,1)}, u32[]{:S(2)}, u32[]{:S(2)}) collective-permute-start(bf16[16,1536]{1,0:T(8,128)(2,1)} %get-tuple-element.41), channel_id=1, source_target_pairs={{1,2},{3,4},{5,6},{7,8},{9,10},{11,12},{13,14},{15,16},{17,18},{19... | collective-permute-start | bytes 147464 | tf_op jit(solution)/shard_map/edge_frames/ppermute | solution.py:422
  31.2 36.8 %all-to-all-start.1 = ((bf16[16,144,128]{2,1,0:T(8,128)(2,1)}), bf16[16,144,128]{2,1,0:T(8,128)(2,1)S(1)}, u32[]{:S(2)}, u32[]{:S(2)}) async-start(bf16[16,144,128]{2,1,0:T(8,128)(2,1)} %split.1), calls=%async_computation.1 | async-start | bytes 1179648 | tf_op jit(solution)/shard_map/frames_to_channels/all_to_all | solution.py:439
  44.0 87.3 %all-gather.4.cloned.1.call-start = ((), (), s32[]{:S(2)}) async-start(), calls=%async_computation.6 | async-start | bytes 5013504 | tf_op jit(solution)/shard_map/weights_of_group/all_gather | solution.py:478
  90.5 1.0 copy-start.1
  91.5 12.1 %all-to-all-start.3 = ((bf16[16,6,1664]{2,1,0:T(8,128)(2,1)}), bf16[16,6,1664]{2,1,0:T(8,128)(2,1)S(1)}, u32[]{:S(2)}, u32[]{:S(2)}) async-start(bf16[16,6,1664]{2,1,0:T(8,128)(2,1)} %get-tuple-element.54), calls=%async_computation.3 | async-start | bytes 851968 | tf_op jit(solution)/shard_map/norm_grad_sums/all_to_all | solution.py:528
  95.0 14.9 %collective-permute-start.1 = (bf16[8,2,16,128]{3,2,1,0:T(8,128)(2,1)S(1)}, bf16[8,2,16,128]{3,2,1,0:T(8,128)(2,1)S(1)}, u32[]{:S(2)}, u32[]{:S(2)}) collective-permute-start(bf16[8,2,16,128]{3,2,1,0:T(8,128)(2,1)S(1)} %get-tuple-element.56), channel_id=1, source_target_pairs={{0,2},{2,4},{4,6},{6,8},{8,10},{10,12},{12,14},{14,16},{16,18},{18... | collective-permute-start | bytes 196616 | tf_op jit(solution)/shard_map/edge_grads/ppermute | solution.py:524
  96.3 13.7 %collective-permute-start.2 = (bf16[8,2,16,128]{3,2,1,0:T(8,128)(2,1)S(1)}, bf16[8,2,16,128]{3,2,1,0:T(8,128)(2,1)S(1)}, u32[]{:S(2)}, u32[]{:S(2)}) collective-permute-start(bf16[8,2,16,128]{3,2,1,0:T(8,128)(2,1)S(1)} %get-tuple-element.57), channel_id=1, source_target_pairs={{2,0},{4,2},{6,4},{8,6},{10,8},{12,10},{14,12},{16,14},{18,16},{20... | collective-permute-start | bytes 196616 | tf_op jit(solution)/shard_map/edge_grads/ppermute | solution.py:525
  103.6 23.1 %all-to-all-start.4 = ((bf16[16,128,128]{2,1,0:T(8,128)(2,1)}), bf16[16,128,128]{2,1,0:T(8,128)(2,1)S(1)}, u32[]{:S(2)}, u32[]{:S(2)}) async-start(bf16[16,128,128]{2,1,0:T(8,128)(2,1)} %get-tuple-element.60), calls=%async_computation.4 | async-start | bytes 1048576 | tf_op jit(solution)/shard_map/act_to_frames/all_to_all | solution.py:532
  110.0 1.2 copy-start.2
  126.7 21.2 %all-to-all-start.5 = ((bf16[16,128,128]{2,1,0:T(8,128)(2,1)}), bf16[16,128,128]{2,1,0:T(8,128)(2,1)S(1)}, u32[]{:S(2)}, u32[]{:S(2)}) async-start(bf16[16,128,128]{2,1,0:T(8,128)(2,1)} %get-tuple-element.69), calls=%async_computation.5 | async-start | bytes 1048576 | tf_op jit(solution)/shard_map/channels_to_frames/all_to_all | solution.py:570
  131.3 9.1 %collective-permute-start.3 = (f32[32,128]{1,0:T(8,128)S(1)}, f32[32,128]{1,0:T(8,128)S(1)}, u32[]{:S(2)}, u32[]{:S(2)}) collective-permute-start(f32[32,128]{1,0:T(8,128)S(1)} %get-tuple-element.61), channel_id=1, source_target_pairs={{0,8},{8,16},{16,24},{24,0},{1,9},{9,17},{17,25},{25,1},{2,10},{10... | collective-permute-start | bytes 49160 | tf_op jit(solution)/shard_map/sums_of_taps/ppermute | solution.py:589
  132.0 8.4 %collective-permute-start.4 = (f32[32,128]{1,0:T(8,128)S(1)}, f32[32,128]{1,0:T(8,128)S(1)}, u32[]{:S(2)}, u32[]{:S(2)}) collective-permute-start(f32[32,128]{1,0:T(8,128)S(1)} %get-tuple-element.61), channel_id=1, source_target_pairs={{0,16},{8,24},{16,0},{24,8},{1,17},{9,25},{17,1},{25,9},{2,18},{10... | collective-permute-start | bytes 49160 | tf_op jit(solution)/shard_map/sums_of_taps/ppermute | solution.py:589
  134.4 6.0 %collective-permute-start.5 = (f32[32,128]{1,0:T(8,128)S(1)}, f32[32,128]{1,0:T(8,128)S(1)}, u32[]{:S(2)}, u32[]{:S(2)}) collective-permute-start(f32[32,128]{1,0:T(8,128)S(1)} %get-tuple-element.61), channel_id=1, source_target_pairs={{0,24},{8,0},{16,8},{24,16},{1,25},{9,1},{17,9},{25,17},{2,26},{10... | collective-permute-start | bytes 49160 | tf_op jit(solution)/shard_map/sums_of_taps/ppermute | solution.py:589
  135.5 2.3 %copy-start = (bf16[1536,1536]{1,0:T(8,128)(2,1)S(1)}, bf16[1536,1536]{1,0:T(8,128)(2,1)}, u32[]{:S(2)}) copy-start(bf16[1536,1536]{1,0:T(8,128)(2,1)} %all-gather.4.cloned.1.call-done.w_ref) | copy-start | bytes 14155780
  140.4 8.9 %collective-permute-start.6 = (f32[32,128]{1,0:T(8,128)S(1)}, f32[32,128]{1,0:T(8,128)S(1)}, u32[]{:S(2)}, u32[]{:S(2)}) collective-permute-start(f32[32,128]{1,0:T(8,128)S(1)} %add_add_fusion), channel_id=1, source_target_pairs={{0,2},{2,4},{4,6},{6,0},{1,3},{3,5},{5,7},{7,1},{8,10},{10,12},{12... | collective-permute-start | bytes 49160 | tf_op jit(solution)/shard_map/sums_of_taps/ppermute | solution.py:589
  140.9 8.5 %collective-permute-start.7 = (f32[32,128]{1,0:T(8,128)S(1)}, f32[32,128]{1,0:T(8,128)S(1)}, u32[]{:S(2)}, u32[]{:S(2)}) collective-permute-start(f32[32,128]{1,0:T(8,128)S(1)} %add_add_fusion), channel_id=1, source_target_pairs={{0,4},{2,6},{4,0},{6,2},{1,5},{3,7},{5,1},{7,3},{8,12},{10,14},{12... | collective-permute-start | bytes 49160 | tf_op jit(solution)/shard_map/sums_of_taps/ppermute | solution.py:589
  143.0 6.3 %collective-permute-start.8 = (f32[32,128]{1,0:T(8,128)S(1)}, f32[32,128]{1,0:T(8,128)S(1)}, u32[]{:S(2)}, u32[]{:S(2)}) collective-permute-start(f32[32,128]{1,0:T(8,128)S(1)} %add_add_fusion), channel_id=1, source_target_pairs={{0,6},{2,0},{4,2},{6,4},{1,7},{3,1},{5,3},{7,5},{8,14},{10,8},{12,... | collective-permute-start | bytes 49160 | tf_op jit(solution)/shard_map/sums_of_taps/ppermute | solution.py:589
Sparse Core Ops, SparseCore 0:
  9.8 63.1 all-gather.5
  75.4 44.5 all-gather.3

commit v5 on v4

--- a/solution.py
+++ b/solution.py
@@ -22,6 +22,7 @@
 CHUNK = 64
 WIDE = D + LANES
 PART = 40
+GA = 48
 MASK_LANE, PREV_LANE, NEXT_LANE = CHAN, CHAN + 1, CHAN + 2
 ALL = ("z", "x", "y", "core")
 IN_GROUP = ("z", "core")
@@ -215,6 +216,29 @@
             stat_ref[d] = run_ref[...]
 
 
+def fold(x):
+    tail = x[CHAN:]
+    lane = lax.broadcasted_iota(jnp.int32, tail.shape, 1)
+    size = LANES - CHAN
+    return jnp.concatenate(
+        [
+            jnp.where(lane < CHAN, x[g * size : (g + 1) * size], pltpu.roll(tail, CHAN - g * size, 1))
+            for g in range(CHAN // size)
+        ],
+        axis=0,
+    )
+
+
+def unfold(x):
+    size = LANES - CHAN
+    lane = lax.broadcasted_iota(jnp.int32, (size, LANES), 1)
+    tail = jnp.zeros((size, LANES), F32)
+    for g in range(CHAN // size):
+        turned = pltpu.roll(x[g * size : (g + 1) * size], (g + 1) * size, 1)
+        tail = jnp.where((lane >= g * size) & (lane < (g + 1) * size), turned, tail)
+    return jnp.concatenate([x, tail], axis=0)
+
+
 def moments(stat_ref):
     each = [stat_ref[d] for d in range(SETS)]
     count = sum(e[0:1] for e in each)
@@ -227,8 +251,14 @@
     return count, mean, inv_std
 
 
+def grad_act_body(cot_ref, wide_ref, out_ref):
+    out_ref[0] = lax.dot_general(
+        cot_ref[...].reshape(BLOCK, D), wide_ref[...], (((1,), (1,)), ((), ())), preferred_element_type=F32
+    )
+
+
 def grad_body(
-    conv_ref, x_ref, wide_ref, par_ref, stat_ref, cot_hbm,
+    conv_ref, x_ref, ga_ref, par_ref, stat_ref, cot_hbm,
     act_ref, gp_ref, first_ref, last_ref, gw_ref,
     total_ref, acc_ref, mom_ref, cot_ref, sem,
 ):
@@ -259,13 +289,11 @@
     pre = scale * normed + shift
     sig = jax.nn.sigmoid(pre)
     act = (m * pre * sig).astype(BF16)
-    act_ref[0] = act[:ROWS]
-    act_ref[1] = act[ROWS:]
+    for half in range(CORES):
+        act_ref[half] = fold(act[half * ROWS : (half + 1) * ROWS].astype(F32)).astype(BF16)
     fetch(step).wait()
     cot = cot_ref[pl.ds(step * CORES, CORES)].reshape(BLOCK, D)
-    grad_act = lax.dot_general(
-        cot, wide_ref[...], (((1,), (1,)), ((), ())), preferred_element_type=F32
-    )
+    grad_act = ga_ref[0]
     gp = m * grad_act * sig * (1.0 + pre * (1.0 - sig))
     nm = m * normed
     gp_ref[0] = gp
@@ -348,7 +376,7 @@
             pieces[core * (ROWS // CHUNK) : (core + 1) * (ROWS // CHUNK)], axis=0
         )
         half = half * m[core * ROWS : (core + 1) * ROWS]
-        pack_ref[core] = half.astype(BF16)
+        pack_ref[core] = fold(half).astype(BF16)
 
     @pl.when(b == Z - 1)
     def _():
@@ -359,7 +387,7 @@
     total = jnp.zeros((ROWS, D), F32)
     for at in range(GROUP):
         total = total + jnp.dot(
-            act_ref[at][:, :CHAN], w_ref[at * CHAN : (at + 1) * CHAN], preferred_element_type=F32
+            unfold(act_ref[at].astype(F32)).astype(BF16)[:, :CHAN], w_ref[at * CHAN : (at + 1) * CHAN], preferred_element_type=F32
         )
     out_ref[...] = total.astype(BF16)
 
@@ -369,7 +397,7 @@
     permute = one_hot()
     for part in range(Z // 2):
         for i in range(4):
-            four_ref[:, i * LANES : (i + 1) * LANES] = back_ref[4 * part + i]
+            four_ref[:, i * LANES : (i + 1) * LANES] = unfold(back_ref[4 * part + i].astype(F32)).astype(BF16)
         gh_ref[:, part * width : (part + 1) * width] = lax.dot_general(
             four_ref[...], permute, (((1,), (1,)), ((), ())), preferred_element_type=F32
         ).astype(BF16)
@@ -480,17 +508,32 @@
     with jax.named_scope("norm_sums"):
         stat = lax.all_to_all(stat, OVER_SETS, 0, 0)
 
+    with jax.named_scope("grad_act"):
+        wide, conv = lax.optimization_barrier((wide, conv))
+        grad_act = call(
+            grad_act_body,
+            shape((Z, BLOCK, LANES), F32),
+            (cot_all, wide),
+            [],
+            "grad_act",
+            limit=GA,
+            work=4 * 10**9,
+            grid=(Z,),
+            in_specs=[each(CORES, ROWS, D), whole(LANES, D)],
+            out_specs=each(1, BLOCK, LANES),
+        )
+
     with jax.named_scope("activation_grad"):
         act, gp, first, last_rows, gw = call(
             grad_body,
             (
-                shape((GROUP, ROWS, LANES), BF16),
+                shape((GROUP, CHAN, LANES), BF16),
                 shape((Z, BLOCK, LANES), F32),
                 shape((Z, 2, HALO, LANES), BF16),
                 shape((Z, 2, HALO, LANES), BF16),
                 shape((SETS, OWN, WIDE), BF16),
             ),
-            (conv, x, wide, par, stat, cot_all),
+            (conv, x, grad_act, par, stat, cot_all),
             [
                 pltpu.VMEM((LANES, D), F32),
                 pltpu.VMEM((2, 8, LANES), F32),
@@ -504,13 +547,13 @@
             in_specs=[
                 pl.BlockSpec((1, BLOCK, LANES), lambda i: (i, 0, 0)),
                 pl.BlockSpec((1, SPAN, LANES), lambda i: (i, 0, 0)),
-                whole(LANES, D),
+                pl.BlockSpec((1, BLOCK, LANES), lambda i: (i, 0, 0)),
                 whole(PART, LANES),
                 whole(SETS, 8, LANES),
                 hbm(),
             ],
             out_specs=[
-                pl.BlockSpec((CORES, ROWS, LANES), lambda i: (i, 0, 0)),
+                pl.BlockSpec((CORES, CHAN, LANES), lambda i: (i, 0, 0)),
                 pl.BlockSpec((1, BLOCK, LANES), lambda i: (i, 0, 0)),
                 pl.BlockSpec((1, 2, HALO, LANES), lambda i: (i, 0, 0, 0)),
                 pl.BlockSpec((1, 2, HALO, LANES), lambda i: (i, 0, 0, 0)),
@@ -535,7 +578,7 @@
         pack, taps, both = call(
             back_body,
             (
-                shape((GROUP, ROWS, LANES), BF16),
+                shape((GROUP, CHAN, LANES), BF16),
                 shape((32, LANES), F32),
                 shape((8, LANES), F32),
             ),
@@ -563,7 +606,7 @@
                 whole(Z, 2, HALO, LANES),
                 whole(Z, 2, HALO, LANES),
             ],
-            out_specs=[each(CORES, ROWS, LANES), whole(32, LANES), whole(8, LANES)],
+            out_specs=[each(CORES, CHAN, LANES), whole(32, LANES), whole(8, LANES)],
         )
 
     with jax.named_scope("channels_to_frames"):

time: 158 us -> 156 us (0.987)
  blocking collectives: 10.3 us -> 0 us
  Pallas kernels: 32.1 us -> 39.2 us
  starting transfers between devices: 51.6 us -> 56 us
  waiting for transfers between devices: 40.9 us -> 37.3 us
    all_to_all x1 -> x0, blocking collectives: 10.3 us -> none  [local(): stat = lax.all_to_all(stat, OVER_SETS, 0, 0)]
    pallas_call x8 -> x9, Pallas kernels: 32.1 us -> 39.2 us  [call(): pl.pallas_call(body, out_shape=outs, name=name, compiler_params=pltpu.Com...]
    all_to_all x0 -> x1, starting transfers between devices: none -> 3.97 us  [local(): stat = lax.all_to_all(stat, OVER_SETS, 0, 0)]
    all_to_all x1, starting transfers between devices: 3.56 us -> 6.64 us  [local(): gw = lax.all_to_all(gw, OVER_SETS, 0, 0)]
    all_to_all x1, waiting for transfers between devices: 6.91 us -> 4.33 us  [local(): act = lax.all_to_all(act, IN_GROUP, 0, 0)]
    all_to_all x1, waiting for transfers between devices: 3.14 us -> 1.31 us  [local(): back = lax.all_to_all(pack, IN_GROUP, 0, 0)]
  transfers between devices with their start and end apart: 16 -> 17, of which waited for: 5 -> 5; matrix products, arithmetic and copies ran while one was open for 2% -> 2% of each run, Pallas kernels for 20% -> 25%
where the time goes in v5:
time: 156 us; the launch traced here: 155 us
  starting transfers between devices  56 us (36%)
  Pallas kernels  39.2 us (25%)
  waiting for transfers between devices  37.3 us (24%)
  between operations  14.2 us (9%)
  local copies, waits for them, and re-layouts  7.14 us (5%)
    pallas_call x9, Pallas kernels, call(): pl.pallas_call(body, out_shape=outs, name=name, compiler_params=pltpu.Com...  39.2 us
    all_to_all x1, waiting for transfers between devices, local(): x = lax.all_to_all(frames, IN_GROUP, 0, 0).reshape(Z, SPAN, LANES)  22 us
    all_to_all x1, starting transfers between devices, local(): x = lax.all_to_all(frames, IN_GROUP, 0, 0).reshape(Z, SPAN, LANES)  12.8 us
    all_to_all x1, starting transfers between devices, local(): wp = lax.all_to_all(wp, OVER_SETS, 0, 0)  7.64 us
    all_to_all x1, starting transfers between devices, local(): gw = lax.all_to_all(gw, OVER_SETS, 0, 0)  6.64 us
    ppermute x6, starting transfers between devices, local(): lax.ppermute(taps, axis, [(i, (i + by) % size) for i in range(size)])  6.51 us
    all_to_all x1, starting transfers between devices, local(): act = lax.all_to_all(act, IN_GROUP, 0, 0)  5.62 us
    unnamed x7, local copies, waits for them, and re-layouts  5.21 us
  transfers between devices with their start and end apart: 17, of which 5 were waited for; matrix products, arithmetic and copies ran while one was open for 2% of the time, Pallas kernels for 25%

profile of v5, /device:TPU:1, one launch (start us, length us, event | category | flops | bytes accessed | tf_op | source)
XLA Modules:
  0.0 154.7 jit_solution(8688735275581625850)
XLA Ops:
  7.9 1.4 pad_dynamic-slice_fusion
  9.3 3.1 %prepare.1 = (bf16[16,6,1664]{2,1,0:T(8,128)(2,1)}, f32[128,128]{1,0:T(8,128)}, bf16[128,1536]{1,0:T(8,128)(2,1)}, bf16[16,1536]{1,0:T(8,128)(2,1)}) custom-call(s32[1]{0:T(128)} %bitcast.1.core_ref, s32[1,256]{1,0:T(1,128)} %bitcast.19, f32[6,31]{1,0:T(8,128)} %bitcast.18, f32[1,6]{1,0:T(1,128)} %bitcast.20, f32[1,6]{1,0:T(1,128)} %bitcast.21, ...), custom_call_target="tpu_custom_call" | custom-call | tf_op jit(solution)/shard_map/prepare/prepare/pallas_call | solution.py:38
  12.3 7.6 %all-to-all-start = ((bf16[16,6,1664]{2,1,0:T(8,128)(2,1)}), bf16[16,6,1664]{2,1,0:T(8,128)(2,1)}, u32[]{:S(2)}, u32[]{:S(2)}) async-start(bf16[16,6,1664]{2,1,0:T(8,128)(2,1)} %get-tuple-element.45), calls=%async_computation | async-start | bytes 851968 | tf_op jit(solution)/shard_map/rows_and_params/all_to_all | solution.py:453
  20.0 4.3 %collective-permute-start = (bf16[16,1536]{1,0:T(8,128)(2,1)}, bf16[16,1536]{1,0:T(8,128)(2,1)}, u32[]{:S(2)}, u32[]{:S(2)}) collective-permute-start(bf16[16,1536]{1,0:T(8,128)(2,1)} %get-tuple-element.43), channel_id=1, source_target_pairs={{1,2},{3,4},{5,6},{7,8},{9,10},{11,12},{13,14},{15,16},{17,18},{19... | collective-permute-start | bytes 147464 | tf_op jit(solution)/shard_map/edge_frames/ppermute | solution.py:450
  24.3 4.4 %collective-permute-done.halo_ref = bf16[16,1536]{1,0:T(8,128)(2,1)} collective-permute-done((bf16[16,1536]{1,0:T(8,128)(2,1)}, bf16[16,1536]{1,0:T(8,128)(2,1)}, u32[]{:S(2)}, u32[]{:S(2)}) %collective-permute-start) | collective-permute-done | bytes 49184 | tf_op jit(solution)/shard_map/edge_frames/ppermute | solution.py:450
  28.7 2.4 %split.1 = bf16[16,144,128]{2,1,0:T(8,128)(2,1)} custom-call(s32[1]{0:T(128)} %bitcast.1.core_ref, bf16[128,1536]{1,0:T(8,128)(2,1)} %get-tuple-element.42.own_ref, bf16[16,1536]{1,0:T(8,128)(2,1)} %collective-permute-done.halo_ref, f32[128,128]{1,0:T(8,128)} %get-tuple-element.44.ext_ref), custom_call_target="tpu_custom_call" | custom-call | tf_op jit(solution)/shard_map/frames_to_channels/split/pallas_call | solution.py:38
  31.2 12.8 %all-to-all-start.1 = ((bf16[16,144,128]{2,1,0:T(8,128)(2,1)}), bf16[16,144,128]{2,1,0:T(8,128)(2,1)S(1)}, u32[]{:S(2)}, u32[]{:S(2)}) async-start(bf16[16,144,128]{2,1,0:T(8,128)(2,1)} %split.1), calls=%async_computation.1 | async-start | bytes 1179648 | tf_op jit(solution)/shard_map/frames_to_channels/all_to_all | solution.py:467
  44.1 1.9 %rows.1 = (f32[40,128]{1,0:T(8,128)S(1)}, bf16[96,1536]{1,0:T(8,128)(2,1)}, bf16[128,1536]{1,0:T(8,128)(2,1)S(1)}) custom-call(bf16[16,6,1664]{2,1,0:T(8,128)(2,1)} %all-to-all-done.wp_ref), custom_call_target="tpu_custom_call" | custom-call | flops 2000000000 | bytes 1048576 | tf_op jit(solution)/shard_map/unpack_rows/rows/pallas_call | solution.py:38
  45.9 22.0 %all-to-all-done.1 = bf16[16,144,128]{2,1,0:T(8,128)(2,1)S(1)} async-done(((bf16[16,144,128]{2,1,0:T(8,128)(2,1)}), bf16[16,144,128]{2,1,0:T(8,128)(2,1)S(1)}, u32[]{:S(2)}, u32[]{:S(2)}) %all-to-all-start.1) | async-done | bytes 589856 | tf_op jit(solution)/shard_map/frames_to_channels/all_to_all | solution.py:467
  67.9 6.0 %conv.1 = (f32[8,256,128]{2,1,0:T(8,128)S(1)}, f32[16,8,128]{2,1,0:T(8,128)}) custom-call(bf16[8,288,128]{2,1,0:T(8,128)(2,1)S(1)} %bitcast.13, f32[40,128]{1,0:T(8,128)S(1)} %get-tuple-element.50.par_ref), custom_call_target="tpu_custom_call" | custom-call | flops 6000000000 | bytes 1048576 | tf_op jit(solution)/shard_map/conv/conv/pallas_call | solution.py:38
  74.0 4.0 %all-to-all-start.2 = ((f32[16,8,128]{2,1,0:T(8,128)}), f32[16,8,128]{2,1,0:T(8,128)S(1)}, u32[]{:S(2)}, u32[]{:S(2)}) async-start(f32[16,8,128]{2,1,0:T(8,128)} %get-tuple-element.55), calls=%async_computation.2 | async-start | bytes 131072 | tf_op jit(solution)/shard_map/norm_sums/all_to_all | solution.py:509
  78.0 6.6 %grad_act.1.ga_ref = f32[8,256,128]{2,1,0:T(8,128)S(1)} custom-call(bf16[16,128,1536]{2,1,0:T(8,128)(2,1)} %bitcast.16, bf16[128,1536]{1,0:T(8,128)(2,1)S(1)} %get-tuple-element.54.wide_ref), custom_call_target="tpu_custom_call" | custom-call | flops 4000000000 | bytes 1048576 | tf_op jit(solution)/shard_map/grad_act/grad_act/pallas_call | solution.py:38
  84.6 6.4 %activation.1 = (bf16[16,96,128]{2,1,0:T(8,128)(2,1)}, f32[8,256,128]{2,1,0:T(8,128)S(1)}, bf16[8,2,16,128]{3,2,1,0:T(8,128)(2,1)S(1)}, bf16[8,2,16,128]{3,2,1,0:T(8,128)(2,1)S(1)}, bf16[16,6,1664]{2,1,0:T(8,128)(2,1)}) custom-call(f32[8,256,128]{2,1,0:T(8,128)S(1)} %get-tuple-element.53.conv_ref, bf16[8,288,128]{2,1,0:T(8,128)(2,1)S(1)} %bitcast.14, ...), custom_call_target="tpu_custom_call" | custom-call | tf_op jit(solution)/shard_map/activation_grad/activation/pallas_call | solution.py:38
  91.0 1.0 copy-done.1
  92.0 6.6 %all-to-all-start.3 = ((bf16[16,6,1664]{2,1,0:T(8,128)(2,1)}), bf16[16,6,1664]{2,1,0:T(8,128)(2,1)S(1)}, u32[]{:S(2)}, u32[]{:S(2)}) async-start(bf16[16,6,1664]{2,1,0:T(8,128)(2,1)} %get-tuple-element.58), calls=%async_computation.3 | async-start | bytes 851968 | tf_op jit(solution)/shard_map/norm_grad_sums/all_to_all | solution.py:571
  98.6 1.4 collective-permute-start.1
  100.0 3.5 %collective-permute-start.2 = (bf16[8,2,16,128]{3,2,1,0:T(8,128)(2,1)S(1)}, bf16[8,2,16,128]{3,2,1,0:T(8,128)(2,1)S(1)}, u32[]{:S(2)}, u32[]{:S(2)}) collective-permute-start(bf16[8,2,16,128]{3,2,1,0:T(8,128)(2,1)S(1)} %get-tuple-element.61), channel_id=1, source_target_pairs={{2,0},{4,2},{6,4},{8,6},{10,8},{12,10},{14,12},{16,14},{18,16},{20... | collective-permute-start | bytes 196616 | tf_op jit(solution)/shard_map/edge_grads/ppermute | solution.py:568
  103.5 4.5 %all-to-all-done.3.sum_ref = bf16[16,6,1664]{2,1,0:T(8,128)(2,1)S(1)} async-done(((bf16[16,6,1664]{2,1,0:T(8,128)(2,1)}), bf16[16,6,1664]{2,1,0:T(8,128)(2,1)S(1)}, u32[]{:S(2)}, u32[]{:S(2)}) %all-to-all-start.3) | async-done | bytes 319520 | tf_op jit(solution)/shard_map/norm_grad_sums/all_to_all | solution.py:571
  108.0 5.6 %all-to-all-start.4 = ((bf16[16,96,128]{2,1,0:T(8,128)(2,1)}), bf16[16,96,128]{2,1,0:T(8,128)(2,1)S(1)}, u32[]{:S(2)}, u32[]{:S(2)}) async-start(bf16[16,96,128]{2,1,0:T(8,128)(2,1)} %get-tuple-element.64), calls=%async_computation.4 | async-start | bytes 786432 | tf_op jit(solution)/shard_map/act_to_frames/all_to_all | solution.py:575
  113.6 1.2 copy-done.2
  114.8 9.0 %conv_grad.1 = (bf16[16,96,128]{2,1,0:T(8,128)(2,1)}, f32[32,128]{1,0:T(8,128)S(1)}, f32[8,128]{1,0:T(8,128)S(1)}) custom-call(s32[1]{0:T(128)} %bitcast.set_ref, f32[8,256,128]{2,1,0:T(8,128)S(1)} %copy-done.2, f32[8,256,128]{2,1,0:T(8,128)S(1)} %get-tuple-element.53.conv_ref, bf16[8,288,128]{2,1,0:T(8,128)(2,1)S(1)} %bitcast.15, ...), custom_call_target="tpu_custom_call" | custom-call | flops 10000000000 | bytes 1048576 | tf_op jit(solution)/shard_map/conv_grad/conv_grad/pallas_call | solution.py:38
  123.8 4.3 %all-to-all-done.4.act_ref = bf16[16,96,128]{2,1,0:T(8,128)(2,1)S(1)} async-done(((bf16[16,96,128]{2,1,0:T(8,128)(2,1)}), bf16[16,96,128]{2,1,0:T(8,128)(2,1)S(1)}, u32[]{:S(2)}, u32[]{:S(2)}) %all-to-all-start.4) | async-done | bytes 393248 | tf_op jit(solution)/shard_map/act_to_frames/all_to_all | solution.py:575
  128.1 3.4 %all-to-all-start.5 = ((bf16[16,96,128]{2,1,0:T(8,128)(2,1)}), bf16[16,96,128]{2,1,0:T(8,128)(2,1)S(1)}, u32[]{:S(2)}, u32[]{:S(2)}) async-start(bf16[16,96,128]{2,1,0:T(8,128)(2,1)} %get-tuple-element.73), calls=%async_computation.5 | async-start | bytes 786432 | tf_op jit(solution)/shard_map/channels_to_frames/all_to_all | solution.py:613
  131.6 0.7 convert_reduce_fusion
  132.8 1.2 collective-permute-start.4
  134.0 2.0 %collective-permute-start.5 = (f32[32,128]{1,0:T(8,128)S(1)}, f32[32,128]{1,0:T(8,128)S(1)}, u32[]{:S(2)}, u32[]{:S(2)}) collective-permute-start(f32[32,128]{1,0:T(8,128)S(1)} %get-tuple-element.65), channel_id=1, source_target_pairs={{0,24},{8,0},{16,8},{24,16},{1,25},{9,1},{17,9},{25,17},{2,26},{10... | collective-permute-start | bytes 49160 | tf_op jit(solution)/shard_map/sums_of_taps/ppermute | solution.py:632
  136.1 2.3 %copy-done = bf16[1536,1536]{1,0:T(8,128)(2,1)S(1)} copy-done((bf16[1536,1536]{1,0:T(8,128)(2,1)S(1)}, bf16[1536,1536]{1,0:T(8,128)(2,1)}, u32[]{:S(2)}) %copy-start) | copy-done | bytes 4718616
  138.4 2.5 %module_out.1 = bf16[128,1536]{1,0:T(8,128)(2,1)} custom-call(bf16[16,96,128]{2,1,0:T(8,128)(2,1)S(1)} %all-to-all-done.4.act_ref, bf16[1536,1536]{1,0:T(8,128)(2,1)S(1)} %copy-done), custom_call_target="tpu_custom_call" | custom-call | flops 4000000000 | bytes 1048576 | tf_op jit(solution)/shard_map/module_out/module_out/pallas_call | solution.py:38
  141.1 1.3 collective-permute-start.7
  142.4 1.3 collective-permute-start.8
  144.3 1.3 all-to-all-done.5.back_ref
  145.6 1.4 join.1
  (25 shorter events, 2.8 us)
Async XLA Ops:
  7.2 70.8 %all-gather.6.cloned.1.call-start = ((), (), s32[]{:S(2)}) async-start(), calls=%async_computation.7 | async-start | bytes 6684672 | tf_op jit(solution)/shard_map/cotangent_of_group/all_gather | solution.py:416
  12.3 18.8 %all-to-all-start = ((bf16[16,6,1664]{2,1,0:T(8,128)(2,1)}), bf16[16,6,1664]{2,1,0:T(8,128)(2,1)}, u32[]{:S(2)}, u32[]{:S(2)}) async-start(bf16[16,6,1664]{2,1,0:T(8,128)(2,1)} %get-tuple-element.45), calls=%async_computation | async-start | bytes 851968 | tf_op jit(solution)/shard_map/rows_and_params/all_to_all | solution.py:453
  20.0 8.8 %collective-permute-start = (bf16[16,1536]{1,0:T(8,128)(2,1)}, bf16[16,1536]{1,0:T(8,128)(2,1)}, u32[]{:S(2)}, u32[]{:S(2)}) collective-permute-start(bf16[16,1536]{1,0:T(8,128)(2,1)} %get-tuple-element.43), channel_id=1, source_target_pairs={{1,2},{3,4},{5,6},{7,8},{9,10},{11,12},{13,14},{15,16},{17,18},{19... | collective-permute-start | bytes 147464 | tf_op jit(solution)/shard_map/edge_frames/ppermute | solution.py:450
  31.2 36.8 %all-to-all-start.1 = ((bf16[16,144,128]{2,1,0:T(8,128)(2,1)}), bf16[16,144,128]{2,1,0:T(8,128)(2,1)S(1)}, u32[]{:S(2)}, u32[]{:S(2)}) async-start(bf16[16,144,128]{2,1,0:T(8,128)(2,1)} %split.1), calls=%async_computation.1 | async-start | bytes 1179648 | tf_op jit(solution)/shard_map/frames_to_channels/all_to_all | solution.py:467
  44.0 88.3 %all-gather.4.cloned.1.call-start = ((), (), s32[]{:S(2)}) async-start(), calls=%async_computation.6 | async-start | bytes 5013504 | tf_op jit(solution)/shard_map/weights_of_group/all_gather | solution.py:506
  74.0 10.6 %all-to-all-start.2 = ((f32[16,8,128]{2,1,0:T(8,128)}), f32[16,8,128]{2,1,0:T(8,128)S(1)}, u32[]{:S(2)}, u32[]{:S(2)}) async-start(f32[16,8,128]{2,1,0:T(8,128)} %get-tuple-element.55), calls=%async_computation.2 | async-start | bytes 131072 | tf_op jit(solution)/shard_map/norm_sums/all_to_all | solution.py:509
  91.0 1.0 copy-start.1
  92.0 16.0 %all-to-all-start.3 = ((bf16[16,6,1664]{2,1,0:T(8,128)(2,1)}), bf16[16,6,1664]{2,1,0:T(8,128)(2,1)S(1)}, u32[]{:S(2)}, u32[]{:S(2)}) async-start(bf16[16,6,1664]{2,1,0:T(8,128)(2,1)} %get-tuple-element.58), calls=%async_computation.3 | async-start | bytes 851968 | tf_op jit(solution)/shard_map/norm_grad_sums/all_to_all | solution.py:571
  98.6 15.0 %collective-permute-start.1 = (bf16[8,2,16,128]{3,2,1,0:T(8,128)(2,1)S(1)}, bf16[8,2,16,128]{3,2,1,0:T(8,128)(2,1)S(1)}, u32[]{:S(2)}, u32[]{:S(2)}) collective-permute-start(bf16[8,2,16,128]{3,2,1,0:T(8,128)(2,1)S(1)} %get-tuple-element.60), channel_id=1, source_target_pairs={{0,2},{2,4},{4,6},{6,8},{8,10},{10,12},{12,14},{14,16},{16,18},{18... | collective-permute-start | bytes 196616 | tf_op jit(solution)/shard_map/edge_grads/ppermute | solution.py:567
  100.0 13.6 %collective-permute-start.2 = (bf16[8,2,16,128]{3,2,1,0:T(8,128)(2,1)S(1)}, bf16[8,2,16,128]{3,2,1,0:T(8,128)(2,1)S(1)}, u32[]{:S(2)}, u32[]{:S(2)}) collective-permute-start(bf16[8,2,16,128]{3,2,1,0:T(8,128)(2,1)S(1)} %get-tuple-element.61), channel_id=1, source_target_pairs={{2,0},{4,2},{6,4},{8,6},{10,8},{12,10},{14,12},{16,14},{18,16},{20... | collective-permute-start | bytes 196616 | tf_op jit(solution)/shard_map/edge_grads/ppermute | solution.py:568
  108.0 20.2 %all-to-all-start.4 = ((bf16[16,96,128]{2,1,0:T(8,128)(2,1)}), bf16[16,96,128]{2,1,0:T(8,128)(2,1)S(1)}, u32[]{:S(2)}, u32[]{:S(2)}) async-start(bf16[16,96,128]{2,1,0:T(8,128)(2,1)} %get-tuple-element.64), calls=%async_computation.4 | async-start | bytes 786432 | tf_op jit(solution)/shard_map/act_to_frames/all_to_all | solution.py:575
  113.6 1.2 copy-start.2
  128.1 17.5 %all-to-all-start.5 = ((bf16[16,96,128]{2,1,0:T(8,128)(2,1)}), bf16[16,96,128]{2,1,0:T(8,128)(2,1)S(1)}, u32[]{:S(2)}, u32[]{:S(2)}) async-start(bf16[16,96,128]{2,1,0:T(8,128)(2,1)} %get-tuple-element.73), calls=%async_computation.5 | async-start | bytes 786432 | tf_op jit(solution)/shard_map/channels_to_frames/all_to_all | solution.py:613
  132.3 8.6 %collective-permute-start.3 = (f32[32,128]{1,0:T(8,128)S(1)}, f32[32,128]{1,0:T(8,128)S(1)}, u32[]{:S(2)}, u32[]{:S(2)}) collective-permute-start(f32[32,128]{1,0:T(8,128)S(1)} %get-tuple-element.65), channel_id=1, source_target_pairs={{0,8},{8,16},{16,24},{24,0},{1,9},{9,17},{17,25},{25,1},{2,10},{10... | collective-permute-start | bytes 49160 | tf_op jit(solution)/shard_map/sums_of_taps/ppermute | solution.py:632
  132.8 8.2 %collective-permute-start.4 = (f32[32,128]{1,0:T(8,128)S(1)}, f32[32,128]{1,0:T(8,128)S(1)}, u32[]{:S(2)}, u32[]{:S(2)}) collective-permute-start(f32[32,128]{1,0:T(8,128)S(1)} %get-tuple-element.65), channel_id=1, source_target_pairs={{0,16},{8,24},{16,0},{24,8},{1,17},{9,25},{17,1},{25,9},{2,18},{10... | collective-permute-start | bytes 49160 | tf_op jit(solution)/shard_map/sums_of_taps/ppermute | solution.py:632
  134.0 6.9 %collective-permute-start.5 = (f32[32,128]{1,0:T(8,128)S(1)}, f32[32,128]{1,0:T(8,128)S(1)}, u32[]{:S(2)}, u32[]{:S(2)}) collective-permute-start(f32[32,128]{1,0:T(8,128)S(1)} %get-tuple-element.65), channel_id=1, source_target_pairs={{0,24},{8,0},{16,8},{24,16},{1,25},{9,1},{17,9},{25,17},{2,26},{10... | collective-permute-start | bytes 49160 | tf_op jit(solution)/shard_map/sums_of_taps/ppermute | solution.py:632
  136.1 2.3 %copy-start = (bf16[1536,1536]{1,0:T(8,128)(2,1)S(1)}, bf16[1536,1536]{1,0:T(8,128)(2,1)}, u32[]{:S(2)}) copy-start(bf16[1536,1536]{1,0:T(8,128)(2,1)} %all-gather.4.cloned.1.call-done.w_ref) | copy-start | bytes 14155780
  141.0 6.1 %collective-permute-start.6 = (f32[32,128]{1,0:T(8,128)S(1)}, f32[32,128]{1,0:T(8,128)S(1)}, u32[]{:S(2)}, u32[]{:S(2)}) collective-permute-start(f32[32,128]{1,0:T(8,128)S(1)} %add_add_fusion), channel_id=1, source_target_pairs={{0,2},{2,4},{4,6},{6,0},{1,3},{3,5},{5,7},{7,1},{8,10},{10,12},{12... | collective-permute-start | bytes 49160 | tf_op jit(solution)/shard_map/sums_of_taps/ppermute | solution.py:632
  141.1 5.9 %collective-permute-start.7 = (f32[32,128]{1,0:T(8,128)S(1)}, f32[32,128]{1,0:T(8,128)S(1)}, u32[]{:S(2)}, u32[]{:S(2)}) collective-permute-start(f32[32,128]{1,0:T(8,128)S(1)} %add_add_fusion), channel_id=1, source_target_pairs={{0,4},{2,6},{4,0},{6,2},{1,5},{3,7},{5,1},{7,3},{8,12},{10,14},{12... | collective-permute-start | bytes 49160 | tf_op jit(solution)/shard_map/sums_of_taps/ppermute | solution.py:632
  142.4 4.6 %collective-permute-start.8 = (f32[32,128]{1,0:T(8,128)S(1)}, f32[32,128]{1,0:T(8,128)S(1)}, u32[]{:S(2)}, u32[]{:S(2)}) collective-permute-start(f32[32,128]{1,0:T(8,128)S(1)} %add_add_fusion), channel_id=1, source_target_pairs={{0,6},{2,0},{4,2},{6,4},{1,7},{3,1},{5,3},{7,5},{8,14},{10,8},{12,... | collective-permute-start | bytes 49160 | tf_op jit(solution)/shard_map/sums_of_taps/ppermute | solution.py:632
Sparse Core Ops, SparseCore 0:
  9.8 63.1 all-gather.5
  75.4 41.1 all-gather.3

commit v6 on v5

--- a/solution.py
+++ b/solution.py
@@ -19,7 +19,7 @@
 BLOCK = CORES * ROWS
 SPAN = BLOCK + 2 * HALO
 SENT = ROWS + HALO
-CHUNK = 64
+CHUNK = 32
 WIDE = D + LANES
 PART = 40
 GA = 48

time: 156 us -> 156 us (level)
  no operation moved by 1% of the time
where the time goes in v6:
time: 156 us; the launch traced here: 155 us
  starting transfers between devices  55.9 us (36%)
  Pallas kernels  39.2 us (25%)
  waiting for transfers between devices  37.5 us (24%)
  between operations  14.2 us (9%)
  local copies, waits for them, and re-layouts  7.14 us (5%)
    pallas_call x9, Pallas kernels, call(): pl.pallas_call(body, out_shape=outs, name=name, compiler_params=pltpu.Com...  39.2 us
    all_to_all x1, waiting for transfers between devices, local(): x = lax.all_to_all(frames, IN_GROUP, 0, 0).reshape(Z, SPAN, LANES)  22 us
    all_to_all x1, starting transfers between devices, local(): x = lax.all_to_all(frames, IN_GROUP, 0, 0).reshape(Z, SPAN, LANES)  12.8 us
    all_to_all x1, starting transfers between devices, local(): wp = lax.all_to_all(wp, OVER_SETS, 0, 0)  7.64 us
    all_to_all x1, starting transfers between devices, local(): gw = lax.all_to_all(gw, OVER_SETS, 0, 0)  6.65 us
    ppermute x6, starting transfers between devices, local(): lax.ppermute(taps, axis, [(i, (i + by) % size) for i in range(size)])  6.52 us
    all_to_all x1, starting transfers between devices, local(): act = lax.all_to_all(act, IN_GROUP, 0, 0)  5.55 us
    unnamed x7, local copies, waits for them, and re-layouts  5.21 us
  transfers between devices with their start and end apart: 17, of which 5 were waited for; matrix products, arithmetic and copies ran while one was open for 2% of the time, Pallas kernels for 25%

profile of v6, /device:TPU:1, one launch (start us, length us, event | category | flops | bytes accessed | tf_op | source)
XLA Modules:
  0.0 154.7 jit_solution(3451313234278501101)
XLA Ops:
  7.9 1.4 pad_dynamic-slice_fusion
  9.3 3.1 %prepare.1 = (bf16[16,6,1664]{2,1,0:T(8,128)(2,1)}, f32[128,128]{1,0:T(8,128)}, bf16[128,1536]{1,0:T(8,128)(2,1)}, bf16[16,1536]{1,0:T(8,128)(2,1)}) custom-call(s32[1]{0:T(128)} %bitcast.1.core_ref, s32[1,256]{1,0:T(1,128)} %bitcast.19, f32[6,31]{1,0:T(8,128)} %bitcast.18, f32[1,6]{1,0:T(1,128)} %bitcast.20, f32[1,6]{1,0:T(1,128)} %bitcast.21, ...), custom_call_target="tpu_custom_call" | custom-call | tf_op jit(solution)/shard_map/prepare/prepare/pallas_call | solution.py:38
  12.3 7.6 %all-to-all-start = ((bf16[16,6,1664]{2,1,0:T(8,128)(2,1)}), bf16[16,6,1664]{2,1,0:T(8,128)(2,1)}, u32[]{:S(2)}, u32[]{:S(2)}) async-start(bf16[16,6,1664]{2,1,0:T(8,128)(2,1)} %get-tuple-element.45), calls=%async_computation | async-start | bytes 851968 | tf_op jit(solution)/shard_map/rows_and_params/all_to_all | solution.py:453
  20.0 4.3 %collective-permute-start = (bf16[16,1536]{1,0:T(8,128)(2,1)}, bf16[16,1536]{1,0:T(8,128)(2,1)}, u32[]{:S(2)}, u32[]{:S(2)}) collective-permute-start(bf16[16,1536]{1,0:T(8,128)(2,1)} %get-tuple-element.43), channel_id=1, source_target_pairs={{1,2},{3,4},{5,6},{7,8},{9,10},{11,12},{13,14},{15,16},{17,18},{19... | collective-permute-start | bytes 147464 | tf_op jit(solution)/shard_map/edge_frames/ppermute | solution.py:450
  24.3 4.4 %collective-permute-done.halo_ref = bf16[16,1536]{1,0:T(8,128)(2,1)} collective-permute-done((bf16[16,1536]{1,0:T(8,128)(2,1)}, bf16[16,1536]{1,0:T(8,128)(2,1)}, u32[]{:S(2)}, u32[]{:S(2)}) %collective-permute-start) | collective-permute-done | bytes 49184 | tf_op jit(solution)/shard_map/edge_frames/ppermute | solution.py:450
  28.7 2.4 %split.1 = bf16[16,144,128]{2,1,0:T(8,128)(2,1)} custom-call(s32[1]{0:T(128)} %bitcast.1.core_ref, bf16[128,1536]{1,0:T(8,128)(2,1)} %get-tuple-element.42.own_ref, bf16[16,1536]{1,0:T(8,128)(2,1)} %collective-permute-done.halo_ref, f32[128,128]{1,0:T(8,128)} %get-tuple-element.44.ext_ref), custom_call_target="tpu_custom_call" | custom-call | tf_op jit(solution)/shard_map/frames_to_channels/split/pallas_call | solution.py:38
  31.2 12.8 %all-to-all-start.1 = ((bf16[16,144,128]{2,1,0:T(8,128)(2,1)}), bf16[16,144,128]{2,1,0:T(8,128)(2,1)S(1)}, u32[]{:S(2)}, u32[]{:S(2)}) async-start(bf16[16,144,128]{2,1,0:T(8,128)(2,1)} %split.1), calls=%async_computation.1 | async-start | bytes 1179648 | tf_op jit(solution)/shard_map/frames_to_channels/all_to_all | solution.py:467
  44.1 1.9 %rows.1 = (f32[40,128]{1,0:T(8,128)S(1)}, bf16[96,1536]{1,0:T(8,128)(2,1)}, bf16[128,1536]{1,0:T(8,128)(2,1)S(1)}) custom-call(bf16[16,6,1664]{2,1,0:T(8,128)(2,1)} %all-to-all-done.wp_ref), custom_call_target="tpu_custom_call" | custom-call | flops 2000000000 | bytes 1048576 | tf_op jit(solution)/shard_map/unpack_rows/rows/pallas_call | solution.py:38
  45.9 22.0 %all-to-all-done.1 = bf16[16,144,128]{2,1,0:T(8,128)(2,1)S(1)} async-done(((bf16[16,144,128]{2,1,0:T(8,128)(2,1)}), bf16[16,144,128]{2,1,0:T(8,128)(2,1)S(1)}, u32[]{:S(2)}, u32[]{:S(2)}) %all-to-all-start.1) | async-done | bytes 589856 | tf_op jit(solution)/shard_map/frames_to_channels/all_to_all | solution.py:467
  67.9 6.1 %conv.1 = (f32[8,256,128]{2,1,0:T(8,128)S(1)}, f32[16,8,128]{2,1,0:T(8,128)}) custom-call(bf16[8,288,128]{2,1,0:T(8,128)(2,1)S(1)} %bitcast.13, f32[40,128]{1,0:T(8,128)S(1)} %get-tuple-element.50.par_ref), custom_call_target="tpu_custom_call" | custom-call | flops 6000000000 | bytes 1048576 | tf_op jit(solution)/shard_map/conv/conv/pallas_call | solution.py:38
  74.0 4.0 %all-to-all-start.2 = ((f32[16,8,128]{2,1,0:T(8,128)}), f32[16,8,128]{2,1,0:T(8,128)S(1)}, u32[]{:S(2)}, u32[]{:S(2)}) async-start(f32[16,8,128]{2,1,0:T(8,128)} %get-tuple-element.55), calls=%async_computation.2 | async-start | bytes 131072 | tf_op jit(solution)/shard_map/norm_sums/all_to_all | solution.py:509
  78.0 6.6 %grad_act.1.ga_ref = f32[8,256,128]{2,1,0:T(8,128)S(1)} custom-call(bf16[16,128,1536]{2,1,0:T(8,128)(2,1)} %bitcast.16, bf16[128,1536]{1,0:T(8,128)(2,1)S(1)} %get-tuple-element.54.wide_ref), custom_call_target="tpu_custom_call" | custom-call | flops 4000000000 | bytes 1048576 | tf_op jit(solution)/shard_map/grad_act/grad_act/pallas_call | solution.py:38
  84.6 6.4 %activation.1 = (bf16[16,96,128]{2,1,0:T(8,128)(2,1)}, f32[8,256,128]{2,1,0:T(8,128)S(1)}, bf16[8,2,16,128]{3,2,1,0:T(8,128)(2,1)S(1)}, bf16[8,2,16,128]{3,2,1,0:T(8,128)(2,1)S(1)}, bf16[16,6,1664]{2,1,0:T(8,128)(2,1)}) custom-call(f32[8,256,128]{2,1,0:T(8,128)S(1)} %get-tuple-element.53.conv_ref, bf16[8,288,128]{2,1,0:T(8,128)(2,1)S(1)} %bitcast.14, ...), custom_call_target="tpu_custom_call" | custom-call | tf_op jit(solution)/shard_map/activation_grad/activation/pallas_call | solution.py:38
  91.0 1.0 copy-done.1
  92.0 6.7 %all-to-all-start.3 = ((bf16[16,6,1664]{2,1,0:T(8,128)(2,1)}), bf16[16,6,1664]{2,1,0:T(8,128)(2,1)S(1)}, u32[]{:S(2)}, u32[]{:S(2)}) async-start(bf16[16,6,1664]{2,1,0:T(8,128)(2,1)} %get-tuple-element.58), calls=%async_computation.3 | async-start | bytes 851968 | tf_op jit(solution)/shard_map/norm_grad_sums/all_to_all | solution.py:571
  98.6 1.4 collective-permute-start.1
  100.0 3.5 %collective-permute-start.2 = (bf16[8,2,16,128]{3,2,1,0:T(8,128)(2,1)S(1)}, bf16[8,2,16,128]{3,2,1,0:T(8,128)(2,1)S(1)}, u32[]{:S(2)}, u32[]{:S(2)}) collective-permute-start(bf16[8,2,16,128]{3,2,1,0:T(8,128)(2,1)S(1)} %get-tuple-element.61), channel_id=1, source_target_pairs={{2,0},{4,2},{6,4},{8,6},{10,8},{12,10},{14,12},{16,14},{18,16},{20... | collective-permute-start | bytes 196616 | tf_op jit(solution)/shard_map/edge_grads/ppermute | solution.py:568
  103.5 4.6 %all-to-all-done.3.sum_ref = bf16[16,6,1664]{2,1,0:T(8,128)(2,1)S(1)} async-done(((bf16[16,6,1664]{2,1,0:T(8,128)(2,1)}), bf16[16,6,1664]{2,1,0:T(8,128)(2,1)S(1)}, u32[]{:S(2)}, u32[]{:S(2)}) %all-to-all-start.3) | async-done | bytes 319520 | tf_op jit(solution)/shard_map/norm_grad_sums/all_to_all | solution.py:571
  108.1 5.5 %all-to-all-start.4 = ((bf16[16,96,128]{2,1,0:T(8,128)(2,1)}), bf16[16,96,128]{2,1,0:T(8,128)(2,1)S(1)}, u32[]{:S(2)}, u32[]{:S(2)}) async-start(bf16[16,96,128]{2,1,0:T(8,128)(2,1)} %get-tuple-element.64), calls=%async_computation.4 | async-start | bytes 786432 | tf_op jit(solution)/shard_map/act_to_frames/all_to_all | solution.py:575
  113.6 1.2 copy-done.2
  114.8 8.9 %conv_grad.1 = (bf16[16,96,128]{2,1,0:T(8,128)(2,1)}, f32[32,128]{1,0:T(8,128)S(1)}, f32[8,128]{1,0:T(8,128)S(1)}) custom-call(s32[1]{0:T(128)} %bitcast.set_ref, f32[8,256,128]{2,1,0:T(8,128)S(1)} %copy-done.2, f32[8,256,128]{2,1,0:T(8,128)S(1)} %get-tuple-element.53.conv_ref, bf16[8,288,128]{2,1,0:T(8,128)(2,1)S(1)} %bitcast.15, ...), custom_call_target="tpu_custom_call" | custom-call | flops 10000000000 | bytes 1048576 | tf_op jit(solution)/shard_map/conv_grad/conv_grad/pallas_call | solution.py:38
  123.7 4.4 %all-to-all-done.4.act_ref = bf16[16,96,128]{2,1,0:T(8,128)(2,1)S(1)} async-done(((bf16[16,96,128]{2,1,0:T(8,128)(2,1)}), bf16[16,96,128]{2,1,0:T(8,128)(2,1)S(1)}, u32[]{:S(2)}, u32[]{:S(2)}) %all-to-all-start.4) | async-done | bytes 393248 | tf_op jit(solution)/shard_map/act_to_frames/all_to_all | solution.py:575
  128.2 3.4 %all-to-all-start.5 = ((bf16[16,96,128]{2,1,0:T(8,128)(2,1)}), bf16[16,96,128]{2,1,0:T(8,128)(2,1)S(1)}, u32[]{:S(2)}, u32[]{:S(2)}) async-start(bf16[16,96,128]{2,1,0:T(8,128)(2,1)} %get-tuple-element.73), calls=%async_computation.5 | async-start | bytes 786432 | tf_op jit(solution)/shard_map/channels_to_frames/all_to_all | solution.py:613
  131.6 0.7 convert_reduce_fusion
  132.8 1.2 collective-permute-start.4
  134.0 2.1 %collective-permute-start.5 = (f32[32,128]{1,0:T(8,128)S(1)}, f32[32,128]{1,0:T(8,128)S(1)}, u32[]{:S(2)}, u32[]{:S(2)}) collective-permute-start(f32[32,128]{1,0:T(8,128)S(1)} %get-tuple-element.65), channel_id=1, source_target_pairs={{0,24},{8,0},{16,8},{24,16},{1,25},{9,1},{17,9},{25,17},{2,26},{10... | collective-permute-start | bytes 49160 | tf_op jit(solution)/shard_map/sums_of_taps/ppermute | solution.py:632
  136.1 2.3 %copy-done = bf16[1536,1536]{1,0:T(8,128)(2,1)S(1)} copy-done((bf16[1536,1536]{1,0:T(8,128)(2,1)S(1)}, bf16[1536,1536]{1,0:T(8,128)(2,1)}, u32[]{:S(2)}) %copy-start) | copy-done | bytes 4718616
  138.4 2.5 %module_out.1 = bf16[128,1536]{1,0:T(8,128)(2,1)} custom-call(bf16[16,96,128]{2,1,0:T(8,128)(2,1)S(1)} %all-to-all-done.4.act_ref, bf16[1536,1536]{1,0:T(8,128)(2,1)S(1)} %copy-done), custom_call_target="tpu_custom_call" | custom-call | flops 4000000000 | bytes 1048576 | tf_op jit(solution)/shard_map/module_out/module_out/pallas_call | solution.py:38
  141.1 1.3 collective-permute-start.7
  142.4 1.4 collective-permute-start.8
  144.3 1.3 all-to-all-done.5.back_ref
  145.6 1.4 join.1
  (25 shorter events, 2.8 us)
Async XLA Ops:
  7.2 70.9 %all-gather.6.cloned.1.call-start = ((), (), s32[]{:S(2)}) async-start(), calls=%async_computation.7 | async-start | bytes 6684672 | tf_op jit(solution)/shard_map/cotangent_of_group/all_gather | solution.py:416
  12.3 18.8 %all-to-all-start = ((bf16[16,6,1664]{2,1,0:T(8,128)(2,1)}), bf16[16,6,1664]{2,1,0:T(8,128)(2,1)}, u32[]{:S(2)}, u32[]{:S(2)}) async-start(bf16[16,6,1664]{2,1,0:T(8,128)(2,1)} %get-tuple-element.45), calls=%async_computation | async-start | bytes 851968 | tf_op jit(solution)/shard_map/rows_and_params/all_to_all | solution.py:453
  20.0 8.8 %collective-permute-start = (bf16[16,1536]{1,0:T(8,128)(2,1)}, bf16[16,1536]{1,0:T(8,128)(2,1)}, u32[]{:S(2)}, u32[]{:S(2)}) collective-permute-start(bf16[16,1536]{1,0:T(8,128)(2,1)} %get-tuple-element.43), channel_id=1, source_target_pairs={{1,2},{3,4},{5,6},{7,8},{9,10},{11,12},{13,14},{15,16},{17,18},{19... | collective-permute-start | bytes 147464 | tf_op jit(solution)/shard_map/edge_frames/ppermute | solution.py:450
  31.2 36.8 %all-to-all-start.1 = ((bf16[16,144,128]{2,1,0:T(8,128)(2,1)}), bf16[16,144,128]{2,1,0:T(8,128)(2,1)S(1)}, u32[]{:S(2)}, u32[]{:S(2)}) async-start(bf16[16,144,128]{2,1,0:T(8,128)(2,1)} %split.1), calls=%async_computation.1 | async-start | bytes 1179648 | tf_op jit(solution)/shard_map/frames_to_channels/all_to_all | solution.py:467
  44.0 88.3 %all-gather.4.cloned.1.call-start = ((), (), s32[]{:S(2)}) async-start(), calls=%async_computation.6 | async-start | bytes 5013504 | tf_op jit(solution)/shard_map/weights_of_group/all_gather | solution.py:506
  74.0 10.6 %all-to-all-start.2 = ((f32[16,8,128]{2,1,0:T(8,128)}), f32[16,8,128]{2,1,0:T(8,128)S(1)}, u32[]{:S(2)}, u32[]{:S(2)}) async-start(f32[16,8,128]{2,1,0:T(8,128)} %get-tuple-element.55), calls=%async_computation.2 | async-start | bytes 131072 | tf_op jit(solution)/shard_map/norm_sums/all_to_all | solution.py:509
  91.0 1.0 copy-start.1
  92.0 16.1 %all-to-all-start.3 = ((bf16[16,6,1664]{2,1,0:T(8,128)(2,1)}), bf16[16,6,1664]{2,1,0:T(8,128)(2,1)S(1)}, u32[]{:S(2)}, u32[]{:S(2)}) async-start(bf16[16,6,1664]{2,1,0:T(8,128)(2,1)} %get-tuple-element.58), calls=%async_computation.3 | async-start | bytes 851968 | tf_op jit(solution)/shard_map/norm_grad_sums/all_to_all | solution.py:571
  98.6 15.0 %collective-permute-start.1 = (bf16[8,2,16,128]{3,2,1,0:T(8,128)(2,1)S(1)}, bf16[8,2,16,128]{3,2,1,0:T(8,128)(2,1)S(1)}, u32[]{:S(2)}, u32[]{:S(2)}) collective-permute-start(bf16[8,2,16,128]{3,2,1,0:T(8,128)(2,1)S(1)} %get-tuple-element.60), channel_id=1, source_target_pairs={{0,2},{2,4},{4,6},{6,8},{8,10},{10,12},{12,14},{14,16},{16,18},{18... | collective-permute-start | bytes 196616 | tf_op jit(solution)/shard_map/edge_grads/ppermute | solution.py:567
  100.0 13.6 %collective-permute-start.2 = (bf16[8,2,16,128]{3,2,1,0:T(8,128)(2,1)S(1)}, bf16[8,2,16,128]{3,2,1,0:T(8,128)(2,1)S(1)}, u32[]{:S(2)}, u32[]{:S(2)}) collective-permute-start(bf16[8,2,16,128]{3,2,1,0:T(8,128)(2,1)S(1)} %get-tuple-element.61), channel_id=1, source_target_pairs={{2,0},{4,2},{6,4},{8,6},{10,8},{12,10},{14,12},{16,14},{18,16},{20... | collective-permute-start | bytes 196616 | tf_op jit(solution)/shard_map/edge_grads/ppermute | solution.py:568
  108.1 20.1 %all-to-all-start.4 = ((bf16[16,96,128]{2,1,0:T(8,128)(2,1)}), bf16[16,96,128]{2,1,0:T(8,128)(2,1)S(1)}, u32[]{:S(2)}, u32[]{:S(2)}) async-start(bf16[16,96,128]{2,1,0:T(8,128)(2,1)} %get-tuple-element.64), calls=%async_computation.4 | async-start | bytes 786432 | tf_op jit(solution)/shard_map/act_to_frames/all_to_all | solution.py:575
  113.6 1.2 copy-start.2
  128.2 17.5 %all-to-all-start.5 = ((bf16[16,96,128]{2,1,0:T(8,128)(2,1)}), bf16[16,96,128]{2,1,0:T(8,128)(2,1)S(1)}, u32[]{:S(2)}, u32[]{:S(2)}) async-start(bf16[16,96,128]{2,1,0:T(8,128)(2,1)} %get-tuple-element.73), calls=%async_computation.5 | async-start | bytes 786432 | tf_op jit(solution)/shard_map/channels_to_frames/all_to_all | solution.py:613
  132.3 8.7 %collective-permute-start.3 = (f32[32,128]{1,0:T(8,128)S(1)}, f32[32,128]{1,0:T(8,128)S(1)}, u32[]{:S(2)}, u32[]{:S(2)}) collective-permute-start(f32[32,128]{1,0:T(8,128)S(1)} %get-tuple-element.65), channel_id=1, source_target_pairs={{0,8},{8,16},{16,24},{24,0},{1,9},{9,17},{17,25},{25,1},{2,10},{10... | collective-permute-start | bytes 49160 | tf_op jit(solution)/shard_map/sums_of_taps/ppermute | solution.py:632
  132.8 8.2 %collective-permute-start.4 = (f32[32,128]{1,0:T(8,128)S(1)}, f32[32,128]{1,0:T(8,128)S(1)}, u32[]{:S(2)}, u32[]{:S(2)}) collective-permute-start(f32[32,128]{1,0:T(8,128)S(1)} %get-tuple-element.65), channel_id=1, source_target_pairs={{0,16},{8,24},{16,0},{24,8},{1,17},{9,25},{17,1},{25,9},{2,18},{10... | collective-permute-start | bytes 49160 | tf_op jit(solution)/shard_map/sums_of_taps/ppermute | solution.py:632
  134.0 7.0 %collective-permute-start.5 = (f32[32,128]{1,0:T(8,128)S(1)}, f32[32,128]{1,0:T(8,128)S(1)}, u32[]{:S(2)}, u32[]{:S(2)}) collective-permute-start(f32[32,128]{1,0:T(8,128)S(1)} %get-tuple-element.65), channel_id=1, source_target_pairs={{0,24},{8,0},{16,8},{24,16},{1,25},{9,1},{17,9},{25,17},{2,26},{10... | collective-permute-start | bytes 49160 | tf_op jit(solution)/shard_map/sums_of_taps/ppermute | solution.py:632
  136.1 2.3 %copy-start = (bf16[1536,1536]{1,0:T(8,128)(2,1)S(1)}, bf16[1536,1536]{1,0:T(8,128)(2,1)}, u32[]{:S(2)}) copy-start(bf16[1536,1536]{1,0:T(8,128)(2,1)} %all-gather.4.cloned.1.call-done.w_ref) | copy-start | bytes 14155780
  141.0 6.0 %collective-permute-start.6 = (f32[32,128]{1,0:T(8,128)S(1)}, f32[32,128]{1,0:T(8,128)S(1)}, u32[]{:S(2)}, u32[]{:S(2)}) collective-permute-start(f32[32,128]{1,0:T(8,128)S(1)} %add_add_fusion), channel_id=1, source_target_pairs={{0,2},{2,4},{4,6},{6,0},{1,3},{3,5},{5,7},{7,1},{8,10},{10,12},{12... | collective-permute-start | bytes 49160 | tf_op jit(solution)/shard_map/sums_of_taps/ppermute | solution.py:632
  141.1 6.0 %collective-permute-start.7 = (f32[32,128]{1,0:T(8,128)S(1)}, f32[32,128]{1,0:T(8,128)S(1)}, u32[]{:S(2)}, u32[]{:S(2)}) collective-permute-start(f32[32,128]{1,0:T(8,128)S(1)} %add_add_fusion), channel_id=1, source_target_pairs={{0,4},{2,6},{4,0},{6,2},{1,5},{3,7},{5,1},{7,3},{8,12},{10,14},{12... | collective-permute-start | bytes 49160 | tf_op jit(solution)/shard_map/sums_of_taps/ppermute | solution.py:632
  142.4 4.7 %collective-permute-start.8 = (f32[32,128]{1,0:T(8,128)S(1)}, f32[32,128]{1,0:T(8,128)S(1)}, u32[]{:S(2)}, u32[]{:S(2)}) collective-permute-start(f32[32,128]{1,0:T(8,128)S(1)} %add_add_fusion), channel_id=1, source_target_pairs={{0,6},{2,0},{4,2},{6,4},{1,7},{3,1},{5,3},{7,5},{8,14},{10,8},{12,... | collective-permute-start | bytes 49160 | tf_op jit(solution)/shard_map/sums_of_taps/ppermute | solution.py:632
Sparse Core Ops, SparseCore 0:
  9.8 63.1 all-gather.5
  75.4 41.1 all-gather.3
